TPU v7x, 256 devices: a whole 4x4x8 slice. The times are simulated.
256 devices in a mesh: band: 128 (over z, y, x), feat: 2 (over core).
Axes of the slice: x: 4, y: 4, z: 8, core: 2. Of those that a mesh axis runs over, the one named last changes fastest.
Arguments:
- grid_latent: bfloat16 [131072, 512], P('band', 'feat'), may hold values from -6 to 6
- mesh_latent: bfloat16 [65536, 512], P('band', 'feat'), may hold values from -6 to 6
- encode_weights: bfloat16 [4, 512, 512], P(None, None, 'feat'), may hold values from -0.25 to 0.25
- layer_weights: bfloat16 [2, 4, 512, 512], P(None, None, None, 'feat'), may hold values from -0.25 to 0.25
- decode_weights: bfloat16 [4, 512, 512], P(None, None, 'feat'), may hold values from -0.25 to 0.25
- encode_senders: int32 [128, 5, 512], P('band'), may hold values from 0 to 1023
- encode_targets: int32 [128, 5, 512], P('band'), may hold values from 0 to 511
- encode_live: int32 [128, 5, 512], P('band'), may hold values from 0 to 1, as said below
- mesh_senders: int32 [65536, 8], P('band'), may hold values from 0 to 65535, as said below
- mesh_live: int32 [65536, 8], P('band'), may hold values 0 or 1
- decode_senders: int32 [128, 5, 1024], P('band'), may hold values from 0 to 511
- decode_targets: int32 [128, 5, 1024], P('band'), may hold values from 0 to 1023
- decode_live: int32 [128, 5, 1024], P('band'), may hold values from 0 to 1, as said below
Outputs:
- mesh_out: bfloat16 [65536, 512], P('band', 'feat')
- grid_out: bfloat16 [131072, 512], P('band', 'feat')
Inputs may be any that keep to these rules, and one draw needn't show every extreme that they name: `encode_live`: A slot is live only where its band d - o + 2 exists; all slots of offset 2 (an owner's own band) are live. `decode_live`: A slot is live only where its owner d - o + 2 exists; all slots of offset 2 (a band's own owner) are live. `mesh_senders`: A mesh node's senders are nodes of its own owner or among the 64 rows at the near end of the owner before or after it.
All inputs are finite; a program needn't handle non-finite values. No bound on the sum of `mesh_live` on one device may be relied on, other than what follows from the above.
Results may differ from a plain program's by a relative error of at most 0.018.
Values may be sent and summed in bfloat16 or wider, within the bound.
No kernel may reach another device: no remote copies, remote signals or barrier semaphores. Data moves between devices by JAX's collectives and lax.ppermute only.
A program may use at most 64 MiB of HBM per device.

v0:
```python
import functools

import jax
import jax.numpy as jnp
from jax import lax
from jax.experimental import pallas as pl
from jax.experimental.pallas import tpu as pltpu
from jax.sharding import PartitionSpec as P

REACH = 2
LAYERS = 2
MARGIN = 64
HALF = 256
LANES = 128
F32 = jnp.float32
BF16 = jnp.bfloat16
I32 = jnp.int32
VMEM_LIMIT = 36 * 1024 * 1024


def swap(value):
    return lax.ppermute(value, "feat", [(0, 1), (1, 0)])


def flat(partners):
    return [(2 * s + c, 2 * t + e) for (s, c), (t, e) in partners.items()]


def shift(steps, up, count):
    partners = {}
    for s in range(count):
        partners[s, up] = (s + steps, up) if s + steps < count else (s, 1 - up)
        partners[s, 1 - up] = (s - steps, 1 - up) if s >= steps else (s, up)
    return flat(partners)


near_shift = functools.partial(shift, 1, 0)
skip_shift = functools.partial(shift, 2, 0)
halo_shift = functools.partial(shift, 1, 1)


def halo_pairs(count):
    partners = {}
    for s in range(count):
        partners[s, 1] = ((s + 1) % count, 0)
        partners[(s + 1) % count, 0] = (s, 1)
    return flat(partners)


def exchange(value, pairs):
    return lax.ppermute(value, ("band", "feat"), pairs(lax.axis_size("band")))


def after(value, other):
    return lax.optimization_barrier((value, other))[0]


def silu(v):
    half = 0.5 * v
    return half + half * jnp.tanh(half)


def silu_message(v):
    half = v.astype(BF16) * BF16(0.5)
    return half + half * jnp.tanh(half)


def dot(a, b):
    return jnp.dot(a, b, preferred_element_type=F32)


def window(index, size=HALF):
    return pl.ds(pl.multiple_of(index * size, size), size)


def near_offset(meta):
    return 3 - 2 * meta[0]


def skip_offset(meta):
    return 4 - 4 * meta[0]


def column(row):
    parts = [
        jnp.broadcast_to(row[:, start : start + LANES], (LANES, LANES)).T
        for start in range(0, row.shape[1], LANES)
    ]
    return parts[0] if len(parts) == 1 else jnp.concatenate(parts, axis=0)


def hot_columns(col, width):
    col = col.astype(jnp.int16)
    ids = lax.broadcasted_iota(I32, col.shape, 1).astype(jnp.int16)
    one, zero = BF16(1), BF16(0)
    parts = [
        jnp.where(col == ids + jnp.int16(start), one, zero) for start in range(0, width, LANES)
    ]
    return parts[0] if len(parts) == 1 else jnp.concatenate(parts, axis=1)


def hot_rows(row, height):
    ids = lax.broadcasted_iota(I32, (height, row.shape[1]), 0)
    return jnp.where(row == ids, 1.0, 0.0).astype(BF16)


class Part:
    def __init__(self, spec, index):
        self.spec, self.index = spec, index


def call(kernel, name, operands, specs, outs, flops, scratch=()):
    def viewed(*refs):
        refs = [
            ref.at[specs[i].index] if i < len(specs) and isinstance(specs[i], Part) else ref
            for i, ref in enumerate(refs)
        ]
        kernel(*refs)

    size = sum(x.size * x.dtype.itemsize for x in outs)
    return pl.pallas_call(
        viewed,
        name=name,
        grid=(1,),
        in_specs=[spec.spec if isinstance(spec, Part) else spec for spec in specs],
        out_specs=[whole(x) for x in outs],
        out_shape=list(outs),
        scratch_shapes=list(scratch),
        compiler_params=pltpu.CompilerParams(vmem_limit_bytes=VMEM_LIMIT),
        cost_estimate=pl.CostEstimate(
            flops=flops // 64, bytes_accessed=size // 64, transcendentals=0
        ),
    )(*operands)


def whole(x):
    return pl.BlockSpec(x.shape, lambda i, n=len(x.shape): (0,) * n)


def part(x, *index):
    return Part(whole(x), index)


SMEM = pl.BlockSpec(memory_space=pltpu.SMEM)


def shape(*dims, dtype=BF16):
    return jax.ShapeDtypeStruct(dims, dtype)


def encode_begin_kernel(meta, own, w_own, out):
    for start in range(0, own.shape[0], HALF):
        rows = pl.ds(start, HALF)
        out[rows, :] = dot(own[rows, :], w_own[window(meta[0]), :])


def gather_slots(senders_row, sent, out):
    for start in range(0, senders_row.shape[1], HALF):
        col = column(senders_row[:, start : start + HALF])
        out[pl.ds(start, HALF), :] = dot(hot_columns(col, sent.shape[0]), sent[...]).astype(BF16)


def encode_near_kernel(meta, own, other, begun, w_own, w_other, senders, sent, piece):
    mine, rest = window(meta[0]), window(1 - meta[0])
    for start in range(0, own.shape[0], HALF):
        rows = pl.ds(start, HALF)
        a, b = own[rows, :], other[rows, :]
        sent[rows, mine] = (begun[rows, :] + dot(b, w_own[rest, :])).astype(BF16)
        sent[rows, rest] = (dot(a, w_other[mine, :]) + dot(b, w_other[rest, :])).astype(BF16)
    gather_slots(senders[near_offset(meta)], sent, piece)


def live_targets(targets, live, offset, columns=slice(None)):
    return jnp.where(live[offset, :, columns] > 0, targets[offset, :, columns], -1)


def encode_skip_kernel(
    meta, own, other, w1, w1_other, sent, senders, targets, piece, recv, before
):
    gather_slots(senders[skip_offset(meta)], sent, piece)
    mine, rest = window(meta[0]), window(1 - meta[0])
    for start in range(0, own.shape[0], HALF):
        rows = pl.ds(start, HALF)
        a, b = own[rows, :], other[rows, :]
        recv[rows, mine] = (dot(a, w1[mine, :]) + dot(b, w1[rest, :])).astype(BF16)
        recv[rows, rest] = (dot(a, w1_other[mine, :]) + dot(b, w1_other[rest, :])).astype(BF16)
    gather_slots(targets[near_offset(meta)], recv, before)


def encode_near_sum_kernel(
    meta, rows, before, recv, sent, own, other, w2, w2_other, senders, targets, live,
    total, before_skip, self_term, message, own_message,
):
    mine, rest = window(meta[0]), window(1 - meta[0])
    nodes = recv.shape[0]
    from_rows = hot_columns(column(senders[REACH, :, mine]), sent.shape[0])
    to_rows = hot_columns(column(targets[REACH, :, mine]), nodes)
    own_message[...] = silu_message(dot(from_rows, sent[...]) + dot(to_rows, recv[...]))
    message[...] = silu_message(rows[...] + before[...])
    row = live_targets(targets, live, near_offset(meta))
    own_row = live_targets(targets, live, REACH, mine)
    for start in range(0, nodes, HALF):
        value = dot(hot_rows(row - start, HALF), message[...])
        value = value + dot(hot_rows(own_row - start, HALF), own_message[...])
        total[pl.ds(start, HALF), :] = value
    gather_slots(targets[skip_offset(meta)], recv, before_skip)
    a, b = own[mine, :], other[mine, :]
    self_term[:, mine] = (dot(a, w2[mine, :]) + dot(b, w2[rest, :])).astype(BF16)
    self_term[:, rest] = (dot(a, w2_other[mine, :]) + dot(b, w2_other[rest, :])).astype(BF16)


def encode_skip_sum_kernel(meta, rows, before, targets, live, total, out_own, out_other, message):
    message[...] = silu_message(rows[...] + before[...])
    row = live_targets(targets, live, skip_offset(meta))
    for out, half in ((out_other, 1 - meta[0]), (out_own, meta[0])):
        value = dot(hot_rows(row - half * HALF, HALF), message[...]) + total[window(half), :]
        out[...] = value.astype(out.dtype)


def put_edge(meta, now, w0, w0_other, edge):
    mine, rest = window(meta[0]), window(1 - meta[0])
    rows = now[pl.ds(pl.multiple_of(meta[0] * (HALF - MARGIN), MARGIN), MARGIN), :]
    edge[:, mine] = dot(rows, w0[...]).astype(BF16)
    edge[:, rest] = dot(rows, w0_other[...]).astype(BF16)


def encode_update_kernel(
    meta, own, other, self_term, sum_own, sum_other, w3, w3_other, w0, w0_other, now, edge
):
    mine, rest = window(meta[0]), window(1 - meta[0])
    summed = (sum_own[...] + sum_other[...].astype(F32)).astype(BF16)
    for cols, latent, w in ((mine, own, w3), (rest, other, w3_other)):
        step = silu(self_term[:, cols] + dot(summed, w[...]))
        now[:, cols] = (latent[mine, :].astype(F32) + step).astype(BF16)
    put_edge(meta, now, w0, w0_other, edge)


def layer_project_kernel(
    last, meta, own, other, w0, w0_other, w1, w1_other, w2, w2_other,
    sent_own, sent_other, recv, self_own, *self_other,
):
    mine, rest = window(meta[0]), window(1 - meta[0])
    for cols, w in ((mine, w0), (rest, w0_other)):
        sent_own[:, cols] = dot(own[...], w[...]).astype(BF16)
        sent_other[:, cols] = dot(other[...], w[...]).astype(BF16)
    for cols, w in ((mine, w1), (rest, w1_other)):
        recv[:, cols] = dot(own[...], w[...]).astype(BF16)
    for cols, w in ((mine, w2), (rest, w2_other)):
        self_own[:, cols] = dot(own[...], w[...]).astype(BF16)
        if last:
            self_other[0][:, cols] = dot(other[...], w[...]).astype(BF16)


def layer_gather_kernel(meta, own, other, senders, out):
    mine = window(meta[0])
    base = meta[1] * (2 * HALF)
    for k in range(senders.shape[0]):
        local = senders[k : k + 1, mine] - base
        col = column(local - meta[0] * HALF)
        col_other = column(local - (1 - meta[0]) * HALF)
        value = dot(hot_columns(col, HALF), own[...])
        value = value + dot(hot_columns(col_other, HALF), other[...])
        out[k] = value.astype(BF16)


def layer_sum(meta, gathered, recv, near, far, senders, live, halo, total):
    mine = window(meta[0])
    nodes = 2 * HALF
    base = meta[1] * nodes
    count = senders.shape[0]
    hots, flags = [], []
    for k in range(count):
        local = senders[k : k + 1, mine] - base
        where = jnp.where(local < 0, local + MARGIN, local - nodes + MARGIN)
        where = jnp.where((local >= 0) & (local < nodes), -1, where)
        hots.append(hot_columns(column(where), 2 * MARGIN))
        flags.append(column(live[k : k + 1, mine]).astype(BF16))
    halo[pl.ds(pl.multiple_of(meta[0] * MARGIN, MARGIN), MARGIN), :] = near[...]
    halo[pl.ds(pl.multiple_of((1 - meta[0]) * MARGIN, MARGIN), MARGIN), :] = far[...]
    outside = dot(jnp.concatenate(hots, axis=0), halo[...]).astype(BF16)
    step = 32
    for start in range(0, HALF, step):
        rows = pl.ds(start, step)
        side = recv[rows, :]
        running = None
        for k in range(count):
            row = k * HALF + start
            message = silu_message(outside[row : row + step, :] + gathered[k, rows, :] + side)
            flag = jnp.concatenate([flags[k][start : start + step, :]] * 4, axis=1)
            message = (message * flag).astype(F32)
            running = message if running is None else running + message
        total[rows, :] = running.astype(BF16)


def layer_update_kernel(
    meta, gathered, recv, near, far, senders, live, now, self_term, w3, w3_other, w0, w0_other,
    out, edge, halo, total,
):
    mine, rest = window(meta[0]), window(1 - meta[0])
    layer_sum(meta, gathered, recv, near, far, senders, live, halo, total)
    summed = total[...]
    for cols, w in ((mine, w3), (rest, w3_other)):
        step = silu(self_term[:, cols] + dot(summed, w[...]))
        out[:, cols] = (now[:, cols].astype(F32) + step).astype(BF16)
    put_edge(meta, out, w0, w0_other, edge)


def layer_sum_kernel(meta, gathered, recv, near, far, senders, live, out, halo):
    layer_sum(meta, gathered, recv, near, far, senders, live, halo, out)


def last_update_kernel(
    meta, now_own, now_other, self_own, self_other, sum_own, sum_other, w3, w3_other,
    w0, w0_other, out, sent, now,
):
    mine, rest = window(meta[0]), window(1 - meta[0])
    for rows, latent, self_term, summed in (
        (mine, now_own, self_own, sum_own),
        (rest, now_other, self_other, sum_other),
    ):
        for cols, w in ((mine, w3), (rest, w3_other)):
            step = silu(self_term[:, cols] + dot(summed[...], w[...]))
            now[:, cols] = (latent[:, cols].astype(F32) + step).astype(BF16)
        out[rows, :] = now[:, mine]
        for cols, w in ((mine, w0), (rest, w0_other)):
            sent[rows, cols] = dot(now[...], w[...]).astype(BF16)


def decode_prepare_kernel(
    meta, own, other, w1, w1_other, w2, targets,
    before_own, before_near, before_skip, self_term, recv,
):
    mine, rest = window(meta[0]), window(1 - meta[0])
    for start in range(0, own.shape[0], HALF):
        rows = pl.ds(start, HALF)
        a, b = own[rows, :], other[rows, :]
        recv[rows, mine] = (dot(a, w1[mine, :]) + dot(b, w1[rest, :])).astype(BF16)
        recv[rows, rest] = (dot(a, w1_other[mine, :]) + dot(b, w1_other[rest, :])).astype(BF16)
        self_term[rows, :] = (dot(a, w2[mine, :]) + dot(b, w2[rest, :])).astype(BF16)
    half = before_own.shape[0]
    gather_slots(targets[REACH, :, window(meta[0], half)], recv, before_own)
    gather_slots(targets[near_offset(meta)], recv, before_near)
    gather_slots(targets[skip_offset(meta)], recv, before_skip)


def decode_messages(meta, offset, columns, sent, before, senders, message):
    from_row = senders[offset, :, columns]
    for start in range(0, before.shape[0], HALF):
        rows = pl.ds(start, HALF)
        hot = hot_columns(column(from_row[:, start : start + HALF]), sent.shape[0])
        pre = dot(hot, sent[...]) + before[rows, :].astype(F32)
        message[rows, :] = silu_message(pre)


def decode_scatter(row, message, total, first, out):
    for start in range(0, out.shape[0], HALF):
        value = dot(hot_rows(row - (first + start), HALF), message[...])
        if total is not None:
            value = value + total[pl.ds(first + start, HALF), :].astype(F32)
        out[pl.ds(start, HALF), :] = value.astype(BF16)


def decode_own_kernel(meta, sent, before, senders, targets, live, out, message):
    columns = window(meta[0], before.shape[0])
    decode_messages(meta, REACH, columns, sent, before, senders, message)
    decode_scatter(live_targets(targets, live, REACH, columns), message, None, 0, out)


def decode_near_kernel(meta, sent, before, senders, targets, live, total, out, message):
    offset = near_offset(meta)
    decode_messages(meta, offset, slice(None), sent, before, senders, message)
    decode_scatter(live_targets(targets, live, offset), message, total, 0, out)


def decode_skip_kernel(meta, sent, before, senders, targets, live, total, out, message):
    offset = skip_offset(meta)
    decode_messages(meta, offset, slice(None), sent, before, senders, message)
    decode_scatter(live_targets(targets, live, offset), message, total, 0, out)


def decode_rest_kernel(meta, message, targets, live, total, out):
    row = live_targets(targets, live, skip_offset(meta))
    decode_scatter(row, message, total, out.shape[0], out)


def final_kernel(first, meta, own, self_term, sum_own, sum_other, weights, *refs):
    out, w3 = refs[-1], weights.at[3]
    for start in range(0, out.shape[0], HALF):
        rows, from_rows = pl.ds(start, HALF), pl.ds(first + start, HALF)
        summed = sum_own[rows, :] + sum_other[rows, :]
        step = silu(self_term[from_rows, :].astype(F32) + dot(summed, w3[...]))
        out[rows, :] = (own[from_rows, :].astype(F32) + step).astype(BF16)


def body(
    grid_latent,
    mesh_latent,
    encode_weights,
    layer_weights,
    decode_weights,
    encode_senders,
    encode_targets,
    encode_live,
    mesh_senders,
    mesh_live,
    decode_senders,
    decode_targets,
    decode_live,
):
    meta = jnp.stack([lax.axis_index("feat"), lax.axis_index("band")]).astype(I32)
    grid_rows, cols = grid_latent.shape
    mesh_rows = mesh_latent.shape[0]
    full = 2 * cols
    senders, targets, live = (x.transpose(1, 0, 2) for x in (encode_senders, encode_targets, encode_live))
    slots = senders.shape[2]

    grid_other = swap(grid_latent)
    encode_other = swap(encode_weights)
    mesh_other = swap(mesh_latent)
    (begun,) = call(
        encode_begin_kernel,
        "encode_begin",
        (meta, grid_latent, encode_weights),
        [SMEM, whole(grid_latent), part(encode_weights, 0)],
        [shape(grid_rows, cols, dtype=F32)],
        2 * grid_rows * cols * cols,
    )
    grid_other, mesh_other = lax.optimization_barrier((grid_other, mesh_other))
    operands = (meta, grid_latent, grid_other, begun, encode_weights, encode_other, senders)
    sent, near_piece = call(
        encode_near_kernel,
        "encode_near",
        operands,
        [SMEM] + [whole(x) for x in operands[1:4]]
        + [part(encode_weights, 0), part(encode_other, 0), whole(senders)],
        [shape(grid_rows, full), shape(slots, full)],
        2 * full * (grid_rows * full + slots * grid_rows),
    )
    near_rows = exchange(near_piece, near_shift)
    layer_other = swap(after(layer_weights, near_piece))
    operands = (
        meta, mesh_latent, mesh_other, encode_weights, encode_other, sent, senders, targets
    )
    skip_piece, recv, before_near = call(
        encode_skip_kernel,
        "encode_skip",
        operands,
        [SMEM, whole(mesh_latent), whole(mesh_other)]
        + [part(encode_weights, 1), part(encode_other, 1)]
        + [whole(sent), whole(senders), whole(targets)],
        [shape(slots, full), shape(mesh_rows, full), shape(slots, full)],
        2 * full * (mesh_rows * full + slots * (grid_rows + mesh_rows)),
    )
    skip_rows = exchange(skip_piece, skip_shift)
    operands = (
        meta, near_rows, before_near, recv, sent, mesh_latent, mesh_other,
        encode_weights, encode_other, senders, targets, live,
    )
    total, before_skip, self_term = call(
        encode_near_sum_kernel,
        "encode_near_sum",
        operands,
        [SMEM] + [whole(x) for x in operands[1:7]]
        + [part(encode_weights, 2), part(encode_other, 2)]
        + [whole(x) for x in operands[9:]],
        [
            shape(mesh_rows, full, dtype=F32),
            shape(slots, full),
            shape(HALF, full),
        ],
        2 * full * mesh_rows * slots * 3,
        [pltpu.VMEM((slots, full), BF16), pltpu.VMEM((HALF, full), BF16)],
    )
    operands = (meta, skip_rows, before_skip, targets, live, total)
    sum_own, sum_other = call(
        encode_skip_sum_kernel,
        "encode_skip_sum",
        operands,
        [SMEM, whole(skip_rows), whole(before_skip), whole(targets), whole(live), whole(total)],
        [shape(HALF, full, dtype=F32), shape(HALF, full)],
        2 * full * mesh_rows * slots,
        [pltpu.VMEM((slots, full), BF16)],
    )
    operands = (
        meta, mesh_latent, mesh_other, self_term, sum_own, swap(sum_other),
        encode_weights, encode_other, layer_weights, layer_other,
    )
    now, edge = call(
        encode_update_kernel,
        "encode_update",
        operands,
        [SMEM] + [whole(x) for x in operands[1:6]]
        + [part(encode_weights, 3), part(encode_other, 3)]
        + [part(layer_weights, 0, 0), part(layer_other, 0, 0)],
        [shape(HALF, full), shape(MARGIN, full)],
        2 * HALF * full * full,
    )

    decode_other = swap(after(decode_weights, now))
    senders_t, live_t = mesh_senders.T, mesh_live.T
    degree = senders_t.shape[0]
    for layer in range(LAYERS):
        last = layer == LAYERS - 1
        far = exchange(edge, halo_shift)
        near = exchange(edge, halo_pairs)
        now_other = swap(now)
        operands = (meta, now, now_other) + (layer_weights, layer_other) * 3
        results = call(
            functools.partial(layer_project_kernel, last),
            f"layer_project_{layer}",
            operands,
            [SMEM, whole(now), whole(now_other)]
            + [part(operands[3 + i], layer, i // 2) for i in range(6)],
            [shape(HALF, full)] * (5 if last else 4),
            2 * HALF * full * full * 4,
        )
        sent_own, sent_other, recv, self_own = results[:4]
        operands = (meta, sent_own, sent_other, senders_t)
        (gathered,) = call(
            layer_gather_kernel,
            f"layer_gather_{layer}",
            operands,
            [SMEM, whole(sent_own), whole(sent_other), whole(senders_t)],
            [shape(degree, HALF, full)],
            2 * degree * HALF * full * mesh_rows,
        )
        operands = (meta, gathered, recv, near, far, senders_t, live_t)
        scratch = [pltpu.VMEM((2 * MARGIN, full), BF16)]
        sum_specs = (
            [SMEM] + [whole(x) for x in operands[1:5]]
            + [whole(senders_t), whole(live_t)]
        )
        if last:
            (summed,) = call(
                layer_sum_kernel,
                f"layer_sum_{layer}",
                operands,
                sum_specs,
                [shape(HALF, full)],
                2 * degree * HALF * full * 2 * MARGIN,
                scratch,
            )
            continue
        operands += (now, self_own) + (layer_weights, layer_other) * 2
        now, edge = call(
            layer_update_kernel,
            f"layer_update_{layer}",
            operands,
            sum_specs + [whole(now), whole(self_own)]
            + [part(layer_weights, layer, 3), part(layer_other, layer, 3)]
            + [part(layer_weights, layer + 1, 0), part(layer_other, layer + 1, 0)],
            [shape(HALF, full), shape(MARGIN, full)],
            2 * HALF * full * (degree * 2 * MARGIN + full),
            scratch + [pltpu.VMEM((HALF, full), BF16)],
        )
    operands = (
        meta, now, now_other, self_own, results[4], summed, swap(summed),
        layer_weights, layer_other, decode_weights, decode_other,
    )
    mesh_now, sent = call(
        last_update_kernel,
        "last_update",
        operands,
        [SMEM] + [whole(x) for x in operands[1:7]]
        + [part(layer_weights, LAYERS - 1, 3), part(layer_other, LAYERS - 1, 3)]
        + [part(decode_weights, 0), part(decode_other, 0)],
        [shape(mesh_rows, cols), shape(mesh_rows, full)],
        2 * mesh_rows * full * full * 2,
        [pltpu.VMEM((HALF, full), BF16)],
    )

    near_rows = exchange(sent, near_shift)
    skip_rows = exchange(sent, skip_shift)
    senders, targets, live = (x.transpose(1, 0, 2) for x in (decode_senders, decode_targets, decode_live))
    slots = senders.shape[2]
    operands = (
        meta, grid_latent, grid_other, decode_weights, decode_other, decode_weights, targets
    )
    before_own, before_near, before_skip, self_term = call(
        decode_prepare_kernel,
        "decode_prepare",
        operands,
        [SMEM, whole(grid_latent), whole(grid_other)]
        + [part(decode_weights, 1), part(decode_other, 1), part(decode_weights, 2), whole(targets)],
        [
            shape(slots // 2, full),
            shape(slots, full),
            shape(slots, full),
            shape(grid_rows, cols),
        ],
        2 * full * grid_rows * (full + 5 * slots // 2),
        [pltpu.VMEM((grid_rows, full), BF16)],
    )
    flops = 2 * full * slots * (grid_rows + mesh_rows)
    message_space = [pltpu.VMEM((slots, full), BF16)]
    operands = (meta, sent, before_own, senders, targets, live)
    (total,) = call(
        decode_own_kernel,
        "decode_own",
        operands,
        [SMEM] + [whole(x) for x in operands[1:]],
        [shape(grid_rows, full)],
        flops // 2,
        [pltpu.VMEM(before_own.shape, BF16)],
    )
    operands = (meta, near_rows, before_near, senders, targets, live, total)
    (total,) = call(
        decode_near_kernel,
        "decode_near",
        operands,
        [SMEM] + [whole(x) for x in operands[1:]],
        [shape(grid_rows, full)],
        flops,
        message_space,
    )
    half = grid_rows // 2
    operands = (meta, skip_rows, before_skip, senders, targets, live, total)
    head, message = call(
        decode_skip_kernel,
        "decode_skip",
        operands,
        [SMEM] + [whole(x) for x in operands[1:]],
        [shape(half, full), shape(slots, full)],
        flops,
    )
    operands = (meta, message, targets, live, total)
    (tail,) = call(
        decode_rest_kernel,
        "decode_rest",
        operands,
        [SMEM] + [whole(x) for x in operands[1:]],
        [shape(half, full)],
        flops // 2,
    )
    grid_now = None
    for index, summed in enumerate((head, tail)):
        block = pl.BlockSpec((half, cols), lambda i, index=index: (index, 0))
        operands = (meta, grid_latent, self_term, summed, swap(summed), decode_weights)
        specs = [SMEM] + [whole(x) for x in operands[1:]]
        aliases = {}
        if index:
            operands, specs, aliases = operands + (grid_now,), specs + [pl.BlockSpec(memory_space=pl.ANY)], {6: 0}
        grid_now = pl.pallas_call(
            functools.partial(final_kernel, index * half),
            name=f"final_update_{index}",
            grid=(1,),
            in_specs=specs,
            out_specs=block,
            out_shape=shape(grid_rows, cols),
            input_output_aliases=aliases,
            compiler_params=pltpu.CompilerParams(vmem_limit_bytes=VMEM_LIMIT),
        )(*operands)
    return mesh_now, grid_now


def solution(mesh):
    placed = (
        P("band", "feat"),
        P("band", "feat"),
        P(None, None, "feat"),
        P(None, None, None, "feat"),
        P(None, None, "feat"),
        P("band", None, None),
        P("band", None, None),
        P("band", None, None),
        P("band", None),
        P("band", None),
        P("band", None, None),
        P("band", None, None),
        P("band", None, None),
    )
    return jax.shard_map(
        body,
        mesh=mesh,
        in_specs=placed,
        out_specs=(P("band", "feat"), P("band", "feat")),
        check_vma=False,
    )
```

profile of v0, /device:TPU:1, one launch (start us, length us, event | category | flops | bytes accessed | tf_op | source)
XLA Modules:
  0.0 98.3 jit_solution(1873823678112115104)
XLA Ops:
  0.6 3.3 %collective-permute-start.2 = (bf16[4,512,256]{2,1,0:T(8,128)(2,1)}, bf16[4,512,256]{2,1,0:T(8,128)(2,1)S(1)}, u32[]{:S(2)}, u32[]{:S(2)}) collective-permute-start(bf16[4,512,256]{2,1,0:T(8,128)(2,1)} %refs_6_.1), channel_id=1, source_target_pairs={{0,1},{1,0},{2,3},{3,2},{4,5},{5,4},{6,7},{7,6},{8,9},{9,8},{10,11... | collective-permute-start | bytes 3145736 | tf_op jit(solution)/shard_map/ppermute | solution.py:22
  7.8 1.9 %encode_near.1 = (bf16[1024,512]{1,0:T(8,128)(2,1)S(1)}, bf16[512,512]{1,0:T(8,128)(2,1)S(1)}) custom-call(s32[2]{0:T(128)S(1)} %pad_add_fusion.refs_0_.meta, bf16[1024,256]{1,0:T(8,128)(2,1)S(1)} %copy-done.4, bf16[1024,256]{1,0:T(8,128)(2,1)S(1)} %collective-permute-done.refs_2_, f32[1024,256]{1,0:T(8,128)S(1)} %encode_begin.1.refs_3_, ...), custom_call_target="tpu_custom_call" | custom-call | flops 16777216 | bytes 24576 | tf_op jit(solution)/shard_map/encode_near/pallas_call | solution.py:121
  10.3 2.0 %encode_skip.1 = (bf16[512,512]{1,0:T(8,128)(2,1)S(1)}, bf16[512,512]{1,0:T(8,128)(2,1)S(1)}, bf16[512,512]{1,0:T(8,128)(2,1)S(1)}) custom-call(s32[2]{0:T(128)S(1)} %pad_add_fusion.refs_0_.meta, bf16[512,256]{1,0:T(8,128)(2,1)S(1)} %copy-done.6, bf16[512,256]{1,0:T(8,128)(2,1)S(1)} %collective-permute-done.1.refs_2_.refs_6_, ...), custom_call_target="tpu_custom_call" | custom-call | flops 16777216 | bytes 24576 | tf_op jit(solution)/shard_map/encode_skip/pallas_call | solution.py:121
  12.4 16.0 %collective-permute-done.3.refs_1_ = bf16[512,512]{1,0:T(8,128)(2,1)S(1)} collective-permute-done((bf16[512,512]{1,0:T(8,128)(2,1)S(1)}, bf16[512,512]{1,0:T(8,128)(2,1)S(1)}, u32[]{:S(2)}, u32[]{:S(2)}) %collective-permute-start.3) | collective-permute-done | bytes 524320 | tf_op jit(solution)/shard_map/ppermute | solution.py:51
  28.5 2.2 %encode_near_sum.1 = (f32[512,512]{1,0:T(8,128)S(1)}, bf16[512,512]{1,0:T(8,128)(2,1)S(1)}, bf16[256,512]{1,0:T(8,128)(2,1)S(1)}) custom-call(s32[2]{0:T(128)S(1)} %pad_add_fusion.refs_0_.meta, bf16[512,512]{1,0:T(8,128)(2,1)S(1)} %collective-permute-done.3.refs_1_, bf16[512,512]{1,0:T(8,128)(2,1)S(1)} %get-tuple-element.41.refs_2_, ...), custom_call_target="tpu_custom_call" | custom-call | flops 12582912 | bytes 28672 | tf_op jit(solution)/shard_map/encode_near_sum/pallas_call | solution.py:121
  31.8 1.5 %collective-permute-done.5.refs_5_ = bf16[256,512]{1,0:T(8,128)(2,1)S(1)} collective-permute-done((bf16[256,512]{1,0:T(8,128)(2,1)S(1)}, bf16[256,512]{1,0:T(8,128)(2,1)S(1)}, u32[]{:S(2)}, u32[]{:S(2)}) %collective-permute-start.5) | collective-permute-done | bytes 262176 | tf_op jit(solution)/shard_map/ppermute | solution.py:22
  35.1 1.9 %collective-permute-start.8 = (bf16[64,512]{1,0:T(8,128)(2,1)S(1)}, bf16[64,512]{1,0:T(8,128)(2,1)S(1)}, u32[]{:S(2)}, u32[]{:S(2)}) collective-permute-start(bf16[64,512]{1,0:T(8,128)(2,1)S(1)} %get-tuple-element.54), channel_id=1, source_target_pairs={{1,2},{2,1},{3,4},{4,3},{5,6},{6,5},{7,8},{8,7},{9,10},{10,9},{11,... | collective-permute-start | bytes 196616 | tf_op jit(solution)/shard_map/ppermute | solution.py:51
  38.9 1.9 %layer_gather_0.1.refs_1_ = bf16[8,256,512]{2,1,0:T(8,128)(2,1)S(1)} custom-call(s32[2]{0:T(128)S(1)} %pad_add_fusion.refs_0_.meta, bf16[256,512]{1,0:T(8,128)(2,1)S(1)} %get-tuple-element.51.refs_1_, bf16[256,512]{1,0:T(8,128)(2,1)S(1)} %get-tuple-element.52.refs_2_, s32[8,512]{1,0:T(8,128)S(1)} %bitcast.19), custom_call_target="tpu_custom_call" | custom-call | flops 16777216 | bytes 32768 | tf_op jit(solution)/shard_map/layer_gather_0/pallas_call | solution.py:121
  40.8 4.0 %collective-permute-done.9.refs_4_ = bf16[64,512]{1,0:T(8,128)(2,1)S(1)} collective-permute-done((bf16[64,512]{1,0:T(8,128)(2,1)S(1)}, bf16[64,512]{1,0:T(8,128)(2,1)S(1)}, u32[]{:S(2)}, u32[]{:S(2)}) %collective-permute-start.9) | collective-permute-done | bytes 65568 | tf_op jit(solution)/shard_map/ppermute | solution.py:51
  44.8 2.4 %layer_update_0.1 = (bf16[256,512]{1,0:T(8,128)(2,1)S(1)}, bf16[64,512]{1,0:T(8,128)(2,1)S(1)}) custom-call(s32[2]{0:T(128)S(1)} %pad_add_fusion.refs_0_.meta, bf16[8,256,512]{2,1,0:T(8,128)(2,1)S(1)} %layer_gather_0.1.refs_1_, bf16[256,512]{1,0:T(8,128)(2,1)S(1)} %get-tuple-element.53.refs_2_, bf16[64,512]{1,0:T(8,128)(2,1)S(1)} %collective-permute-done.8.refs_3_, ...), custom_call_target="tpu_custom_call" | custom-call | flops 6291456 | bytes 5120 | tf_op jit(solution)/shard_map/layer_update_0/pallas_call | solution.py:121
  47.2 3.6 %collective-permute-start.10 = (bf16[256,512]{1,0:T(8,128)(2,1)S(1)}, bf16[256,512]{1,0:T(8,128)(2,1)S(1)}, u32[]{:S(2)}, u32[]{:S(2)}) collective-permute-start(bf16[256,512]{1,0:T(8,128)(2,1)S(1)} %get-tuple-element.56.refs_1_), channel_id=1, source_target_pairs={{0,1},{1,0},{2,3},{3,2},{4,5},{5,4},{6,7},{7,6},{8,9},{9,8},{10,11... | collective-permute-start | bytes 786440 | tf_op jit(solution)/shard_map/ppermute | solution.py:22
  52.0 1.4 %layer_project_1.1 = (bf16[256,512]{1,0:T(8,128)(2,1)S(1)}, bf16[256,512]{1,0:T(8,128)(2,1)S(1)}, bf16[256,512]{1,0:T(8,128)(2,1)S(1)}, bf16[256,512]{1,0:T(8,128)(2,1)S(1)}, bf16[256,512]{1,0:T(8,128)(2,1)S(1)}) custom-call(s32[2]{0:T(128)S(1)} %pad_add_fusion.refs_0_.meta, bf16[256,512]{1,0:T(8,128)(2,1)S(1)} %get-tuple-element.56.refs_1_, ...), custom_call_target="tpu_custom_call" | custom-call | flops 8388608 | bytes 20480 | tf_op jit(solution)/shard_map/layer_project_1/pallas_call | solution.py:121
  53.4 1.8 %layer_gather_1.1.refs_1_ = bf16[8,256,512]{2,1,0:T(8,128)(2,1)S(1)} custom-call(s32[2]{0:T(128)S(1)} %pad_add_fusion.refs_0_.meta, bf16[256,512]{1,0:T(8,128)(2,1)S(1)} %get-tuple-element.59.refs_1_, bf16[256,512]{1,0:T(8,128)(2,1)S(1)} %get-tuple-element.60.refs_2_, s32[8,512]{1,0:T(8,128)S(1)} %bitcast.21), custom_call_target="tpu_custom_call" | custom-call | flops 16777216 | bytes 32768 | tf_op jit(solution)/shard_map/layer_gather_1/pallas_call | solution.py:121
  55.3 1.3 %collective-permute-done.12.refs_4_ = bf16[64,512]{1,0:T(8,128)(2,1)S(1)} collective-permute-done((bf16[64,512]{1,0:T(8,128)(2,1)S(1)}, bf16[64,512]{1,0:T(8,128)(2,1)S(1)}, u32[]{:S(2)}, u32[]{:S(2)}) %collective-permute-start.12) | collective-permute-done | bytes 65568 | tf_op jit(solution)/shard_map/ppermute | solution.py:51
  56.5 2.0 %layer_sum_1.1.refs_5_ = bf16[256,512]{1,0:T(8,128)(2,1)S(1)} custom-call(s32[2]{0:T(128)S(1)} %pad_add_fusion.refs_0_.meta, bf16[8,256,512]{2,1,0:T(8,128)(2,1)S(1)} %layer_gather_1.1.refs_1_, bf16[256,512]{1,0:T(8,128)(2,1)S(1)} %get-tuple-element.61.refs_2_, bf16[64,512]{1,0:T(8,128)(2,1)S(1)} %collective-permute-done.11.refs_3_, ...), custom_call_target="tpu_custom_call" | custom-call | flops 4194304 | bytes 4096 | tf_op jit(solution)/shard_map/layer_sum_1/pallas_call | solution.py:121
  58.5 3.6 %collective-permute-start.13 = (bf16[256,512]{1,0:T(8,128)(2,1)S(1)}, bf16[256,512]{1,0:T(8,128)(2,1)S(1)}, u32[]{:S(2)}, u32[]{:S(2)}) collective-permute-start(bf16[256,512]{1,0:T(8,128)(2,1)S(1)} %layer_sum_1.1.refs_5_), channel_id=1, source_target_pairs={{0,1},{1,0},{2,3},{3,2},{4,5},{5,4},{6,7},{7,6},{8,9},{9,8},{10,11... | collective-permute-start | bytes 786440 | tf_op jit(solution)/shard_map/ppermute | solution.py:22
  63.3 2.2 %last_update.1 = (bf16[512,256]{1,0:T(8,128)(2,1)}, bf16[512,512]{1,0:T(8,128)(2,1)S(1)}) custom-call(s32[2]{0:T(128)S(1)} %pad_add_fusion.refs_0_.meta, bf16[256,512]{1,0:T(8,128)(2,1)S(1)} %get-tuple-element.56.refs_1_, bf16[256,512]{1,0:T(8,128)(2,1)S(1)} %collective-permute-done.10.refs_2_, bf16[256,512]{1,0:T(8,128)(2,1)S(1)} %get-tuple-element.57.refs_3_, ...), custom_call_target="tpu_custom_call" | custom-call | flops 8388608 | bytes 12288 | tf_op jit(solution)/shard_map/last_update/pallas_call | solution.py:121
  67.0 4.4 %decode_prepare.1 = (bf16[512,512]{1,0:T(8,128)(2,1)S(1)}, bf16[1024,512]{1,0:T(8,128)(2,1)S(1)}, bf16[1024,512]{1,0:T(8,128)(2,1)S(1)}, bf16[1024,256]{1,0:T(8,128)(2,1)S(1)}) custom-call(s32[2]{0:T(128)S(1)} %pad_add_fusion.refs_0_.meta, bf16[1024,256]{1,0:T(8,128)(2,1)S(1)} %copy-done.5, bf16[1024,256]{1,0:T(8,128)(2,1)S(1)} %collective-permute-done.refs_2_, ...), custom_call_target="tpu_custom_call" | custom-call | flops 50331648 | bytes 49152 | tf_op jit(solution)/shard_map/decode_prepare/pallas_call | solution.py:121
  71.4 1.7 %decode_own.1.refs_6_ = bf16[1024,512]{1,0:T(8,128)(2,1)S(1)} custom-call(s32[2]{0:T(128)S(1)} %pad_add_fusion.refs_0_.meta, bf16[512,512]{1,0:T(8,128)(2,1)S(1)} %get-tuple-element.66.refs_1_, bf16[512,512]{1,0:T(8,128)(2,1)S(1)} %get-tuple-element.69.refs_2_, s32[5,1,1024]{2,1,0:T(1,128)S(1)} %bitcast.23, s32[5,1,1024]{2,1,0:T(1,128)S(1)} %bitcast.11, ...), custom_call_target="tpu_custom_call" | custom-call | flops 12582912 | bytes 16384 | tf_op jit(solution)/shard_map/decode_own/pallas_call | solution.py:121
  73.1 15.5 %collective-permute-done.16.refs_1_ = bf16[512,512]{1,0:T(8,128)(2,1)S(1)} collective-permute-done((bf16[512,512]{1,0:T(8,128)(2,1)S(1)}, bf16[512,512]{1,0:T(8,128)(2,1)S(1)}, u32[]{:S(2)}, u32[]{:S(2)}) %collective-permute-start.16) | collective-permute-done | bytes 524320 | tf_op jit(solution)/shard_map/ppermute | solution.py:51
  88.6 2.5 %decode_near.1.refs_6_.refs_4_ = bf16[1024,512]{1,0:T(8,128)(2,1)S(1)} custom-call(s32[2]{0:T(128)S(1)} %pad_add_fusion.refs_0_.meta, bf16[512,512]{1,0:T(8,128)(2,1)S(1)} %collective-permute-done.16.refs_1_, bf16[1024,512]{1,0:T(8,128)(2,1)S(1)} %get-tuple-element.68.refs_2_, s32[5,1,1024]{2,1,0:T(1,128)S(1)} %bitcast.24, s32[5,1,1024]{2,1,0:T(1,128)S(1)} %bitcast.12, ...), custom_call_target="tpu_custom_call" | custom-call | flops 25165824 | bytes 16384 | tf_op jit(solution)/shard_map/decode_near/pallas_call | solution.py:121
  91.1 1.9 %decode_skip.1 = (bf16[512,512]{1,0:T(8,128)(2,1)S(1)}, bf16[1024,512]{1,0:T(8,128)(2,1)S(1)}) custom-call(s32[2]{0:T(128)S(1)} %pad_add_fusion.refs_0_.meta, bf16[512,512]{1,0:T(8,128)(2,1)S(1)} %collective-permute-done.15.refs_1_, bf16[1024,512]{1,0:T(8,128)(2,1)S(1)} %get-tuple-element.67.refs_2_, s32[5,1,1024]{2,1,0:T(1,128)S(1)} %bitcast.25, ...), custom_call_target="tpu_custom_call" | custom-call | flops 25165824 | bytes 24576 | tf_op jit(solution)/shard_map/decode_skip/pallas_call | solution.py:121
  95.0 1.7 %final_update_0.1.refs_0_ = bf16[1024,256]{1,0:T(8,128)(2,1)} custom-call(s32[2]{0:T(128)S(1)} %pad_add_fusion.refs_0_.meta, bf16[1024,256]{1,0:T(8,128)(2,1)S(1)} %copy-done.5, bf16[1024,256]{1,0:T(8,128)(2,1)S(1)} %get-tuple-element.65.self_term, bf16[512,512]{1,0:T(8,128)(2,1)S(1)} %get-tuple-element.71.sum_own, ...), custom_call_target="tpu_custom_call" | custom-call | tf_op jit(solution)/shard_map/final_update_0/pallas_call | solution.py:643
  96.7 1.7 %final_update_1.1 = bf16[1024,256]{1,0:T(8,128)(2,1)} custom-call(s32[2]{0:T(128)S(1)} %pad_add_fusion.refs_0_.meta, bf16[1024,256]{1,0:T(8,128)(2,1)S(1)} %copy-done.5, bf16[1024,256]{1,0:T(8,128)(2,1)S(1)} %get-tuple-element.65.self_term, bf16[512,512]{1,0:T(8,128)(2,1)S(1)} %decode_rest.1.sum_own, ...), custom_call_target="tpu_custom_call", output_to_operand_aliasing={{}: (6, {})} | custom-call | tf_op jit(solution)/shard_map/final_update_1/pallas_call | solution.py:643
  (65 shorter events, 15.0 us)
Async XLA Ops:
  0.6 7.1 %copy-start.11 = (s32[1,5,512]{2,0,1:T(1,128)S(1)}, s32[1,5,512]{2,0,1:T(1,128)}, u32[]{:S(2)}) copy-start(s32[1,5,512]{2,0,1:T(1,128)} %param.18) | copy-start | bytes 30724
  0.6 7.1 %collective-permute-start.2 = (bf16[4,512,256]{2,1,0:T(8,128)(2,1)}, bf16[4,512,256]{2,1,0:T(8,128)(2,1)S(1)}, u32[]{:S(2)}, u32[]{:S(2)}) collective-permute-start(bf16[4,512,256]{2,1,0:T(8,128)(2,1)} %refs_6_.1), channel_id=1, source_target_pairs={{0,1},{1,0},{2,3},{3,2},{4,5},{5,4},{6,7},{7,6},{8,9},{9,8},{10,11... | collective-permute-start | bytes 3145736 | tf_op jit(solution)/shard_map/ppermute | solution.py:22
  4.0 3.7 %collective-permute-start = (bf16[1024,256]{1,0:T(8,128)(2,1)}, bf16[1024,256]{1,0:T(8,128)(2,1)S(1)}, u32[]{:S(2)}, u32[]{:S(2)}) collective-permute-start(bf16[1024,256]{1,0:T(8,128)(2,1)} %own.3), channel_id=1, source_target_pairs={{0,1},{1,0},{2,3},{3,2},{4,5},{5,4},{6,7},{7,6},{8,9},{9,8},{10,11... | collective-permute-start | bytes 1572872 | tf_op jit(solution)/shard_map/ppermute | solution.py:22
  4.1 3.6 %collective-permute-start.1 = (bf16[512,256]{1,0:T(8,128)(2,1)}, bf16[512,256]{1,0:T(8,128)(2,1)S(1)}, u32[]{:S(2)}, u32[]{:S(2)}) collective-permute-start(bf16[512,256]{1,0:T(8,128)(2,1)} %refs_1_.8), channel_id=1, source_target_pairs={{0,1},{1,0},{2,3},{3,2},{4,5},{5,4},{6,7},{7,6},{8,9},{9,8},{10,11... | collective-permute-start | bytes 786440 | tf_op jit(solution)/shard_map/ppermute | solution.py:22
  9.7 18.8 %copy-start.14 = (s32[1,5,512]{2,0,1:T(1,128)S(1)}, s32[1,5,512]{2,0,1:T(1,128)}, u32[]{:S(2)}) copy-start(s32[1,5,512]{2,0,1:T(1,128)} %param.20) | copy-start | bytes 30724
  9.7 23.6 %collective-permute-start.6 = (bf16[2,4,512,256]{3,2,1,0:T(8,128)(2,1)S(1)}, bf16[2,4,512,256]{3,2,1,0:T(8,128)(2,1)S(1)}, u32[]{:S(2)}, u32[]{:S(2)}) collective-permute-start(bf16[2,4,512,256]{3,2,1,0:T(8,128)(2,1)S(1)} %copy-done), channel_id=1, source_target_pairs={{0,1},{1,0},{2,3},{3,2},{4,5},{5,4},{6,7},{7,6},{8,9},{9,8},{10,11... | collective-permute-start | bytes 6291464 | tf_op jit(solution)/shard_map/ppermute | solution.py:22
  10.0 18.4 %collective-permute-start.3 = (bf16[512,512]{1,0:T(8,128)(2,1)S(1)}, bf16[512,512]{1,0:T(8,128)(2,1)S(1)}, u32[]{:S(2)}, u32[]{:S(2)}) collective-permute-start(bf16[512,512]{1,0:T(8,128)(2,1)S(1)} %get-tuple-element.39), channel_id=1, source_target_pairs={{0,2},{1,0},{2,4},{3,1},{4,6},{5,3},{6,8},{7,5},{8,10},{9,7},{10,1... | collective-permute-start | bytes 1572872 | tf_op jit(solution)/shard_map/ppermute | solution.py:51
  12.3 18.3 %collective-permute-start.4 = (bf16[512,512]{1,0:T(8,128)(2,1)S(1)}, bf16[512,512]{1,0:T(8,128)(2,1)S(1)}, u32[]{:S(2)}, u32[]{:S(2)}) collective-permute-start(bf16[512,512]{1,0:T(8,128)(2,1)S(1)} %get-tuple-element.44), channel_id=1, source_target_pairs={{0,4},{1,0},{2,6},{3,2},{4,8},{5,1},{6,10},{7,3},{8,12},{9,5},{10,... | collective-permute-start | bytes 1572872 | tf_op jit(solution)/shard_map/ppermute | solution.py:51
  31.7 1.6 %collective-permute-start.5 = (bf16[256,512]{1,0:T(8,128)(2,1)S(1)}, bf16[256,512]{1,0:T(8,128)(2,1)S(1)}, u32[]{:S(2)}, u32[]{:S(2)}) collective-permute-start(bf16[256,512]{1,0:T(8,128)(2,1)S(1)} %get-tuple-element.48), channel_id=1, source_target_pairs={{0,1},{1,0},{2,3},{3,2},{4,5},{5,4},{6,7},{7,6},{8,9},{9,8},{10,11... | collective-permute-start | bytes 786440 | tf_op jit(solution)/shard_map/ppermute | solution.py:22
  34.6 28.7 %collective-permute-start.14 = (bf16[4,512,256]{2,1,0:T(8,128)(2,1)S(1)}, bf16[4,512,256]{2,1,0:T(8,128)(2,1)S(1)}, u32[]{:S(2)}, u32[]{:S(2)}) collective-permute-start(bf16[4,512,256]{2,1,0:T(8,128)(2,1)S(1)} %copy-done.1), channel_id=1, source_target_pairs={{0,1},{1,0},{2,3},{3,2},{4,5},{5,4},{6,7},{7,6},{8,9},{9,8},{10,11... | collective-permute-start | bytes 3145736 | tf_op jit(solution)/shard_map/ppermute | solution.py:22
  34.7 2.9 %collective-permute-start.7 = (bf16[256,512]{1,0:T(8,128)(2,1)S(1)}, bf16[256,512]{1,0:T(8,128)(2,1)S(1)}, u32[]{:S(2)}, u32[]{:S(2)}) collective-permute-start(bf16[256,512]{1,0:T(8,128)(2,1)S(1)} %get-tuple-element.50.refs_1_.refs_7_), channel_id=1, source_target_pairs={{0,1},{1,0},{2,3},{3,2},{4,5},{5,4},{6,7},{7,6},{8,9},{9,8},{10,11... | collective-permute-start | bytes 786440 | tf_op jit(solution)/shard_map/ppermute | solution.py:22
  35.1 5.7 %collective-permute-start.8 = (bf16[64,512]{1,0:T(8,128)(2,1)S(1)}, bf16[64,512]{1,0:T(8,128)(2,1)S(1)}, u32[]{:S(2)}, u32[]{:S(2)}) collective-permute-start(bf16[64,512]{1,0:T(8,128)(2,1)S(1)} %get-tuple-element.54), channel_id=1, source_target_pairs={{1,2},{2,1},{3,4},{4,3},{5,6},{6,5},{7,8},{8,7},{9,10},{10,9},{11,... | collective-permute-start | bytes 196616 | tf_op jit(solution)/shard_map/ppermute | solution.py:51
  37.0 7.8 %collective-permute-start.9 = (bf16[64,512]{1,0:T(8,128)(2,1)S(1)}, bf16[64,512]{1,0:T(8,128)(2,1)S(1)}, u32[]{:S(2)}, u32[]{:S(2)}) collective-permute-start(bf16[64,512]{1,0:T(8,128)(2,1)S(1)} %get-tuple-element.54), channel_id=1, source_target_pairs={{1,3},{0,1},{3,5},{2,0},{5,7},{4,2},{7,9},{6,4},{9,11},{8,6},{11,1... | collective-permute-start | bytes 196616 | tf_op jit(solution)/shard_map/ppermute | solution.py:51
  38.9 5.9 %copy-start.13 = (s32[512,8]{0,1:T(8,128)S(1)}, s32[512,8]{0,1:T(8,128)}, u32[]{:S(2)}) copy-start(s32[512,8]{0,1:T(8,128)} %param.22) | copy-start | bytes 49156
  47.2 4.8 %collective-permute-start.10 = (bf16[256,512]{1,0:T(8,128)(2,1)S(1)}, bf16[256,512]{1,0:T(8,128)(2,1)S(1)}, u32[]{:S(2)}, u32[]{:S(2)}) collective-permute-start(bf16[256,512]{1,0:T(8,128)(2,1)S(1)} %get-tuple-element.56.refs_1_), channel_id=1, source_target_pairs={{0,1},{1,0},{2,3},{3,2},{4,5},{5,4},{6,7},{7,6},{8,9},{9,8},{10,11... | collective-permute-start | bytes 786440 | tf_op jit(solution)/shard_map/ppermute | solution.py:22
  50.8 4.4 %collective-permute-start.11 = (bf16[64,512]{1,0:T(8,128)(2,1)S(1)}, bf16[64,512]{1,0:T(8,128)(2,1)S(1)}, u32[]{:S(2)}, u32[]{:S(2)}) collective-permute-start(bf16[64,512]{1,0:T(8,128)(2,1)S(1)} %get-tuple-element.62), channel_id=1, source_target_pairs={{1,2},{2,1},{3,4},{4,3},{5,6},{6,5},{7,8},{8,7},{9,10},{10,9},{11,... | collective-permute-start | bytes 196616 | tf_op jit(solution)/shard_map/ppermute | solution.py:51
  51.5 5.1 %collective-permute-start.12 = (bf16[64,512]{1,0:T(8,128)(2,1)S(1)}, bf16[64,512]{1,0:T(8,128)(2,1)S(1)}, u32[]{:S(2)}, u32[]{:S(2)}) collective-permute-start(bf16[64,512]{1,0:T(8,128)(2,1)S(1)} %get-tuple-element.62), channel_id=1, source_target_pairs={{1,3},{0,1},{3,5},{2,0},{5,7},{4,2},{7,9},{6,4},{9,11},{8,6},{11,1... | collective-permute-start | bytes 196616 | tf_op jit(solution)/shard_map/ppermute | solution.py:51
  58.5 4.8 %collective-permute-start.13 = (bf16[256,512]{1,0:T(8,128)(2,1)S(1)}, bf16[256,512]{1,0:T(8,128)(2,1)S(1)}, u32[]{:S(2)}, u32[]{:S(2)}) collective-permute-start(bf16[256,512]{1,0:T(8,128)(2,1)S(1)} %layer_sum_1.1.refs_5_), channel_id=1, source_target_pairs={{0,1},{1,0},{2,3},{3,2},{4,5},{5,4},{6,7},{7,6},{8,9},{9,8},{10,11... | collective-permute-start | bytes 786440 | tf_op jit(solution)/shard_map/ppermute | solution.py:22
  65.5 23.1 %collective-permute-start.16 = (bf16[512,512]{1,0:T(8,128)(2,1)S(1)}, bf16[512,512]{1,0:T(8,128)(2,1)S(1)}, u32[]{:S(2)}, u32[]{:S(2)}) collective-permute-start(bf16[512,512]{1,0:T(8,128)(2,1)S(1)} %get-tuple-element.66.refs_1_), channel_id=1, source_target_pairs={{0,2},{1,0},{2,4},{3,1},{4,6},{5,3},{6,8},{7,5},{8,10},{9,7},{10,1... | collective-permute-start | bytes 1572872 | tf_op jit(solution)/shard_map/ppermute | solution.py:51
  65.9 25.2 %collective-permute-start.15 = (bf16[512,512]{1,0:T(8,128)(2,1)S(1)}, bf16[512,512]{1,0:T(8,128)(2,1)S(1)}, u32[]{:S(2)}, u32[]{:S(2)}) collective-permute-start(bf16[512,512]{1,0:T(8,128)(2,1)S(1)} %get-tuple-element.66.refs_1_), channel_id=1, source_target_pairs={{0,4},{1,0},{2,6},{3,2},{4,8},{5,1},{6,10},{7,3},{8,12},{9,5},{10,... | collective-permute-start | bytes 1572872 | tf_op jit(solution)/shard_map/ppermute | solution.py:51
  66.9 4.5 %copy-start.8 = (s32[1,5,1024]{2,0,1:T(1,128)S(1)}, s32[1,5,1024]{2,0,1:T(1,128)}, u32[]{:S(2)}) copy-start(s32[1,5,1024]{2,0,1:T(1,128)} %param.25) | copy-start | bytes 61444
  66.9 4.5 %copy-start.10 = (s32[1,5,1024]{2,0,1:T(1,128)S(1)}, s32[1,5,1024]{2,0,1:T(1,128)}, u32[]{:S(2)}) copy-start(s32[1,5,1024]{2,0,1:T(1,128)} %param.23) | copy-start | bytes 61444
  93.0 2.0 %collective-permute-start.18 = (bf16[512,512]{1,0:T(8,128)(2,1)S(1)}, bf16[512,512]{1,0:T(8,128)(2,1)S(1)}, u32[]{:S(2)}, u32[]{:S(2)}) collective-permute-start(bf16[512,512]{1,0:T(8,128)(2,1)S(1)} %get-tuple-element.71.sum_own), channel_id=1, source_target_pairs={{0,1},{1,0},{2,3},{3,2},{4,5},{5,4},{6,7},{7,6},{8,9},{9,8},{10,11... | collective-permute-start | bytes 1572872 | tf_op jit(solution)/shard_map/ppermute | solution.py:22
  94.4 2.3 %collective-permute-start.17 = (bf16[512,512]{1,0:T(8,128)(2,1)S(1)}, bf16[512,512]{1,0:T(8,128)(2,1)S(1)}, u32[]{:S(2)}, u32[]{:S(2)}) collective-permute-start(bf16[512,512]{1,0:T(8,128)(2,1)S(1)} %decode_rest.1.sum_own), channel_id=1, source_target_pairs={{0,1},{1,0},{2,3},{3,2},{4,5},{5,4},{6,7},{7,6},{8,9},{9,8},{10,11... | collective-permute-start | bytes 1572872 | tf_op jit(solution)/shard_map/ppermute | solution.py:22
  (10 other events, 24.2 us)
where the time goes:
time: 98.5 us; the launch traced here: 98.3 us
  waiting for transfers between devices  40.8 us (41%)
  Pallas kernels  37.2 us (38%)
  starting transfers between devices  17 us (17%)
  local copies, waits for them, and re-layouts  2.39 us (2%)
    ppermute x8, waiting for transfers between devices, exchange(): return lax.ppermute(value, ('band', 'feat'), pairs(lax.axis_size('band')))  36.8 us
    pallas_call x18, Pallas kernels, call(): pl.pallas_call(viewed, name=name, grid=(1,), in_specs=[spec.spec if isins...  33.9 us
    ppermute x11, starting transfers between devices, swap(): return lax.ppermute(value, 'feat', [(0, 1), (1, 0)])  12.7 us
    ppermute x8, starting transfers between devices, exchange(): return lax.ppermute(value, ('band', 'feat'), pairs(lax.axis_size('band')))  4.28 us
    ppermute x11, waiting for transfers between devices, swap(): return lax.ppermute(value, 'feat', [(0, 1), (1, 0)])  3.91 us
    pallas_call x2, Pallas kernels, body(): pl.pallas_call(functools.partial(final_kernel, index * half), name=f'fina...  3.31 us
    unnamed x30, local copies, waits for them, and re-layouts  2.39 us
  transfers between devices with their start and end apart: 19, of which 9 were waited for; matrix products, arithmetic and copies ran while one was open for 0% of the time, Pallas kernels for 29%

commit v1 on v0

--- a/solution.py
+++ b/solution.py
@@ -11,6 +11,7 @@
 LAYERS = 2
 MARGIN = 64
 HALF = 256
+HELD = HALF + MARGIN
 LANES = 128
 F32 = jnp.float32
 BF16 = jnp.bfloat16
@@ -36,15 +37,19 @@
 
 near_shift = functools.partial(shift, 1, 0)
 skip_shift = functools.partial(shift, 2, 0)
-halo_shift = functools.partial(shift, 1, 1)
-
-
-def halo_pairs(count):
+
+
+def cross_pairs(count):
     partners = {}
     for s in range(count):
-        partners[s, 1] = ((s + 1) % count, 0)
-        partners[(s + 1) % count, 0] = (s, 1)
+        other = s + 1 if s % 2 else s - 1
+        for c in range(2):
+            partners[s, c] = (other, c) if 0 <= other < count else (s, 1 - c)
     return flat(partners)
+
+
+def line_pairs(count):
+    return flat({(s, c): (s ^ 1, c) for s in range(count) for c in range(2)})
 
 
 def exchange(value, pairs):
@@ -71,6 +76,14 @@
 
 def window(index, size=HALF):
     return pl.ds(pl.multiple_of(index * size, size), size)
+
+
+def extra_rows(meta):
+    return pl.ds(pl.multiple_of((1 - meta[0]) * (HALF - MARGIN), MARGIN), MARGIN)
+
+
+def margin_rows(meta):
+    return pl.ds(pl.multiple_of((1 - meta[0]) * (2 * HALF - MARGIN), MARGIN), MARGIN)
 
 
 def near_offset(meta):
@@ -149,9 +162,7 @@
 
 
 def encode_begin_kernel(meta, own, w_own, out):
-    for start in range(0, own.shape[0], HALF):
-        rows = pl.ds(start, HALF)
-        out[rows, :] = dot(own[rows, :], w_own[window(meta[0]), :])
+    out[...] = dot(own[pl.ds(0, HALF), :], w_own[window(meta[0]), :])
 
 
 def gather_slots(senders_row, sent, out):
@@ -165,7 +176,8 @@
     for start in range(0, own.shape[0], HALF):
         rows = pl.ds(start, HALF)
         a, b = own[rows, :], other[rows, :]
-        sent[rows, mine] = (begun[rows, :] + dot(b, w_own[rest, :])).astype(BF16)
+        first = begun[...] if start == 0 else dot(a, w_own[mine, :])
+        sent[rows, mine] = (first + dot(b, w_own[rest, :])).astype(BF16)
         sent[rows, rest] = (dot(a, w_other[mine, :]) + dot(b, w_other[rest, :])).astype(BF16)
     gather_slots(senders[near_offset(meta)], sent, piece)
 
@@ -204,35 +216,55 @@
         value = value + dot(hot_rows(own_row - start, HALF), own_message[...])
         total[pl.ds(start, HALF), :] = value
     gather_slots(targets[skip_offset(meta)], recv, before_skip)
-    a, b = own[mine, :], other[mine, :]
-    self_term[:, mine] = (dot(a, w2[mine, :]) + dot(b, w2[rest, :])).astype(BF16)
-    self_term[:, rest] = (dot(a, w2_other[mine, :]) + dot(b, w2_other[rest, :])).astype(BF16)
-
-
-def encode_skip_sum_kernel(meta, rows, before, targets, live, total, out_own, out_other, message):
+    far = margin_rows(meta)
+    for held, rows in ((pl.ds(0, HALF), mine), (pl.ds(HALF, MARGIN), far)):
+        a, b = own[rows, :], other[rows, :]
+        self_term[held, mine] = (dot(a, w2[mine, :]) + dot(b, w2[rest, :])).astype(BF16)
+        self_term[held, rest] = (dot(a, w2_other[mine, :]) + dot(b, w2_other[rest, :])).astype(BF16)
+
+
+def encode_skip_sum_kernel(
+    meta, rows, before, targets, live, total, out_own, out_other, message, halves
+):
     message[...] = silu_message(rows[...] + before[...])
     row = live_targets(targets, live, skip_offset(meta))
-    for out, half in ((out_other, 1 - meta[0]), (out_own, meta[0])):
+    for index, half in enumerate((1 - meta[0], meta[0])):
         value = dot(hot_rows(row - half * HALF, HALF), message[...]) + total[window(half), :]
-        out[...] = value.astype(out.dtype)
-
-
-def put_edge(meta, now, w0, w0_other, edge):
-    mine, rest = window(meta[0]), window(1 - meta[0])
-    rows = now[pl.ds(pl.multiple_of(meta[0] * (HALF - MARGIN), MARGIN), MARGIN), :]
-    edge[:, mine] = dot(rows, w0[...]).astype(BF16)
-    edge[:, rest] = dot(rows, w0_other[...]).astype(BF16)
+        halves[index] = value.astype(BF16)
+    held, far = pl.ds(0, HALF), pl.ds(HALF, MARGIN)
+    out_own[held, :] = halves[1]
+    out_own[far, :] = halves[0, extra_rows(meta), :]
+    out_other[held, :] = halves[0]
+    start = pl.multiple_of(meta[0] * (HALF - MARGIN), MARGIN)
+    out_other[far, :] = halves[1, pl.ds(start, MARGIN), :]
+
+
+def put_edges(meta, now, w0, w0_other, cross, line):
+    mine, rest = window(meta[0]), window(1 - meta[0])
+    odd = meta[1] % 2
+    head, tail = HALF * meta[0], HALF - MARGIN * meta[0]
+    for edge, start in (
+        (cross, (1 - odd) * head + odd * tail),
+        (line, (1 - odd) * tail + odd * head),
+    ):
+        rows = now[pl.ds(pl.multiple_of(start, MARGIN), MARGIN), :]
+        edge[:, mine] = dot(rows, w0[...]).astype(BF16)
+        edge[:, rest] = dot(rows, w0_other[...]).astype(BF16)
 
 
 def encode_update_kernel(
-    meta, own, other, self_term, sum_own, sum_other, w3, w3_other, w0, w0_other, now, edge
-):
-    mine, rest = window(meta[0]), window(1 - meta[0])
-    summed = (sum_own[...] + sum_other[...].astype(F32)).astype(BF16)
+    meta, own, other, self_term, sum_own, sum_other, w3, w3_other, w0, w0_other,
+    now, cross, line, held_now,
+):
+    mine, rest = window(meta[0]), window(1 - meta[0])
+    summed = sum_own[...] + sum_other[...]
+    far = margin_rows(meta)
     for cols, latent, w in ((mine, own, w3), (rest, other, w3_other)):
-        step = silu(self_term[:, cols] + dot(summed, w[...]))
-        now[:, cols] = (latent[mine, :].astype(F32) + step).astype(BF16)
-    put_edge(meta, now, w0, w0_other, edge)
+        step = silu(self_term[:, cols].astype(F32) + dot(summed, w[...]))
+        for held, rows in ((slice(0, HALF), mine), (slice(HALF, HELD), far)):
+            held_now[held, cols] = (latent[rows, :].astype(F32) + step[held, :]).astype(BF16)
+    now[...] = held_now[pl.ds(0, HALF), :]
+    put_edges(meta, held_now, w0, w0_other, cross, line)
 
 
 def layer_project_kernel(
@@ -240,51 +272,64 @@
     sent_own, sent_other, recv, self_own, *self_other,
 ):
     mine, rest = window(meta[0]), window(1 - meta[0])
+    held, far = pl.ds(0, HALF), pl.ds(HALF, MARGIN)
     for cols, w in ((mine, w0), (rest, w0_other)):
         sent_own[:, cols] = dot(own[...], w[...]).astype(BF16)
         sent_other[:, cols] = dot(other[...], w[...]).astype(BF16)
     for cols, w in ((mine, w1), (rest, w1_other)):
-        recv[:, cols] = dot(own[...], w[...]).astype(BF16)
+        recv[held, cols] = dot(own[...], w[...]).astype(BF16)
+        if not last:
+            recv[far, cols] = dot(other[extra_rows(meta), :], w[...]).astype(BF16)
     for cols, w in ((mine, w2), (rest, w2_other)):
-        self_own[:, cols] = dot(own[...], w[...]).astype(BF16)
+        self_own[held, cols] = dot(own[...], w[...]).astype(BF16)
         if last:
             self_other[0][:, cols] = dot(other[...], w[...]).astype(BF16)
+        else:
+            self_own[far, cols] = dot(other[extra_rows(meta), :], w[...]).astype(BF16)
+
+
+def held_slots(meta, slots):
+    tail = pltpu.roll(slots[:, 2 * HALF - LANES :], LANES - MARGIN, 1)
+    far = jnp.where(meta[0] == 0, tail, slots[:, :LANES])
+    return jnp.concatenate([slots[:, window(meta[0])], far], axis=1)
 
 
 def layer_gather_kernel(meta, own, other, senders, out):
-    mine = window(meta[0])
     base = meta[1] * (2 * HALF)
+    nodes = out.shape[1]
+    held = held_slots(meta, senders) - base
     for k in range(senders.shape[0]):
-        local = senders[k : k + 1, mine] - base
-        col = column(local - meta[0] * HALF)
-        col_other = column(local - (1 - meta[0]) * HALF)
+        local = held[k : k + 1, :]
+        col = column(local - meta[0] * HALF)[:nodes]
+        col_other = column(local - (1 - meta[0]) * HALF)[:nodes]
         value = dot(hot_columns(col, HALF), own[...])
         value = value + dot(hot_columns(col_other, HALF), other[...])
         out[k] = value.astype(BF16)
 
 
-def layer_sum(meta, gathered, recv, near, far, senders, live, halo, total):
-    mine = window(meta[0])
+def layer_sum(meta, gathered, recv, cross, line, senders, live, halo, total):
     nodes = 2 * HALF
     base = meta[1] * nodes
-    count = senders.shape[0]
+    count, held = gathered.shape[0], gathered.shape[1]
     hots, flags = [], []
+    slots, alive = held_slots(meta, senders) - base, held_slots(meta, live)
     for k in range(count):
-        local = senders[k : k + 1, mine] - base
+        local = slots[k : k + 1, :]
         where = jnp.where(local < 0, local + MARGIN, local - nodes + MARGIN)
         where = jnp.where((local >= 0) & (local < nodes), -1, where)
-        hots.append(hot_columns(column(where), 2 * MARGIN))
-        flags.append(column(live[k : k + 1, mine]).astype(BF16))
-    halo[pl.ds(pl.multiple_of(meta[0] * MARGIN, MARGIN), MARGIN), :] = near[...]
-    halo[pl.ds(pl.multiple_of((1 - meta[0]) * MARGIN, MARGIN), MARGIN), :] = far[...]
+        hots.append(hot_columns(column(where)[:held], 2 * MARGIN))
+        flags.append(column(alive[k : k + 1, :])[:held].astype(BF16))
+    odd = meta[1] % 2
+    halo[pl.ds(pl.multiple_of(odd * MARGIN, MARGIN), MARGIN), :] = cross[...]
+    halo[pl.ds(pl.multiple_of((1 - odd) * MARGIN, MARGIN), MARGIN), :] = line[...]
     outside = dot(jnp.concatenate(hots, axis=0), halo[...]).astype(BF16)
     step = 32
-    for start in range(0, HALF, step):
+    for start in range(0, held, step):
         rows = pl.ds(start, step)
         side = recv[rows, :]
         running = None
         for k in range(count):
-            row = k * HALF + start
+            row = k * held + start
             message = silu_message(outside[row : row + step, :] + gathered[k, rows, :] + side)
             flag = jnp.concatenate([flags[k][start : start + step, :]] * 4, axis=1)
             message = (message * flag).astype(F32)
@@ -293,20 +338,23 @@
 
 
 def layer_update_kernel(
-    meta, gathered, recv, near, far, senders, live, now, self_term, w3, w3_other, w0, w0_other,
-    out, edge, halo, total,
-):
-    mine, rest = window(meta[0]), window(1 - meta[0])
-    layer_sum(meta, gathered, recv, near, far, senders, live, halo, total)
+    meta, gathered, recv, line, cross, senders, live, now, now_other, self_term,
+    w3, w3_other, w0, w0_other, out, edge_cross, edge_line, halo, total, held_now,
+):
+    mine, rest = window(meta[0]), window(1 - meta[0])
+    layer_sum(meta, gathered, recv, cross, line, senders, live, halo, total)
     summed = total[...]
     for cols, w in ((mine, w3), (rest, w3_other)):
-        step = silu(self_term[:, cols] + dot(summed, w[...]))
-        out[:, cols] = (now[:, cols].astype(F32) + step).astype(BF16)
-    put_edge(meta, out, w0, w0_other, edge)
-
-
-def layer_sum_kernel(meta, gathered, recv, near, far, senders, live, out, halo):
-    layer_sum(meta, gathered, recv, near, far, senders, live, halo, out)
+        step = silu(self_term[:, cols].astype(F32) + dot(summed, w[...]))
+        far = now_other[extra_rows(meta), cols].astype(F32)
+        held_now[pl.ds(0, HALF), cols] = (now[:, cols].astype(F32) + step[:HALF]).astype(BF16)
+        held_now[pl.ds(HALF, MARGIN), cols] = (far + step[HALF:]).astype(BF16)
+    out[...] = held_now[pl.ds(0, HALF), :]
+    put_edges(meta, held_now, w0, w0_other, edge_cross, edge_line)
+
+
+def layer_sum_kernel(meta, gathered, recv, cross, line, senders, live, out, halo):
+    layer_sum(meta, gathered, recv, cross, line, senders, live, halo, out)
 
 
 def last_update_kernel(
@@ -327,9 +375,10 @@
 
 
 def decode_prepare_kernel(
-    meta, own, other, w1, w1_other, w2, targets,
-    before_own, before_near, before_skip, self_term, recv,
-):
+    meta, own, other, w1, w1_other, w2, targets, mesh_now,
+    before_own, before_near, before_skip, self_term, mesh_out, recv,
+):
+    mesh_out[...] = mesh_now[...]
     mine, rest = window(meta[0]), window(1 - meta[0])
     for start in range(0, own.shape[0], HALF):
         rows = pl.ds(start, HALF)
@@ -422,8 +471,8 @@
         "encode_begin",
         (meta, grid_latent, encode_weights),
         [SMEM, whole(grid_latent), part(encode_weights, 0)],
-        [shape(grid_rows, cols, dtype=F32)],
-        2 * grid_rows * cols * cols,
+        [shape(HALF, cols, dtype=F32)],
+        2 * HALF * cols * cols,
     )
     grid_other, mesh_other = lax.optimization_barrier((grid_other, mesh_other))
     operands = (meta, grid_latent, grid_other, begun, encode_weights, encode_other, senders)
@@ -466,7 +515,7 @@
         [
             shape(mesh_rows, full, dtype=F32),
             shape(slots, full),
-            shape(HALF, full),
+            shape(HELD, full),
         ],
         2 * full * mesh_rows * slots * 3,
         [pltpu.VMEM((slots, full), BF16), pltpu.VMEM((HALF, full), BF16)],
@@ -477,32 +526,34 @@
         "encode_skip_sum",
         operands,
         [SMEM, whole(skip_rows), whole(before_skip), whole(targets), whole(live), whole(total)],
-        [shape(HALF, full, dtype=F32), shape(HALF, full)],
+        [shape(HELD, full), shape(HELD, full)],
         2 * full * mesh_rows * slots,
-        [pltpu.VMEM((slots, full), BF16)],
-    )
+        [pltpu.VMEM((slots, full), BF16), pltpu.VMEM((2, HALF, full), BF16)],
+    )
+    sum_arrived = swap(sum_other)
+    decode_other = swap(after(decode_weights, sum_other))
     operands = (
-        meta, mesh_latent, mesh_other, self_term, sum_own, swap(sum_other),
+        meta, mesh_latent, mesh_other, self_term, sum_own, sum_arrived,
         encode_weights, encode_other, layer_weights, layer_other,
     )
-    now, edge = call(
+    now, cross_edge, line_edge = call(
         encode_update_kernel,
         "encode_update",
         operands,
         [SMEM] + [whole(x) for x in operands[1:6]]
         + [part(encode_weights, 3), part(encode_other, 3)]
         + [part(layer_weights, 0, 0), part(layer_other, 0, 0)],
-        [shape(HALF, full), shape(MARGIN, full)],
+        [shape(HALF, full), shape(MARGIN, full), shape(MARGIN, full)],
         2 * HALF * full * full,
-    )
-
-    decode_other = swap(after(decode_weights, now))
+        [pltpu.VMEM((HELD, full), BF16)],
+    )
+
     senders_t, live_t = mesh_senders.T, mesh_live.T
     degree = senders_t.shape[0]
     for layer in range(LAYERS):
         last = layer == LAYERS - 1
-        far = exchange(edge, halo_shift)
-        near = exchange(edge, halo_pairs)
+        cross = exchange(cross_edge, cross_pairs)
+        line = exchange(line_edge, line_pairs)
         now_other = swap(now)
         operands = (meta, now, now_other) + (layer_weights, layer_other) * 3
         results = call(
@@ -511,7 +562,8 @@
             operands,
             [SMEM, whole(now), whole(now_other)]
             + [part(operands[3 + i], layer, i // 2) for i in range(6)],
-            [shape(HALF, full)] * (5 if last else 4),
+            [shape(HALF, full)] * 2 + [shape(HALF if last else HELD, full)] * 2
+            + [shape(HALF, full)] * last,
             2 * HALF * full * full * 4,
         )
         sent_own, sent_other, recv, self_own = results[:4]
@@ -521,10 +573,11 @@
             f"layer_gather_{layer}",
             operands,
             [SMEM, whole(sent_own), whole(sent_other), whole(senders_t)],
-            [shape(degree, HALF, full)],
+            [shape(degree, HALF if last else HELD, full)],
             2 * degree * HALF * full * mesh_rows,
         )
-        operands = (meta, gathered, recv, near, far, senders_t, live_t)
+        halo = (cross, line) if last else (line, cross)
+        operands = (meta, gathered, recv) + halo + (senders_t, live_t)
         scratch = [pltpu.VMEM((2 * MARGIN, full), BF16)]
         sum_specs = (
             [SMEM] + [whole(x) for x in operands[1:5]]
@@ -541,17 +594,17 @@
                 scratch,
             )
             continue
-        operands += (now, self_own) + (layer_weights, layer_other) * 2
-        now, edge = call(
+        operands += (now, now_other, self_own) + (layer_weights, layer_other) * 2
+        now, cross_edge, line_edge = call(
             layer_update_kernel,
             f"layer_update_{layer}",
             operands,
-            sum_specs + [whole(now), whole(self_own)]
+            sum_specs + [whole(now), whole(now_other), whole(self_own)]
             + [part(layer_weights, layer, 3), part(layer_other, layer, 3)]
             + [part(layer_weights, layer + 1, 0), part(layer_other, layer + 1, 0)],
-            [shape(HALF, full), shape(MARGIN, full)],
+            [shape(HALF, full), shape(MARGIN, full), shape(MARGIN, full)],
             2 * HALF * full * (degree * 2 * MARGIN + full),
-            scratch + [pltpu.VMEM((HALF, full), BF16)],
+            scratch + [pltpu.VMEM((HELD, full), BF16)] * 2,
         )
     operands = (
         meta, now, now_other, self_own, results[4], summed, swap(summed),
@@ -574,19 +627,22 @@
     senders, targets, live = (x.transpose(1, 0, 2) for x in (decode_senders, decode_targets, decode_live))
     slots = senders.shape[2]
     operands = (
-        meta, grid_latent, grid_other, decode_weights, decode_other, decode_weights, targets
-    )
-    before_own, before_near, before_skip, self_term = call(
+        meta, grid_latent, grid_other, decode_weights, decode_other, decode_weights, targets,
+        mesh_now,
+    )
+    before_own, before_near, before_skip, self_term, mesh_now = call(
         decode_prepare_kernel,
         "decode_prepare",
         operands,
         [SMEM, whole(grid_latent), whole(grid_other)]
-        + [part(decode_weights, 1), part(decode_other, 1), part(decode_weights, 2), whole(targets)],
+        + [part(decode_weights, 1), part(decode_other, 1), part(decode_weights, 2), whole(targets)]
+        + [whole(mesh_now)],
         [
             shape(slots // 2, full),
             shape(slots, full),
             shape(slots, full),
             shape(grid_rows, cols),
+            shape(mesh_rows, cols),
         ],
         2 * full * grid_rows * (full + 5 * slots // 2),
         [pltpu.VMEM((grid_rows, full), BF16)],

time: 98.5 us -> 95.8 us (0.973)
  the two profiles are of different devices: /device:TPU:1 before, /device:TPU:129 now
where the time goes in v1:
time: 95.8 us; the launch traced here: 95.6 us
  Pallas kernels  38.4 us (40%)
  waiting for transfers between devices  30.7 us (32%)
  starting transfers between devices  22.3 us (23%)
  local copies, waits for them, and re-layouts  3.18 us (3%)
    pallas_call x18, Pallas kernels, call(): pl.pallas_call(viewed, name=name, grid=(1,), in_specs=[spec.spec if isins...  35.1 us
    ppermute x8, waiting for transfers between devices, exchange(): return lax.ppermute(value, ('band', 'feat'), pairs(lax.axis_size('band')))  28.3 us
    ppermute x8, starting transfers between devices, exchange(): return lax.ppermute(value, ('band', 'feat'), pairs(lax.axis_size('band')))  16.5 us
    ppermute x11, starting transfers between devices, swap(): return lax.ppermute(value, 'feat', [(0, 1), (1, 0)])  5.77 us
    pallas_call x2, Pallas kernels, body(): pl.pallas_call(functools.partial(final_kernel, index * half), name=f'fina...  3.31 us
    unnamed x30, local copies, waits for them, and re-layouts  3.18 us
    ppermute x11, waiting for transfers between devices, swap(): return lax.ppermute(value, 'feat', [(0, 1), (1, 0)])  2.36 us
  transfers between devices with their start and end apart: 19, of which 8 were waited for; matrix products, arithmetic and copies ran while one was open for 0% of the time, Pallas kernels for 33%

profile of v1, /device:TPU:129, one launch (start us, length us, event | category | flops | bytes accessed | tf_op | source)
XLA Modules:
  0.0 95.6 jit_solution(7538112008640156458)
XLA Ops:
  5.9 2.0 %encode_near.1 = (bf16[1024,512]{1,0:T(8,128)(2,1)S(1)}, bf16[512,512]{1,0:T(8,128)(2,1)S(1)}) custom-call(s32[2]{0:T(128)S(1)} %pad_add_fusion.refs_0_.meta, bf16[1024,256]{1,0:T(8,128)(2,1)S(1)} %copy-done.4, bf16[1024,256]{1,0:T(8,128)(2,1)S(1)} %collective-permute-done.refs_2_, f32[256,256]{1,0:T(8,128)S(1)} %encode_begin.1.refs_3_, ...), custom_call_target="tpu_custom_call" | custom-call | flops 16777216 | bytes 24576 | tf_op jit(solution)/shard_map/encode_near/pallas_call | solution.py:134
  8.3 4.5 %collective-permute-start.4 = (bf16[512,512]{1,0:T(8,128)(2,1)S(1)}, bf16[512,512]{1,0:T(8,128)(2,1)S(1)}, u32[]{:S(2)}, u32[]{:S(2)}) collective-permute-start(bf16[512,512]{1,0:T(8,128)(2,1)S(1)} %get-tuple-element.44), channel_id=1, source_target_pairs={{0,2},{1,0},{2,4},{3,1},{4,6},{5,3},{6,8},{7,5},{8,10},{9,7},{10,1... | collective-permute-start | bytes 1572872 | tf_op jit(solution)/shard_map/ppermute | solution.py:56
  12.8 2.0 %encode_skip.1 = (bf16[512,512]{1,0:T(8,128)(2,1)S(1)}, bf16[512,512]{1,0:T(8,128)(2,1)S(1)}, bf16[512,512]{1,0:T(8,128)(2,1)S(1)}) custom-call(s32[2]{0:T(128)S(1)} %pad_add_fusion.refs_0_.meta, bf16[512,256]{1,0:T(8,128)(2,1)S(1)} %copy-done.6, bf16[512,256]{1,0:T(8,128)(2,1)S(1)} %collective-permute-done.1.refs_2_.refs_6_, ...), custom_call_target="tpu_custom_call" | custom-call | flops 16777216 | bytes 24576 | tf_op jit(solution)/shard_map/encode_skip/pallas_call | solution.py:134
  15.4 6.3 %collective-permute-done.4.refs_1_ = bf16[512,512]{1,0:T(8,128)(2,1)S(1)} collective-permute-done((bf16[512,512]{1,0:T(8,128)(2,1)S(1)}, bf16[512,512]{1,0:T(8,128)(2,1)S(1)}, u32[]{:S(2)}, u32[]{:S(2)}) %collective-permute-start.4) | collective-permute-done | bytes 524320 | tf_op jit(solution)/shard_map/ppermute | solution.py:56
  21.7 2.2 %encode_near_sum.1 = (f32[512,512]{1,0:T(8,128)S(1)}, bf16[512,512]{1,0:T(8,128)(2,1)S(1)}, bf16[320,512]{1,0:T(8,128)(2,1)S(1)}) custom-call(s32[2]{0:T(128)S(1)} %pad_add_fusion.refs_0_.meta, bf16[512,512]{1,0:T(8,128)(2,1)S(1)} %collective-permute-done.4.refs_1_, bf16[512,512]{1,0:T(8,128)(2,1)S(1)} %get-tuple-element.45.refs_2_, ...), custom_call_target="tpu_custom_call" | custom-call | flops 12582912 | bytes 29696 | tf_op jit(solution)/shard_map/encode_near_sum/pallas_call | solution.py:134
  24.0 6.2 %collective-permute-done.3.refs_1_ = bf16[512,512]{1,0:T(8,128)(2,1)S(1)} collective-permute-done((bf16[512,512]{1,0:T(8,128)(2,1)S(1)}, bf16[512,512]{1,0:T(8,128)(2,1)S(1)}, u32[]{:S(2)}, u32[]{:S(2)}) %collective-permute-start.3) | collective-permute-done | bytes 524320 | tf_op jit(solution)/shard_map/ppermute | solution.py:56
  34.5 3.8 %collective-permute-start.10 = (bf16[64,512]{1,0:T(8,128)(2,1)S(1)}, bf16[64,512]{1,0:T(8,128)(2,1)S(1)}, u32[]{:S(2)}, u32[]{:S(2)}) collective-permute-start(bf16[64,512]{1,0:T(8,128)(2,1)S(1)} %get-tuple-element.59), channel_id=1, source_target_pairs={{0,1},{1,0},{2,4},{3,5},{4,2},{5,3},{6,8},{7,9},{8,6},{9,7},{10,12... | collective-permute-start | bytes 196616 | tf_op jit(solution)/shard_map/ppermute | solution.py:56
  38.3 1.4 %layer_project_0.1 = (bf16[256,512]{1,0:T(8,128)(2,1)S(1)}, bf16[256,512]{1,0:T(8,128)(2,1)S(1)}, bf16[320,512]{1,0:T(8,128)(2,1)S(1)}, bf16[320,512]{1,0:T(8,128)(2,1)S(1)}) custom-call(s32[2]{0:T(128)S(1)} %pad_add_fusion.refs_0_.meta, bf16[256,512]{1,0:T(8,128)(2,1)S(1)} %get-tuple-element.54.refs_1_.refs_7_, ...), custom_call_target="tpu_custom_call" | custom-call | flops 8388608 | bytes 18432 | tf_op jit(solution)/shard_map/layer_project_0/pallas_call | solution.py:134
  39.7 2.1 %layer_gather_0.1.refs_1_ = bf16[8,320,512]{2,1,0:T(8,128)(2,1)S(1)} custom-call(s32[2]{0:T(128)S(1)} %pad_add_fusion.refs_0_.meta, bf16[256,512]{1,0:T(8,128)(2,1)S(1)} %get-tuple-element.55.refs_1_, bf16[256,512]{1,0:T(8,128)(2,1)S(1)} %get-tuple-element.56.refs_2_, s32[8,512]{1,0:T(8,128)S(1)} %bitcast.19), custom_call_target="tpu_custom_call" | custom-call | flops 16777216 | bytes 40960 | tf_op jit(solution)/shard_map/layer_gather_0/pallas_call | solution.py:134
  43.0 3.0 %layer_update_0.1 = (bf16[256,512]{1,0:T(8,128)(2,1)S(1)}, bf16[64,512]{1,0:T(8,128)(2,1)S(1)}, bf16[64,512]{1,0:T(8,128)(2,1)S(1)}) custom-call(s32[2]{0:T(128)S(1)} %pad_add_fusion.refs_0_.meta, bf16[8,320,512]{2,1,0:T(8,128)(2,1)S(1)} %layer_gather_0.1.refs_1_, bf16[320,512]{1,0:T(8,128)(2,1)S(1)} %get-tuple-element.57.refs_2_, ...), custom_call_target="tpu_custom_call" | custom-call | flops 6291456 | bytes 6144 | tf_op jit(solution)/shard_map/layer_update_0/pallas_call | solution.py:134
  46.0 1.6 %collective-permute-start.11 = (bf16[256,512]{1,0:T(8,128)(2,1)S(1)}, bf16[256,512]{1,0:T(8,128)(2,1)S(1)}, u32[]{:S(2)}, u32[]{:S(2)}) collective-permute-start(bf16[256,512]{1,0:T(8,128)(2,1)S(1)} %get-tuple-element.61.refs_1_), channel_id=1, source_target_pairs={{0,1},{1,0},{2,3},{3,2},{4,5},{5,4},{6,7},{7,6},{8,9},{9,8},{10,11... | collective-permute-start | bytes 786440 | tf_op jit(solution)/shard_map/ppermute | solution.py:23
  47.6 3.8 %collective-permute-start.12 = (bf16[64,512]{1,0:T(8,128)(2,1)S(1)}, bf16[64,512]{1,0:T(8,128)(2,1)S(1)}, u32[]{:S(2)}, u32[]{:S(2)}) collective-permute-start(bf16[64,512]{1,0:T(8,128)(2,1)S(1)} %get-tuple-element.67), channel_id=1, source_target_pairs={{0,1},{1,0},{2,4},{3,5},{4,2},{5,3},{6,8},{7,9},{8,6},{9,7},{10,12... | collective-permute-start | bytes 196616 | tf_op jit(solution)/shard_map/ppermute | solution.py:56
  52.8 1.9 %layer_gather_1.1.refs_1_ = bf16[8,256,512]{2,1,0:T(8,128)(2,1)S(1)} custom-call(s32[2]{0:T(128)S(1)} %pad_add_fusion.refs_0_.meta, bf16[256,512]{1,0:T(8,128)(2,1)S(1)} %get-tuple-element.64.refs_1_, bf16[256,512]{1,0:T(8,128)(2,1)S(1)} %get-tuple-element.65.refs_2_, s32[8,512]{1,0:T(8,128)S(1)} %bitcast.21), custom_call_target="tpu_custom_call" | custom-call | flops 16777216 | bytes 32768 | tf_op jit(solution)/shard_map/layer_gather_1/pallas_call | solution.py:134
  54.7 2.0 %collective-permute-done.12.refs_3_ = bf16[64,512]{1,0:T(8,128)(2,1)S(1)} collective-permute-done((bf16[64,512]{1,0:T(8,128)(2,1)S(1)}, bf16[64,512]{1,0:T(8,128)(2,1)S(1)}, u32[]{:S(2)}, u32[]{:S(2)}) %collective-permute-start.12) | collective-permute-done | bytes 65568 | tf_op jit(solution)/shard_map/ppermute | solution.py:56
  56.7 2.0 %layer_sum_1.1.refs_5_ = bf16[256,512]{1,0:T(8,128)(2,1)S(1)} custom-call(s32[2]{0:T(128)S(1)} %pad_add_fusion.refs_0_.meta, bf16[8,256,512]{2,1,0:T(8,128)(2,1)S(1)} %layer_gather_1.1.refs_1_, bf16[256,512]{1,0:T(8,128)(2,1)S(1)} %get-tuple-element.66.refs_2_, bf16[64,512]{1,0:T(8,128)(2,1)S(1)} %collective-permute-done.12.refs_3_, ...), custom_call_target="tpu_custom_call" | custom-call | flops 4194304 | bytes 4096 | tf_op jit(solution)/shard_map/layer_sum_1/pallas_call | solution.py:134
  60.8 1.8 %last_update.1 = (bf16[512,256]{1,0:T(8,128)(2,1)S(1)}, bf16[512,512]{1,0:T(8,128)(2,1)S(1)}) custom-call(s32[2]{0:T(128)S(1)} %pad_add_fusion.refs_0_.meta, bf16[256,512]{1,0:T(8,128)(2,1)S(1)} %get-tuple-element.61.refs_1_, bf16[256,512]{1,0:T(8,128)(2,1)S(1)} %collective-permute-done.11.refs_2_, bf16[256,512]{1,0:T(8,128)(2,1)S(1)} %get-tuple-element.62.refs_3_, ...), custom_call_target="tpu_custom_call" | custom-call | flops 8388608 | bytes 12288 | tf_op jit(solution)/shard_map/last_update/pallas_call | solution.py:134
  62.6 3.9 %collective-permute-start.16 = (bf16[512,512]{1,0:T(8,128)(2,1)S(1)}, bf16[512,512]{1,0:T(8,128)(2,1)S(1)}, u32[]{:S(2)}, u32[]{:S(2)}) collective-permute-start(bf16[512,512]{1,0:T(8,128)(2,1)S(1)} %get-tuple-element.72.refs_1_), channel_id=1, source_target_pairs={{0,2},{1,0},{2,4},{3,1},{4,6},{5,3},{6,8},{7,5},{8,10},{9,7},{10,1... | collective-permute-start | bytes 1572872 | tf_op jit(solution)/shard_map/ppermute | solution.py:56
  66.5 5.1 %decode_prepare.1 = (bf16[512,512]{1,0:T(8,128)(2,1)S(1)}, bf16[1024,512]{1,0:T(8,128)(2,1)S(1)}, bf16[1024,512]{1,0:T(8,128)(2,1)S(1)}, bf16[1024,256]{1,0:T(8,128)(2,1)S(1)}, bf16[512,256]{1,0:T(8,128)(2,1)}) custom-call(s32[2]{0:T(128)S(1)} %pad_add_fusion.refs_0_.meta, bf16[1024,256]{1,0:T(8,128)(2,1)S(1)} %copy-done.5, ...), custom_call_target="tpu_custom_call" | custom-call | flops 50331648 | bytes 53248 | tf_op jit(solution)/shard_map/decode_prepare/pallas_call | solution.py:134
  71.6 1.7 %decode_own.1.refs_6_ = bf16[1024,512]{1,0:T(8,128)(2,1)S(1)} custom-call(s32[2]{0:T(128)S(1)} %pad_add_fusion.refs_0_.meta, bf16[512,512]{1,0:T(8,128)(2,1)S(1)} %get-tuple-element.72.refs_1_, bf16[512,512]{1,0:T(8,128)(2,1)S(1)} %get-tuple-element.75.refs_2_, s32[5,1,1024]{2,1,0:T(1,128)S(1)} %bitcast.23, s32[5,1,1024]{2,1,0:T(1,128)S(1)} %bitcast.11, ...), custom_call_target="tpu_custom_call" | custom-call | flops 12582912 | bytes 16384 | tf_op jit(solution)/shard_map/decode_own/pallas_call | solution.py:134
  73.2 12.7 %collective-permute-done.16.refs_1_ = bf16[512,512]{1,0:T(8,128)(2,1)S(1)} collective-permute-done((bf16[512,512]{1,0:T(8,128)(2,1)S(1)}, bf16[512,512]{1,0:T(8,128)(2,1)S(1)}, u32[]{:S(2)}, u32[]{:S(2)}) %collective-permute-start.16) | collective-permute-done | bytes 524320 | tf_op jit(solution)/shard_map/ppermute | solution.py:56
  85.9 2.5 %decode_near.1.refs_6_.refs_4_ = bf16[1024,512]{1,0:T(8,128)(2,1)S(1)} custom-call(s32[2]{0:T(128)S(1)} %pad_add_fusion.refs_0_.meta, bf16[512,512]{1,0:T(8,128)(2,1)S(1)} %collective-permute-done.16.refs_1_, bf16[1024,512]{1,0:T(8,128)(2,1)S(1)} %get-tuple-element.74.refs_2_, s32[5,1,1024]{2,1,0:T(1,128)S(1)} %bitcast.24, s32[5,1,1024]{2,1,0:T(1,128)S(1)} %bitcast.12, ...), custom_call_target="tpu_custom_call" | custom-call | flops 25165824 | bytes 16384 | tf_op jit(solution)/shard_map/decode_near/pallas_call | solution.py:134
  88.4 1.9 %decode_skip.1 = (bf16[512,512]{1,0:T(8,128)(2,1)S(1)}, bf16[1024,512]{1,0:T(8,128)(2,1)S(1)}) custom-call(s32[2]{0:T(128)S(1)} %pad_add_fusion.refs_0_.meta, bf16[512,512]{1,0:T(8,128)(2,1)S(1)} %collective-permute-done.15.refs_1_, bf16[1024,512]{1,0:T(8,128)(2,1)S(1)} %get-tuple-element.73.refs_2_, s32[5,1,1024]{2,1,0:T(1,128)S(1)} %bitcast.25, ...), custom_call_target="tpu_custom_call" | custom-call | flops 25165824 | bytes 24576 | tf_op jit(solution)/shard_map/decode_skip/pallas_call | solution.py:134
  92.3 1.7 %final_update_0.1.refs_0_ = bf16[1024,256]{1,0:T(8,128)(2,1)} custom-call(s32[2]{0:T(128)S(1)} %pad_add_fusion.refs_0_.meta, bf16[1024,256]{1,0:T(8,128)(2,1)S(1)} %copy-done.5, bf16[1024,256]{1,0:T(8,128)(2,1)S(1)} %get-tuple-element.71.self_term, bf16[512,512]{1,0:T(8,128)(2,1)S(1)} %get-tuple-element.77.sum_own, ...), custom_call_target="tpu_custom_call" | custom-call | tf_op jit(solution)/shard_map/final_update_0/pallas_call | solution.py:699
  94.0 1.7 %final_update_1.1 = bf16[1024,256]{1,0:T(8,128)(2,1)} custom-call(s32[2]{0:T(128)S(1)} %pad_add_fusion.refs_0_.meta, bf16[1024,256]{1,0:T(8,128)(2,1)S(1)} %copy-done.5, bf16[1024,256]{1,0:T(8,128)(2,1)S(1)} %get-tuple-element.71.self_term, bf16[512,512]{1,0:T(8,128)(2,1)S(1)} %decode_rest.1.sum_own, ...), custom_call_target="tpu_custom_call", output_to_operand_aliasing={{}: (6, {})} | custom-call | tf_op jit(solution)/shard_map/final_update_1/pallas_call | solution.py:699
  (65 shorter events, 17.3 us)
Async XLA Ops:
  0.6 4.4 %collective-permute-start.2 = (bf16[4,512,256]{2,1,0:T(8,128)(2,1)}, bf16[4,512,256]{2,1,0:T(8,128)(2,1)S(1)}, u32[]{:S(2)}, u32[]{:S(2)}) collective-permute-start(bf16[4,512,256]{2,1,0:T(8,128)(2,1)} %refs_6_.1), channel_id=1, source_target_pairs={{0,1},{1,0},{2,3},{3,2},{4,5},{5,4},{6,7},{7,6},{8,9},{9,8},{10,11... | collective-permute-start | bytes 3145736 | tf_op jit(solution)/shard_map/ppermute | solution.py:23
  1.4 3.6 %collective-permute-start = (bf16[1024,256]{1,0:T(8,128)(2,1)}, bf16[1024,256]{1,0:T(8,128)(2,1)S(1)}, u32[]{:S(2)}, u32[]{:S(2)}) collective-permute-start(bf16[1024,256]{1,0:T(8,128)(2,1)} %own.3), channel_id=1, source_target_pairs={{0,1},{1,0},{2,3},{3,2},{4,5},{5,4},{6,7},{7,6},{8,9},{9,8},{10,11... | collective-permute-start | bytes 1572872 | tf_op jit(solution)/shard_map/ppermute | solution.py:23
  1.5 3.5 %collective-permute-start.1 = (bf16[512,256]{1,0:T(8,128)(2,1)}, bf16[512,256]{1,0:T(8,128)(2,1)S(1)}, u32[]{:S(2)}, u32[]{:S(2)}) collective-permute-start(bf16[512,256]{1,0:T(8,128)(2,1)} %refs_1_.8), channel_id=1, source_target_pairs={{0,1},{1,0},{2,3},{3,2},{4,5},{5,4},{6,7},{7,6},{8,9},{9,8},{10,11... | collective-permute-start | bytes 786440 | tf_op jit(solution)/shard_map/ppermute | solution.py:23
  4.2 8.6 %copy-start.12 = (s32[1,5,512]{2,0,1:T(1,128)S(1)}, s32[1,5,512]{2,0,1:T(1,128)}, u32[]{:S(2)}) copy-start(s32[1,5,512]{2,0,1:T(1,128)} %param.19) | copy-start | bytes 30724
  5.0 7.8 %copy-start.2 = (bf16[4,512,256]{2,1,0:T(8,128)(2,1)S(1)}, bf16[4,512,256]{2,1,0:T(8,128)(2,1)}, u32[]{:S(2)}) copy-start(bf16[4,512,256]{2,1,0:T(8,128)(2,1)} %refs_6_.1) | copy-start | bytes 3145732
  5.0 7.8 %copy-start.6 = (bf16[512,256]{1,0:T(8,128)(2,1)S(1)}, bf16[512,256]{1,0:T(8,128)(2,1)}, u32[]{:S(2)}) copy-start(bf16[512,256]{1,0:T(8,128)(2,1)} %refs_1_.8) | copy-start | bytes 786436
  7.9 13.9 %copy-start.14 = (s32[1,5,512]{2,0,1:T(1,128)S(1)}, s32[1,5,512]{2,0,1:T(1,128)}, u32[]{:S(2)}) copy-start(s32[1,5,512]{2,0,1:T(1,128)} %param.20) | copy-start | bytes 30724
  7.9 25.0 %collective-permute-start.7 = (bf16[2,4,512,256]{3,2,1,0:T(8,128)(2,1)S(1)}, bf16[2,4,512,256]{3,2,1,0:T(8,128)(2,1)S(1)}, u32[]{:S(2)}, u32[]{:S(2)}) collective-permute-start(bf16[2,4,512,256]{3,2,1,0:T(8,128)(2,1)S(1)} %copy-done), channel_id=1, source_target_pairs={{0,1},{1,0},{2,3},{3,2},{4,5},{5,4},{6,7},{7,6},{8,9},{9,8},{10,11... | collective-permute-start | bytes 6291464 | tf_op jit(solution)/shard_map/ppermute | solution.py:23
  8.3 13.4 %collective-permute-start.4 = (bf16[512,512]{1,0:T(8,128)(2,1)S(1)}, bf16[512,512]{1,0:T(8,128)(2,1)S(1)}, u32[]{:S(2)}, u32[]{:S(2)}) collective-permute-start(bf16[512,512]{1,0:T(8,128)(2,1)S(1)} %get-tuple-element.44), channel_id=1, source_target_pairs={{0,2},{1,0},{2,4},{3,1},{4,6},{5,3},{6,8},{7,5},{8,10},{9,7},{10,1... | collective-permute-start | bytes 1572872 | tf_op jit(solution)/shard_map/ppermute | solution.py:56
  14.8 15.3 %collective-permute-start.3 = (bf16[512,512]{1,0:T(8,128)(2,1)S(1)}, bf16[512,512]{1,0:T(8,128)(2,1)S(1)}, u32[]{:S(2)}, u32[]{:S(2)}) collective-permute-start(bf16[512,512]{1,0:T(8,128)(2,1)S(1)} %get-tuple-element.43), channel_id=1, source_target_pairs={{0,4},{1,0},{2,6},{3,2},{4,8},{5,1},{6,10},{7,3},{8,12},{9,5},{10,... | collective-permute-start | bytes 1572872 | tf_op jit(solution)/shard_map/ppermute | solution.py:56
  24.0 7.3 %copy-start.3 = (bf16[4,512,256]{2,1,0:T(8,128)(2,1)S(1)}, bf16[4,512,256]{2,1,0:T(8,128)(2,1)}, u32[]{:S(2)}) copy-start(bf16[4,512,256]{2,1,0:T(8,128)(2,1)} %weights.3) | copy-start | bytes 3145732
  31.2 1.7 %collective-permute-start.6 = (bf16[320,512]{1,0:T(8,128)(2,1)S(1)}, bf16[320,512]{1,0:T(8,128)(2,1)S(1)}, u32[]{:S(2)}, u32[]{:S(2)}) collective-permute-start(bf16[320,512]{1,0:T(8,128)(2,1)S(1)} %get-tuple-element.49), channel_id=1, source_target_pairs={{0,1},{1,0},{2,3},{3,2},{4,5},{5,4},{6,7},{7,6},{8,9},{9,8},{10,11... | collective-permute-start | bytes 983048 | tf_op jit(solution)/shard_map/ppermute | solution.py:23
  31.3 28.3 %collective-permute-start.5 = (bf16[4,512,256]{2,1,0:T(8,128)(2,1)S(1)}, bf16[4,512,256]{2,1,0:T(8,128)(2,1)S(1)}, u32[]{:S(2)}, u32[]{:S(2)}) collective-permute-start(bf16[4,512,256]{2,1,0:T(8,128)(2,1)S(1)} %copy-done.3), channel_id=1, source_target_pairs={{0,1},{1,0},{2,3},{3,2},{4,5},{5,4},{6,7},{7,6},{8,9},{9,8},{10,11... | collective-permute-start | bytes 3145736 | tf_op jit(solution)/shard_map/ppermute | solution.py:23
  34.2 4.0 %collective-permute-start.8 = (bf16[256,512]{1,0:T(8,128)(2,1)S(1)}, bf16[256,512]{1,0:T(8,128)(2,1)S(1)}, u32[]{:S(2)}, u32[]{:S(2)}) collective-permute-start(bf16[256,512]{1,0:T(8,128)(2,1)S(1)} %get-tuple-element.54.refs_1_.refs_7_), channel_id=1, source_target_pairs={{0,1},{1,0},{2,3},{3,2},{4,5},{5,4},{6,7},{7,6},{8,9},{9,8},{10,11... | collective-permute-start | bytes 786440 | tf_op jit(solution)/shard_map/ppermute | solution.py:23
  34.5 8.5 %collective-permute-start.10 = (bf16[64,512]{1,0:T(8,128)(2,1)S(1)}, bf16[64,512]{1,0:T(8,128)(2,1)S(1)}, u32[]{:S(2)}, u32[]{:S(2)}) collective-permute-start(bf16[64,512]{1,0:T(8,128)(2,1)S(1)} %get-tuple-element.59), channel_id=1, source_target_pairs={{0,1},{1,0},{2,4},{3,5},{4,2},{5,3},{6,8},{7,9},{8,6},{9,7},{10,12... | collective-permute-start | bytes 196616 | tf_op jit(solution)/shard_map/ppermute | solution.py:56
  38.3 4.8 %collective-permute-start.9 = (bf16[64,512]{1,0:T(8,128)(2,1)S(1)}, bf16[64,512]{1,0:T(8,128)(2,1)S(1)}, u32[]{:S(2)}, u32[]{:S(2)}) collective-permute-start(bf16[64,512]{1,0:T(8,128)(2,1)S(1)} %get-tuple-element.58), channel_id=1, source_target_pairs={{0,2},{1,3},{2,0},{3,1},{4,6},{5,7},{6,4},{7,5},{8,10},{9,11},{10,... | collective-permute-start | bytes 196616 | tf_op jit(solution)/shard_map/ppermute | solution.py:56
  46.0 5.4 %collective-permute-start.11 = (bf16[256,512]{1,0:T(8,128)(2,1)S(1)}, bf16[256,512]{1,0:T(8,128)(2,1)S(1)}, u32[]{:S(2)}, u32[]{:S(2)}) collective-permute-start(bf16[256,512]{1,0:T(8,128)(2,1)S(1)} %get-tuple-element.61.refs_1_), channel_id=1, source_target_pairs={{0,1},{1,0},{2,3},{3,2},{4,5},{5,4},{6,7},{7,6},{8,9},{9,8},{10,11... | collective-permute-start | bytes 786440 | tf_op jit(solution)/shard_map/ppermute | solution.py:23
  47.6 9.1 %collective-permute-start.12 = (bf16[64,512]{1,0:T(8,128)(2,1)S(1)}, bf16[64,512]{1,0:T(8,128)(2,1)S(1)}, u32[]{:S(2)}, u32[]{:S(2)}) collective-permute-start(bf16[64,512]{1,0:T(8,128)(2,1)S(1)} %get-tuple-element.67), channel_id=1, source_target_pairs={{0,1},{1,0},{2,4},{3,5},{4,2},{5,3},{6,8},{7,9},{8,6},{9,7},{10,12... | collective-permute-start | bytes 196616 | tf_op jit(solution)/shard_map/ppermute | solution.py:56
  51.4 5.3 %collective-permute-start.13 = (bf16[64,512]{1,0:T(8,128)(2,1)S(1)}, bf16[64,512]{1,0:T(8,128)(2,1)S(1)}, u32[]{:S(2)}, u32[]{:S(2)}) collective-permute-start(bf16[64,512]{1,0:T(8,128)(2,1)S(1)} %get-tuple-element.68), channel_id=1, source_target_pairs={{0,2},{1,3},{2,0},{3,1},{4,6},{5,7},{6,4},{7,5},{8,10},{9,11},{10,... | collective-permute-start | bytes 196616 | tf_op jit(solution)/shard_map/ppermute | solution.py:56
  58.7 2.1 %collective-permute-start.14 = (bf16[256,512]{1,0:T(8,128)(2,1)S(1)}, bf16[256,512]{1,0:T(8,128)(2,1)S(1)}, u32[]{:S(2)}, u32[]{:S(2)}) collective-permute-start(bf16[256,512]{1,0:T(8,128)(2,1)S(1)} %layer_sum_1.1.refs_5_), channel_id=1, source_target_pairs={{0,1},{1,0},{2,3},{3,2},{4,5},{5,4},{6,7},{7,6},{8,9},{9,8},{10,11... | collective-permute-start | bytes 786440 | tf_op jit(solution)/shard_map/ppermute | solution.py:23
  62.6 23.3 %collective-permute-start.16 = (bf16[512,512]{1,0:T(8,128)(2,1)S(1)}, bf16[512,512]{1,0:T(8,128)(2,1)S(1)}, u32[]{:S(2)}, u32[]{:S(2)}) collective-permute-start(bf16[512,512]{1,0:T(8,128)(2,1)S(1)} %get-tuple-element.72.refs_1_), channel_id=1, source_target_pairs={{0,2},{1,0},{2,4},{3,1},{4,6},{5,3},{6,8},{7,5},{8,10},{9,7},{10,1... | collective-permute-start | bytes 1572872 | tf_op jit(solution)/shard_map/ppermute | solution.py:56
  66.5 21.9 %collective-permute-start.15 = (bf16[512,512]{1,0:T(8,128)(2,1)S(1)}, bf16[512,512]{1,0:T(8,128)(2,1)S(1)}, u32[]{:S(2)}, u32[]{:S(2)}) collective-permute-start(bf16[512,512]{1,0:T(8,128)(2,1)S(1)} %get-tuple-element.72.refs_1_), channel_id=1, source_target_pairs={{0,4},{1,0},{2,6},{3,2},{4,8},{5,1},{6,10},{7,3},{8,12},{9,5},{10,... | collective-permute-start | bytes 1572872 | tf_op jit(solution)/shard_map/ppermute | solution.py:56
  90.3 2.0 %collective-permute-start.18 = (bf16[512,512]{1,0:T(8,128)(2,1)S(1)}, bf16[512,512]{1,0:T(8,128)(2,1)S(1)}, u32[]{:S(2)}, u32[]{:S(2)}) collective-permute-start(bf16[512,512]{1,0:T(8,128)(2,1)S(1)} %get-tuple-element.77.sum_own), channel_id=1, source_target_pairs={{0,1},{1,0},{2,3},{3,2},{4,5},{5,4},{6,7},{7,6},{8,9},{9,8},{10,11... | collective-permute-start | bytes 1572872 | tf_op jit(solution)/shard_map/ppermute | solution.py:23
  91.7 2.3 %collective-permute-start.17 = (bf16[512,512]{1,0:T(8,128)(2,1)S(1)}, bf16[512,512]{1,0:T(8,128)(2,1)S(1)}, u32[]{:S(2)}, u32[]{:S(2)}) collective-permute-start(bf16[512,512]{1,0:T(8,128)(2,1)S(1)} %decode_rest.1.sum_own), channel_id=1, source_target_pairs={{0,1},{1,0},{2,3},{3,2},{4,5},{5,4},{6,7},{7,6},{8,9},{9,8},{10,11... | collective-permute-start | bytes 1572872 | tf_op jit(solution)/shard_map/ppermute | solution.py:23
  (10 other events, 32.3 us)

commit v2 on v1

--- a/solution.py
+++ b/solution.py
@@ -162,7 +162,9 @@
 
 
 def encode_begin_kernel(meta, own, w_own, out):
-    out[...] = dot(own[pl.ds(0, HALF), :], w_own[window(meta[0]), :])
+    for start in range(0, own.shape[0], HALF):
+        rows = pl.ds(start, HALF)
+        out[rows, :] = dot(own[rows, :], w_own[window(meta[0]), :])
 
 
 def gather_slots(senders_row, sent, out):
@@ -176,8 +178,7 @@
     for start in range(0, own.shape[0], HALF):
         rows = pl.ds(start, HALF)
         a, b = own[rows, :], other[rows, :]
-        first = begun[...] if start == 0 else dot(a, w_own[mine, :])
-        sent[rows, mine] = (first + dot(b, w_own[rest, :])).astype(BF16)
+        sent[rows, mine] = (begun[rows, :] + dot(b, w_own[rest, :])).astype(BF16)
         sent[rows, rest] = (dot(a, w_other[mine, :]) + dot(b, w_other[rest, :])).astype(BF16)
     gather_slots(senders[near_offset(meta)], sent, piece)
 
@@ -415,20 +416,16 @@
     decode_scatter(live_targets(targets, live, REACH, columns), message, None, 0, out)
 
 
-def decode_near_kernel(meta, sent, before, senders, targets, live, total, out, message):
-    offset = near_offset(meta)
+def decode_sum_kernel(
+    offset_of, meta, sent, before, senders, targets, live, total, out, message
+):
+    offset = offset_of(meta)
     decode_messages(meta, offset, slice(None), sent, before, senders, message)
     decode_scatter(live_targets(targets, live, offset), message, total, 0, out)
 
 
-def decode_skip_kernel(meta, sent, before, senders, targets, live, total, out, message):
-    offset = skip_offset(meta)
-    decode_messages(meta, offset, slice(None), sent, before, senders, message)
-    decode_scatter(live_targets(targets, live, offset), message, total, 0, out)
-
-
-def decode_rest_kernel(meta, message, targets, live, total, out):
-    row = live_targets(targets, live, skip_offset(meta))
+def decode_rest_kernel(offset_of, meta, message, targets, live, total, out):
+    row = live_targets(targets, live, offset_of(meta))
     decode_scatter(row, message, total, out.shape[0], out)
 
 
@@ -471,8 +468,8 @@
         "encode_begin",
         (meta, grid_latent, encode_weights),
         [SMEM, whole(grid_latent), part(encode_weights, 0)],
-        [shape(HALF, cols, dtype=F32)],
-        2 * HALF * cols * cols,
+        [shape(grid_rows, cols, dtype=F32)],
+        2 * grid_rows * cols * cols,
     )
     grid_other, mesh_other = lax.optimization_barrier((grid_other, mesh_other))
     operands = (meta, grid_latent, grid_other, begun, encode_weights, encode_other, senders)
@@ -659,10 +656,10 @@
         flops // 2,
         [pltpu.VMEM(before_own.shape, BF16)],
     )
-    operands = (meta, near_rows, before_near, senders, targets, live, total)
+    operands = (meta, skip_rows, before_skip, senders, targets, live, total)
     (total,) = call(
-        decode_near_kernel,
-        "decode_near",
+        functools.partial(decode_sum_kernel, skip_offset),
+        "decode_skip",
         operands,
         [SMEM] + [whole(x) for x in operands[1:]],
         [shape(grid_rows, full)],
@@ -670,10 +667,10 @@
         message_space,
     )
     half = grid_rows // 2
-    operands = (meta, skip_rows, before_skip, senders, targets, live, total)
+    operands = (meta, near_rows, before_near, senders, targets, live, total)
     head, message = call(
-        decode_skip_kernel,
-        "decode_skip",
+        functools.partial(decode_sum_kernel, near_offset),
+        "decode_near",
         operands,
         [SMEM] + [whole(x) for x in operands[1:]],
         [shape(half, full), shape(slots, full)],
@@ -681,7 +678,7 @@
     )
     operands = (meta, message, targets, live, total)
     (tail,) = call(
-        decode_rest_kernel,
+        functools.partial(decode_rest_kernel, near_offset),
         "decode_rest",
         operands,
         [SMEM] + [whole(x) for x in operands[1:]],

time: 95.8 us -> 93.4 us (0.975)
  the two profiles are of different devices: /device:TPU:129 before, /device:TPU:103 now
where the time goes in v2:
time: 93.4 us; the launch traced here: 93.2 us
  Pallas kernels  38.5 us (41%)
  waiting for transfers between devices  34.4 us (37%)
  starting transfers between devices  17 us (18%)
  local copies, waits for them, and re-layouts  2.33 us (2%)
    pallas_call x18, Pallas kernels, call(): pl.pallas_call(viewed, name=name, grid=(1,), in_specs=[spec.spec if isins...  35.2 us
    ppermute x8, waiting for transfers between devices, exchange(): return lax.ppermute(value, ('band', 'feat'), pairs(lax.axis_size('band')))  30.7 us
    ppermute x11, starting transfers between devices, swap(): return lax.ppermute(value, 'feat', [(0, 1), (1, 0)])  12.4 us
    ppermute x8, starting transfers between devices, exchange(): return lax.ppermute(value, ('band', 'feat'), pairs(lax.axis_size('band')))  4.59 us
    ppermute x11, waiting for transfers between devices, swap(): return lax.ppermute(value, 'feat', [(0, 1), (1, 0)])  3.7 us
    pallas_call x2, Pallas kernels, body(): pl.pallas_call(functools.partial(final_kernel, index * half), name=f'fina...  3.3 us
    unnamed x30, local copies, waits for them, and re-layouts  2.33 us
  transfers between devices with their start and end apart: 19, of which 10 were waited for; matrix products, arithmetic and copies ran while one was open for 0% of the time, Pallas kernels for 34%

profile of v2, /device:TPU:103, one launch (start us, length us, event | category | flops | bytes accessed | tf_op | source)
XLA Modules:
  0.0 93.2 jit_solution(8121715247462542841)
XLA Ops:
  5.2 1.9 %encode_near.1 = (bf16[1024,512]{1,0:T(8,128)(2,1)S(1)}, bf16[512,512]{1,0:T(8,128)(2,1)S(1)}) custom-call(s32[2]{0:T(128)S(1)} %pad_add_fusion.refs_0_.meta, bf16[1024,256]{1,0:T(8,128)(2,1)S(1)} %copy-done.4, bf16[1024,256]{1,0:T(8,128)(2,1)S(1)} %collective-permute-done.refs_2_, f32[1024,256]{1,0:T(8,128)S(1)} %encode_begin.1.refs_3_, ...), custom_call_target="tpu_custom_call" | custom-call | flops 16777216 | bytes 24576 | tf_op jit(solution)/shard_map/encode_near/pallas_call | solution.py:134
  8.0 2.0 %encode_skip.1 = (bf16[512,512]{1,0:T(8,128)(2,1)S(1)}, bf16[512,512]{1,0:T(8,128)(2,1)S(1)}, bf16[512,512]{1,0:T(8,128)(2,1)S(1)}) custom-call(s32[2]{0:T(128)S(1)} %pad_add_fusion.refs_0_.meta, bf16[512,256]{1,0:T(8,128)(2,1)S(1)} %copy-done.6, bf16[512,256]{1,0:T(8,128)(2,1)S(1)} %collective-permute-done.1.refs_2_.refs_6_, ...), custom_call_target="tpu_custom_call" | custom-call | flops 16777216 | bytes 24576 | tf_op jit(solution)/shard_map/encode_skip/pallas_call | solution.py:134
  11.0 18.2 %collective-permute-done.4.refs_1_ = bf16[512,512]{1,0:T(8,128)(2,1)S(1)} collective-permute-done((bf16[512,512]{1,0:T(8,128)(2,1)S(1)}, bf16[512,512]{1,0:T(8,128)(2,1)S(1)}, u32[]{:S(2)}, u32[]{:S(2)}) %collective-permute-start.4) | collective-permute-done | bytes 524320 | tf_op jit(solution)/shard_map/ppermute | solution.py:56
  29.1 2.2 %encode_near_sum.1 = (f32[512,512]{1,0:T(8,128)S(1)}, bf16[512,512]{1,0:T(8,128)(2,1)S(1)}, bf16[320,512]{1,0:T(8,128)(2,1)S(1)}) custom-call(s32[2]{0:T(128)S(1)} %pad_add_fusion.refs_0_.meta, bf16[512,512]{1,0:T(8,128)(2,1)S(1)} %collective-permute-done.4.refs_1_, bf16[512,512]{1,0:T(8,128)(2,1)S(1)} %get-tuple-element.45.refs_2_, ...), custom_call_target="tpu_custom_call" | custom-call | flops 12582912 | bytes 29696 | tf_op jit(solution)/shard_map/encode_near_sum/pallas_call | solution.py:134
  32.5 1.9 %collective-permute-start.6 = (bf16[320,512]{1,0:T(8,128)(2,1)S(1)}, bf16[320,512]{1,0:T(8,128)(2,1)S(1)}, u32[]{:S(2)}, u32[]{:S(2)}) collective-permute-start(bf16[320,512]{1,0:T(8,128)(2,1)S(1)} %get-tuple-element.49), channel_id=1, source_target_pairs={{0,1},{1,0},{2,3},{3,2},{4,5},{5,4},{6,7},{7,6},{8,9},{9,8},{10,11... | collective-permute-start | bytes 983048 | tf_op jit(solution)/shard_map/ppermute | solution.py:23
  35.6 1.3 %encode_update.1 = (bf16[256,512]{1,0:T(8,128)(2,1)S(1)}, bf16[64,512]{1,0:T(8,128)(2,1)S(1)}, bf16[64,512]{1,0:T(8,128)(2,1)S(1)}) custom-call(s32[2]{0:T(128)S(1)} %pad_add_fusion.refs_0_.meta, bf16[512,256]{1,0:T(8,128)(2,1)S(1)} %copy-done.6, bf16[512,256]{1,0:T(8,128)(2,1)S(1)} %collective-permute-done.1.refs_2_.refs_6_, ...), custom_call_target="tpu_custom_call" | custom-call | flops 2097152 | bytes 6144 | tf_op jit(solution)/shard_map/encode_update/pallas_call | solution.py:134
  38.5 1.4 %layer_project_0.1 = (bf16[256,512]{1,0:T(8,128)(2,1)S(1)}, bf16[256,512]{1,0:T(8,128)(2,1)S(1)}, bf16[320,512]{1,0:T(8,128)(2,1)S(1)}, bf16[320,512]{1,0:T(8,128)(2,1)S(1)}) custom-call(s32[2]{0:T(128)S(1)} %pad_add_fusion.refs_0_.meta, bf16[256,512]{1,0:T(8,128)(2,1)S(1)} %get-tuple-element.54.refs_1_.refs_7_, ...), custom_call_target="tpu_custom_call" | custom-call | flops 8388608 | bytes 18432 | tf_op jit(solution)/shard_map/layer_project_0/pallas_call | solution.py:134
  40.0 2.1 %layer_gather_0.1.refs_1_ = bf16[8,320,512]{2,1,0:T(8,128)(2,1)S(1)} custom-call(s32[2]{0:T(128)S(1)} %pad_add_fusion.refs_0_.meta, bf16[256,512]{1,0:T(8,128)(2,1)S(1)} %get-tuple-element.55.refs_1_, bf16[256,512]{1,0:T(8,128)(2,1)S(1)} %get-tuple-element.56.refs_2_, s32[8,512]{1,0:T(8,128)S(1)} %bitcast.19), custom_call_target="tpu_custom_call" | custom-call | flops 16777216 | bytes 40960 | tf_op jit(solution)/shard_map/layer_gather_0/pallas_call | solution.py:134
  43.1 3.0 %layer_update_0.1 = (bf16[256,512]{1,0:T(8,128)(2,1)S(1)}, bf16[64,512]{1,0:T(8,128)(2,1)S(1)}, bf16[64,512]{1,0:T(8,128)(2,1)S(1)}) custom-call(s32[2]{0:T(128)S(1)} %pad_add_fusion.refs_0_.meta, bf16[8,320,512]{2,1,0:T(8,128)(2,1)S(1)} %layer_gather_0.1.refs_1_, bf16[320,512]{1,0:T(8,128)(2,1)S(1)} %get-tuple-element.57.refs_2_, ...), custom_call_target="tpu_custom_call" | custom-call | flops 6291456 | bytes 6144 | tf_op jit(solution)/shard_map/layer_update_0/pallas_call | solution.py:134
  47.1 1.7 %collective-permute-start.12 = (bf16[64,512]{1,0:T(8,128)(2,1)S(1)}, bf16[64,512]{1,0:T(8,128)(2,1)S(1)}, u32[]{:S(2)}, u32[]{:S(2)}) collective-permute-start(bf16[64,512]{1,0:T(8,128)(2,1)S(1)} %get-tuple-element.67), channel_id=1, source_target_pairs={{0,1},{1,0},{2,4},{3,5},{4,2},{5,3},{6,8},{7,9},{8,6},{9,7},{10,12... | collective-permute-start | bytes 196616 | tf_op jit(solution)/shard_map/ppermute | solution.py:56
  48.8 1.4 %layer_project_1.1 = (bf16[256,512]{1,0:T(8,128)(2,1)S(1)}, bf16[256,512]{1,0:T(8,128)(2,1)S(1)}, bf16[256,512]{1,0:T(8,128)(2,1)S(1)}, bf16[256,512]{1,0:T(8,128)(2,1)S(1)}, bf16[256,512]{1,0:T(8,128)(2,1)S(1)}) custom-call(s32[2]{0:T(128)S(1)} %pad_add_fusion.refs_0_.meta, bf16[256,512]{1,0:T(8,128)(2,1)S(1)} %get-tuple-element.61.refs_1_, ...), custom_call_target="tpu_custom_call" | custom-call | flops 8388608 | bytes 20480 | tf_op jit(solution)/shard_map/layer_project_1/pallas_call | solution.py:134
  50.1 1.9 %layer_gather_1.1.refs_1_ = bf16[8,256,512]{2,1,0:T(8,128)(2,1)S(1)} custom-call(s32[2]{0:T(128)S(1)} %pad_add_fusion.refs_0_.meta, bf16[256,512]{1,0:T(8,128)(2,1)S(1)} %get-tuple-element.64.refs_1_, bf16[256,512]{1,0:T(8,128)(2,1)S(1)} %get-tuple-element.65.refs_2_, s32[8,512]{1,0:T(8,128)S(1)} %bitcast.21), custom_call_target="tpu_custom_call" | custom-call | flops 16777216 | bytes 32768 | tf_op jit(solution)/shard_map/layer_gather_1/pallas_call | solution.py:134
  52.8 2.0 %layer_sum_1.1.refs_5_ = bf16[256,512]{1,0:T(8,128)(2,1)S(1)} custom-call(s32[2]{0:T(128)S(1)} %pad_add_fusion.refs_0_.meta, bf16[8,256,512]{2,1,0:T(8,128)(2,1)S(1)} %layer_gather_1.1.refs_1_, bf16[256,512]{1,0:T(8,128)(2,1)S(1)} %get-tuple-element.66.refs_2_, bf16[64,512]{1,0:T(8,128)(2,1)S(1)} %collective-permute-done.12.refs_3_, ...), custom_call_target="tpu_custom_call" | custom-call | flops 4194304 | bytes 4096 | tf_op jit(solution)/shard_map/layer_sum_1/pallas_call | solution.py:134
  56.9 1.8 %last_update.1 = (bf16[512,256]{1,0:T(8,128)(2,1)S(1)}, bf16[512,512]{1,0:T(8,128)(2,1)S(1)}) custom-call(s32[2]{0:T(128)S(1)} %pad_add_fusion.refs_0_.meta, bf16[256,512]{1,0:T(8,128)(2,1)S(1)} %get-tuple-element.61.refs_1_, bf16[256,512]{1,0:T(8,128)(2,1)S(1)} %collective-permute-done.11.refs_2_, bf16[256,512]{1,0:T(8,128)(2,1)S(1)} %get-tuple-element.62.refs_3_, ...), custom_call_target="tpu_custom_call" | custom-call | flops 8388608 | bytes 12288 | tf_op jit(solution)/shard_map/last_update/pallas_call | solution.py:134
  60.2 5.1 %decode_prepare.1 = (bf16[512,512]{1,0:T(8,128)(2,1)S(1)}, bf16[1024,512]{1,0:T(8,128)(2,1)S(1)}, bf16[1024,512]{1,0:T(8,128)(2,1)S(1)}, bf16[1024,256]{1,0:T(8,128)(2,1)S(1)}, bf16[512,256]{1,0:T(8,128)(2,1)}) custom-call(s32[2]{0:T(128)S(1)} %pad_add_fusion.refs_0_.meta, bf16[1024,256]{1,0:T(8,128)(2,1)S(1)} %copy-done.5, ...), custom_call_target="tpu_custom_call" | custom-call | flops 50331648 | bytes 53248 | tf_op jit(solution)/shard_map/decode_prepare/pallas_call | solution.py:134
  65.3 1.7 %decode_own.1.refs_6_ = bf16[1024,512]{1,0:T(8,128)(2,1)S(1)} custom-call(s32[2]{0:T(128)S(1)} %pad_add_fusion.refs_0_.meta, bf16[512,512]{1,0:T(8,128)(2,1)S(1)} %get-tuple-element.72.refs_1_, bf16[512,512]{1,0:T(8,128)(2,1)S(1)} %get-tuple-element.75.refs_2_, s32[5,1,1024]{2,1,0:T(1,128)S(1)} %bitcast.23, s32[5,1,1024]{2,1,0:T(1,128)S(1)} %bitcast.11, ...), custom_call_target="tpu_custom_call" | custom-call | flops 12582912 | bytes 16384 | tf_op jit(solution)/shard_map/decode_own/pallas_call | solution.py:134
  66.9 7.4 %collective-permute-done.16.refs_1_ = bf16[512,512]{1,0:T(8,128)(2,1)S(1)} collective-permute-done((bf16[512,512]{1,0:T(8,128)(2,1)S(1)}, bf16[512,512]{1,0:T(8,128)(2,1)S(1)}, u32[]{:S(2)}, u32[]{:S(2)}) %collective-permute-start.16) | collective-permute-done | bytes 524320 | tf_op jit(solution)/shard_map/ppermute | solution.py:56
  74.3 2.4 %decode_skip.1.refs_6_.refs_4_ = bf16[1024,512]{1,0:T(8,128)(2,1)S(1)} custom-call(s32[2]{0:T(128)S(1)} %pad_add_fusion.refs_0_.meta, bf16[512,512]{1,0:T(8,128)(2,1)S(1)} %collective-permute-done.16.refs_1_, bf16[1024,512]{1,0:T(8,128)(2,1)S(1)} %get-tuple-element.74.refs_2_, s32[5,1,1024]{2,1,0:T(1,128)S(1)} %bitcast.24, s32[5,1,1024]{2,1,0:T(1,128)S(1)} %bitcast.12, ...), custom_call_target="tpu_custom_call" | custom-call | flops 25165824 | bytes 16384 | tf_op jit(solution)/shard_map/decode_skip/pallas_call | solution.py:134
  76.8 3.4 %collective-permute-done.15.refs_1_ = bf16[512,512]{1,0:T(8,128)(2,1)S(1)} collective-permute-done((bf16[512,512]{1,0:T(8,128)(2,1)S(1)}, bf16[512,512]{1,0:T(8,128)(2,1)S(1)}, u32[]{:S(2)}, u32[]{:S(2)}) %collective-permute-start.15) | collective-permute-done | bytes 524320 | tf_op jit(solution)/shard_map/ppermute | solution.py:56
  80.1 1.9 %decode_near.1 = (bf16[512,512]{1,0:T(8,128)(2,1)S(1)}, bf16[1024,512]{1,0:T(8,128)(2,1)S(1)}) custom-call(s32[2]{0:T(128)S(1)} %pad_add_fusion.refs_0_.meta, bf16[512,512]{1,0:T(8,128)(2,1)S(1)} %collective-permute-done.15.refs_1_, bf16[1024,512]{1,0:T(8,128)(2,1)S(1)} %get-tuple-element.73.refs_2_, s32[5,1,1024]{2,1,0:T(1,128)S(1)} %bitcast.25, ...), custom_call_target="tpu_custom_call" | custom-call | flops 25165824 | bytes 24576 | tf_op jit(solution)/shard_map/decode_near/pallas_call | solution.py:134
  82.1 6.2 %collective-permute-start.18 = (bf16[512,512]{1,0:T(8,128)(2,1)S(1)}, bf16[512,512]{1,0:T(8,128)(2,1)S(1)}, u32[]{:S(2)}, u32[]{:S(2)}) collective-permute-start(bf16[512,512]{1,0:T(8,128)(2,1)S(1)} %get-tuple-element.77.sum_own), channel_id=1, source_target_pairs={{0,1},{1,0},{2,3},{3,2},{4,5},{5,4},{6,7},{7,6},{8,9},{9,8},{10,11... | collective-permute-start | bytes 1572872 | tf_op jit(solution)/shard_map/ppermute | solution.py:23
  88.3 1.2 %decode_rest.1.sum_own = bf16[512,512]{1,0:T(8,128)(2,1)S(1)} custom-call(s32[2]{0:T(128)S(1)} %pad_add_fusion.refs_0_.meta, bf16[1024,512]{1,0:T(8,128)(2,1)S(1)} %get-tuple-element.76.refs_1_, s32[5,1,1024]{2,1,0:T(1,128)S(1)} %bitcast.14, s32[5,1,1024]{2,1,0:T(1,128)S(1)} %bitcast.18, bf16[1024,512]{1,0:T(8,128)(2,1)S(1)} %decode_skip.1.refs_6_.refs_4_), custom_call_target="tpu_custom_call" | custom-call | flops 12582912 | bytes 8192 | tf_op jit(solution)/shard_map/decode_rest/pallas_call | solution.py:134
  89.8 1.7 %final_update_0.1.refs_0_ = bf16[1024,256]{1,0:T(8,128)(2,1)} custom-call(s32[2]{0:T(128)S(1)} %pad_add_fusion.refs_0_.meta, bf16[1024,256]{1,0:T(8,128)(2,1)S(1)} %copy-done.5, bf16[1024,256]{1,0:T(8,128)(2,1)S(1)} %get-tuple-element.71.self_term, bf16[512,512]{1,0:T(8,128)(2,1)S(1)} %get-tuple-element.77.sum_own, ...), custom_call_target="tpu_custom_call" | custom-call | tf_op jit(solution)/shard_map/final_update_0/pallas_call | solution.py:696
  91.5 1.7 %final_update_1.1 = bf16[1024,256]{1,0:T(8,128)(2,1)} custom-call(s32[2]{0:T(128)S(1)} %pad_add_fusion.refs_0_.meta, bf16[1024,256]{1,0:T(8,128)(2,1)S(1)} %copy-done.5, bf16[1024,256]{1,0:T(8,128)(2,1)S(1)} %get-tuple-element.71.self_term, bf16[512,512]{1,0:T(8,128)(2,1)S(1)} %decode_rest.1.sum_own, ...), custom_call_target="tpu_custom_call", output_to_operand_aliasing={{}: (6, {})} | custom-call | tf_op jit(solution)/shard_map/final_update_1/pallas_call | solution.py:696
  (65 shorter events, 17.0 us)
Async XLA Ops:
  0.6 4.5 %copy-start.11 = (s32[1,5,512]{2,0,1:T(1,128)S(1)}, s32[1,5,512]{2,0,1:T(1,128)}, u32[]{:S(2)}) copy-start(s32[1,5,512]{2,0,1:T(1,128)} %param.18) | copy-start | bytes 30724
  0.6 4.5 %collective-permute-start.2 = (bf16[4,512,256]{2,1,0:T(8,128)(2,1)}, bf16[4,512,256]{2,1,0:T(8,128)(2,1)S(1)}, u32[]{:S(2)}, u32[]{:S(2)}) collective-permute-start(bf16[4,512,256]{2,1,0:T(8,128)(2,1)} %refs_6_.1), channel_id=1, source_target_pairs={{0,1},{1,0},{2,3},{3,2},{4,5},{5,4},{6,7},{7,6},{8,9},{9,8},{10,11... | collective-permute-start | bytes 3145736 | tf_op jit(solution)/shard_map/ppermute | solution.py:23
  1.4 3.7 %collective-permute-start = (bf16[1024,256]{1,0:T(8,128)(2,1)}, bf16[1024,256]{1,0:T(8,128)(2,1)S(1)}, u32[]{:S(2)}, u32[]{:S(2)}) collective-permute-start(bf16[1024,256]{1,0:T(8,128)(2,1)} %own.3), channel_id=1, source_target_pairs={{0,1},{1,0},{2,3},{3,2},{4,5},{5,4},{6,7},{7,6},{8,9},{9,8},{10,11... | collective-permute-start | bytes 1572872 | tf_op jit(solution)/shard_map/ppermute | solution.py:23
  1.5 3.6 %collective-permute-start.1 = (bf16[512,256]{1,0:T(8,128)(2,1)}, bf16[512,256]{1,0:T(8,128)(2,1)S(1)}, u32[]{:S(2)}, u32[]{:S(2)}) collective-permute-start(bf16[512,256]{1,0:T(8,128)(2,1)} %refs_1_.8), channel_id=1, source_target_pairs={{0,1},{1,0},{2,3},{3,2},{4,5},{5,4},{6,7},{7,6},{8,9},{9,8},{10,11... | collective-permute-start | bytes 786440 | tf_op jit(solution)/shard_map/ppermute | solution.py:23
  7.1 22.0 %copy-start.14 = (s32[1,5,512]{2,0,1:T(1,128)S(1)}, s32[1,5,512]{2,0,1:T(1,128)}, u32[]{:S(2)}) copy-start(s32[1,5,512]{2,0,1:T(1,128)} %param.20) | copy-start | bytes 30724
  7.1 28.5 %collective-permute-start.7 = (bf16[2,4,512,256]{3,2,1,0:T(8,128)(2,1)S(1)}, bf16[2,4,512,256]{3,2,1,0:T(8,128)(2,1)S(1)}, u32[]{:S(2)}, u32[]{:S(2)}) collective-permute-start(bf16[2,4,512,256]{3,2,1,0:T(8,128)(2,1)S(1)} %copy-done), channel_id=1, source_target_pairs={{0,1},{1,0},{2,3},{3,2},{4,5},{5,4},{6,7},{7,6},{8,9},{9,8},{10,11... | collective-permute-start | bytes 6291464 | tf_op jit(solution)/shard_map/ppermute | solution.py:23
  7.5 21.7 %collective-permute-start.4 = (bf16[512,512]{1,0:T(8,128)(2,1)S(1)}, bf16[512,512]{1,0:T(8,128)(2,1)S(1)}, u32[]{:S(2)}, u32[]{:S(2)}) collective-permute-start(bf16[512,512]{1,0:T(8,128)(2,1)S(1)} %get-tuple-element.44), channel_id=1, source_target_pairs={{0,2},{1,0},{2,4},{3,1},{4,6},{5,3},{6,8},{7,5},{8,10},{9,7},{10,1... | collective-permute-start | bytes 1572872 | tf_op jit(solution)/shard_map/ppermute | solution.py:56
  10.1 21.3 %collective-permute-start.3 = (bf16[512,512]{1,0:T(8,128)(2,1)S(1)}, bf16[512,512]{1,0:T(8,128)(2,1)S(1)}, u32[]{:S(2)}, u32[]{:S(2)}) collective-permute-start(bf16[512,512]{1,0:T(8,128)(2,1)S(1)} %get-tuple-element.43), channel_id=1, source_target_pairs={{0,4},{1,0},{2,6},{3,2},{4,8},{5,1},{6,10},{7,3},{8,12},{9,5},{10,... | collective-permute-start | bytes 1572872 | tf_op jit(solution)/shard_map/ppermute | solution.py:56
  32.5 3.1 %collective-permute-start.6 = (bf16[320,512]{1,0:T(8,128)(2,1)S(1)}, bf16[320,512]{1,0:T(8,128)(2,1)S(1)}, u32[]{:S(2)}, u32[]{:S(2)}) collective-permute-start(bf16[320,512]{1,0:T(8,128)(2,1)S(1)} %get-tuple-element.49), channel_id=1, source_target_pairs={{0,1},{1,0},{2,3},{3,2},{4,5},{5,4},{6,7},{7,6},{8,9},{9,8},{10,11... | collective-permute-start | bytes 983048 | tf_op jit(solution)/shard_map/ppermute | solution.py:23
  34.3 21.4 %collective-permute-start.5 = (bf16[4,512,256]{2,1,0:T(8,128)(2,1)S(1)}, bf16[4,512,256]{2,1,0:T(8,128)(2,1)S(1)}, u32[]{:S(2)}, u32[]{:S(2)}) collective-permute-start(bf16[4,512,256]{2,1,0:T(8,128)(2,1)S(1)} %copy-done.3), channel_id=1, source_target_pairs={{0,1},{1,0},{2,3},{3,2},{4,5},{5,4},{6,7},{7,6},{8,9},{9,8},{10,11... | collective-permute-start | bytes 3145736 | tf_op jit(solution)/shard_map/ppermute | solution.py:23
  36.9 1.6 %collective-permute-start.8 = (bf16[256,512]{1,0:T(8,128)(2,1)S(1)}, bf16[256,512]{1,0:T(8,128)(2,1)S(1)}, u32[]{:S(2)}, u32[]{:S(2)}) collective-permute-start(bf16[256,512]{1,0:T(8,128)(2,1)S(1)} %get-tuple-element.54.refs_1_.refs_7_), channel_id=1, source_target_pairs={{0,1},{1,0},{2,3},{3,2},{4,5},{5,4},{6,7},{7,6},{8,9},{9,8},{10,11... | collective-permute-start | bytes 786440 | tf_op jit(solution)/shard_map/ppermute | solution.py:23
  37.4 5.7 %collective-permute-start.10 = (bf16[64,512]{1,0:T(8,128)(2,1)S(1)}, bf16[64,512]{1,0:T(8,128)(2,1)S(1)}, u32[]{:S(2)}, u32[]{:S(2)}) collective-permute-start(bf16[64,512]{1,0:T(8,128)(2,1)S(1)} %get-tuple-element.59), channel_id=1, source_target_pairs={{0,1},{1,0},{2,4},{3,5},{4,2},{5,3},{6,8},{7,9},{8,6},{9,7},{10,12... | collective-permute-start | bytes 196616 | tf_op jit(solution)/shard_map/ppermute | solution.py:56
  37.4 5.7 %collective-permute-start.9 = (bf16[64,512]{1,0:T(8,128)(2,1)S(1)}, bf16[64,512]{1,0:T(8,128)(2,1)S(1)}, u32[]{:S(2)}, u32[]{:S(2)}) collective-permute-start(bf16[64,512]{1,0:T(8,128)(2,1)S(1)} %get-tuple-element.58), channel_id=1, source_target_pairs={{0,2},{1,3},{2,0},{3,1},{4,6},{5,7},{6,4},{7,5},{8,10},{9,11},{10,... | collective-permute-start | bytes 196616 | tf_op jit(solution)/shard_map/ppermute | solution.py:56
  46.0 2.7 %collective-permute-start.11 = (bf16[256,512]{1,0:T(8,128)(2,1)S(1)}, bf16[256,512]{1,0:T(8,128)(2,1)S(1)}, u32[]{:S(2)}, u32[]{:S(2)}) collective-permute-start(bf16[256,512]{1,0:T(8,128)(2,1)S(1)} %get-tuple-element.61.refs_1_), channel_id=1, source_target_pairs={{0,1},{1,0},{2,3},{3,2},{4,5},{5,4},{6,7},{7,6},{8,9},{9,8},{10,11... | collective-permute-start | bytes 786440 | tf_op jit(solution)/shard_map/ppermute | solution.py:23
  47.1 5.8 %collective-permute-start.12 = (bf16[64,512]{1,0:T(8,128)(2,1)S(1)}, bf16[64,512]{1,0:T(8,128)(2,1)S(1)}, u32[]{:S(2)}, u32[]{:S(2)}) collective-permute-start(bf16[64,512]{1,0:T(8,128)(2,1)S(1)} %get-tuple-element.67), channel_id=1, source_target_pairs={{0,1},{1,0},{2,4},{3,5},{4,2},{5,3},{6,8},{7,9},{8,6},{9,7},{10,12... | collective-permute-start | bytes 196616 | tf_op jit(solution)/shard_map/ppermute | solution.py:56
  48.7 4.1 %collective-permute-start.13 = (bf16[64,512]{1,0:T(8,128)(2,1)S(1)}, bf16[64,512]{1,0:T(8,128)(2,1)S(1)}, u32[]{:S(2)}, u32[]{:S(2)}) collective-permute-start(bf16[64,512]{1,0:T(8,128)(2,1)S(1)} %get-tuple-element.68), channel_id=1, source_target_pairs={{0,2},{1,3},{2,0},{3,1},{4,6},{5,7},{6,4},{7,5},{8,10},{9,11},{10,... | collective-permute-start | bytes 196616 | tf_op jit(solution)/shard_map/ppermute | solution.py:56
  54.8 2.1 %collective-permute-start.14 = (bf16[256,512]{1,0:T(8,128)(2,1)S(1)}, bf16[256,512]{1,0:T(8,128)(2,1)S(1)}, u32[]{:S(2)}, u32[]{:S(2)}) collective-permute-start(bf16[256,512]{1,0:T(8,128)(2,1)S(1)} %layer_sum_1.1.refs_5_), channel_id=1, source_target_pairs={{0,1},{1,0},{2,3},{3,2},{4,5},{5,4},{6,7},{7,6},{8,9},{9,8},{10,11... | collective-permute-start | bytes 786440 | tf_op jit(solution)/shard_map/ppermute | solution.py:23
  56.9 3.2 %copy-start.7 = (s32[1,5,1024]{2,0,1:T(1,128)S(1)}, s32[1,5,1024]{2,0,1:T(1,128)}, u32[]{:S(2)}) copy-start(s32[1,5,1024]{2,0,1:T(1,128)} %param.24) | copy-start | bytes 61444
  58.7 15.6 %collective-permute-start.16 = (bf16[512,512]{1,0:T(8,128)(2,1)S(1)}, bf16[512,512]{1,0:T(8,128)(2,1)S(1)}, u32[]{:S(2)}, u32[]{:S(2)}) collective-permute-start(bf16[512,512]{1,0:T(8,128)(2,1)S(1)} %get-tuple-element.72.refs_1_), channel_id=1, source_target_pairs={{0,4},{1,0},{2,6},{3,2},{4,8},{5,1},{6,10},{7,3},{8,12},{9,5},{10,... | collective-permute-start | bytes 1572872 | tf_op jit(solution)/shard_map/ppermute | solution.py:56
  59.5 20.7 %collective-permute-start.15 = (bf16[512,512]{1,0:T(8,128)(2,1)S(1)}, bf16[512,512]{1,0:T(8,128)(2,1)S(1)}, u32[]{:S(2)}, u32[]{:S(2)}) collective-permute-start(bf16[512,512]{1,0:T(8,128)(2,1)S(1)} %get-tuple-element.72.refs_1_), channel_id=1, source_target_pairs={{0,2},{1,0},{2,4},{3,1},{4,6},{5,3},{6,8},{7,5},{8,10},{9,7},{10,1... | collective-permute-start | bytes 1572872 | tf_op jit(solution)/shard_map/ppermute | solution.py:56
  60.2 5.1 %copy-start.8 = (s32[1,5,1024]{2,0,1:T(1,128)S(1)}, s32[1,5,1024]{2,0,1:T(1,128)}, u32[]{:S(2)}) copy-start(s32[1,5,1024]{2,0,1:T(1,128)} %param.25) | copy-start | bytes 61444
  60.2 5.1 %copy-start.10 = (s32[1,5,1024]{2,0,1:T(1,128)S(1)}, s32[1,5,1024]{2,0,1:T(1,128)}, u32[]{:S(2)}) copy-start(s32[1,5,1024]{2,0,1:T(1,128)} %param.23) | copy-start | bytes 61444
  82.1 7.7 %collective-permute-start.18 = (bf16[512,512]{1,0:T(8,128)(2,1)S(1)}, bf16[512,512]{1,0:T(8,128)(2,1)S(1)}, u32[]{:S(2)}, u32[]{:S(2)}) collective-permute-start(bf16[512,512]{1,0:T(8,128)(2,1)S(1)} %get-tuple-element.77.sum_own), channel_id=1, source_target_pairs={{0,1},{1,0},{2,3},{3,2},{4,5},{5,4},{6,7},{7,6},{8,9},{9,8},{10,11... | collective-permute-start | bytes 1572872 | tf_op jit(solution)/shard_map/ppermute | solution.py:23
  89.5 2.0 %collective-permute-start.17 = (bf16[512,512]{1,0:T(8,128)(2,1)S(1)}, bf16[512,512]{1,0:T(8,128)(2,1)S(1)}, u32[]{:S(2)}, u32[]{:S(2)}) collective-permute-start(bf16[512,512]{1,0:T(8,128)(2,1)S(1)} %decode_rest.1.sum_own), channel_id=1, source_target_pairs={{0,1},{1,0},{2,3},{3,2},{4,5},{5,4},{6,7},{7,6},{8,9},{9,8},{10,11... | collective-permute-start | bytes 1572872 | tf_op jit(solution)/shard_map/ppermute | solution.py:23
  (10 other events, 24.7 us)

commit v3 on v2

--- a/solution.py
+++ b/solution.py
@@ -173,36 +173,36 @@
         out[pl.ds(start, HALF), :] = dot(hot_columns(col, sent.shape[0]), sent[...]).astype(BF16)
 
 
-def encode_near_kernel(meta, own, other, begun, w_own, w_other, senders, sent, piece):
+def encode_skip_kernel(meta, own, other, begun, w_own, w_other, senders, sent, piece):
     mine, rest = window(meta[0]), window(1 - meta[0])
     for start in range(0, own.shape[0], HALF):
         rows = pl.ds(start, HALF)
         a, b = own[rows, :], other[rows, :]
         sent[rows, mine] = (begun[rows, :] + dot(b, w_own[rest, :])).astype(BF16)
         sent[rows, rest] = (dot(a, w_other[mine, :]) + dot(b, w_other[rest, :])).astype(BF16)
-    gather_slots(senders[near_offset(meta)], sent, piece)
+    gather_slots(senders[skip_offset(meta)], sent, piece)
 
 
 def live_targets(targets, live, offset, columns=slice(None)):
     return jnp.where(live[offset, :, columns] > 0, targets[offset, :, columns], -1)
 
 
-def encode_skip_kernel(
+def encode_near_kernel(
     meta, own, other, w1, w1_other, sent, senders, targets, piece, recv, before
 ):
-    gather_slots(senders[skip_offset(meta)], sent, piece)
+    gather_slots(senders[near_offset(meta)], sent, piece)
     mine, rest = window(meta[0]), window(1 - meta[0])
     for start in range(0, own.shape[0], HALF):
         rows = pl.ds(start, HALF)
         a, b = own[rows, :], other[rows, :]
         recv[rows, mine] = (dot(a, w1[mine, :]) + dot(b, w1[rest, :])).astype(BF16)
         recv[rows, rest] = (dot(a, w1_other[mine, :]) + dot(b, w1_other[rest, :])).astype(BF16)
-    gather_slots(targets[near_offset(meta)], recv, before)
-
-
-def encode_near_sum_kernel(
+    gather_slots(targets[skip_offset(meta)], recv, before)
+
+
+def encode_skip_sum_kernel(
     meta, rows, before, recv, sent, own, other, w2, w2_other, senders, targets, live,
-    total, before_skip, self_term, message, own_message,
+    total, before_near, self_term, message, own_message,
 ):
     mine, rest = window(meta[0]), window(1 - meta[0])
     nodes = recv.shape[0]
@@ -210,13 +210,13 @@
     to_rows = hot_columns(column(targets[REACH, :, mine]), nodes)
     own_message[...] = silu_message(dot(from_rows, sent[...]) + dot(to_rows, recv[...]))
     message[...] = silu_message(rows[...] + before[...])
-    row = live_targets(targets, live, near_offset(meta))
+    row = live_targets(targets, live, skip_offset(meta))
     own_row = live_targets(targets, live, REACH, mine)
     for start in range(0, nodes, HALF):
         value = dot(hot_rows(row - start, HALF), message[...])
         value = value + dot(hot_rows(own_row - start, HALF), own_message[...])
         total[pl.ds(start, HALF), :] = value
-    gather_slots(targets[skip_offset(meta)], recv, before_skip)
+    gather_slots(targets[near_offset(meta)], recv, before_near)
     far = margin_rows(meta)
     for held, rows in ((pl.ds(0, HALF), mine), (pl.ds(HALF, MARGIN), far)):
         a, b = own[rows, :], other[rows, :]
@@ -224,11 +224,11 @@
         self_term[held, rest] = (dot(a, w2_other[mine, :]) + dot(b, w2_other[rest, :])).astype(BF16)
 
 
-def encode_skip_sum_kernel(
+def encode_near_sum_kernel(
     meta, rows, before, targets, live, total, out_own, out_other, message, halves
 ):
     message[...] = silu_message(rows[...] + before[...])
-    row = live_targets(targets, live, skip_offset(meta))
+    row = live_targets(targets, live, near_offset(meta))
     for index, half in enumerate((1 - meta[0], meta[0])):
         value = dot(hot_rows(row - half * HALF, HALF), message[...]) + total[window(half), :]
         halves[index] = value.astype(BF16)
@@ -473,23 +473,23 @@
     )
     grid_other, mesh_other = lax.optimization_barrier((grid_other, mesh_other))
     operands = (meta, grid_latent, grid_other, begun, encode_weights, encode_other, senders)
-    sent, near_piece = call(
-        encode_near_kernel,
-        "encode_near",
+    sent, skip_piece = call(
+        encode_skip_kernel,
+        "encode_skip",
         operands,
         [SMEM] + [whole(x) for x in operands[1:4]]
         + [part(encode_weights, 0), part(encode_other, 0), whole(senders)],
         [shape(grid_rows, full), shape(slots, full)],
         2 * full * (grid_rows * full + slots * grid_rows),
     )
-    near_rows = exchange(near_piece, near_shift)
-    layer_other = swap(after(layer_weights, near_piece))
+    skip_rows = exchange(skip_piece, skip_shift)
+    layer_other = swap(after(layer_weights, skip_piece))
     operands = (
         meta, mesh_latent, mesh_other, encode_weights, encode_other, sent, senders, targets
     )
-    skip_piece, recv, before_near = call(
-        encode_skip_kernel,
-        "encode_skip",
+    near_piece, recv, before_skip = call(
+        encode_near_kernel,
+        "encode_near",
         operands,
         [SMEM, whole(mesh_latent), whole(mesh_other)]
         + [part(encode_weights, 1), part(encode_other, 1)]
@@ -497,14 +497,14 @@
         [shape(slots, full), shape(mesh_rows, full), shape(slots, full)],
         2 * full * (mesh_rows * full + slots * (grid_rows + mesh_rows)),
     )
-    skip_rows = exchange(skip_piece, skip_shift)
+    near_rows = exchange(near_piece, near_shift)
     operands = (
-        meta, near_rows, before_near, recv, sent, mesh_latent, mesh_other,
+        meta, skip_rows, before_skip, recv, sent, mesh_latent, mesh_other,
         encode_weights, encode_other, senders, targets, live,
     )
-    total, before_skip, self_term = call(
-        encode_near_sum_kernel,
-        "encode_near_sum",
+    total, before_near, self_term = call(
+        encode_skip_sum_kernel,
+        "encode_skip_sum",
         operands,
         [SMEM] + [whole(x) for x in operands[1:7]]
         + [part(encode_weights, 2), part(encode_other, 2)]
@@ -517,12 +517,12 @@
         2 * full * mesh_rows * slots * 3,
         [pltpu.VMEM((slots, full), BF16), pltpu.VMEM((HALF, full), BF16)],
     )
-    operands = (meta, skip_rows, before_skip, targets, live, total)
+    operands = (meta, near_rows, before_near, targets, live, total)
     sum_own, sum_other = call(
-        encode_skip_sum_kernel,
-        "encode_skip_sum",
-        operands,
-        [SMEM, whole(skip_rows), whole(before_skip), whole(targets), whole(live), whole(total)],
+        encode_near_sum_kernel,
+        "encode_near_sum",
+        operands,
+        [SMEM, whole(near_rows), whole(before_near), whole(targets), whole(live), whole(total)],
         [shape(HELD, full), shape(HELD, full)],
         2 * full * mesh_rows * slots,
         [pltpu.VMEM((slots, full), BF16), pltpu.VMEM((2, HALF, full), BF16)],

time: 93.4 us -> 92.6 us (level)
  the two profiles are of different devices: /device:TPU:103 before, /device:TPU:129 now
where the time goes in v3:
time: 92.6 us; the launch traced here: 92.4 us
  Pallas kernels  38.5 us (42%)
  waiting for transfers between devices  28.8 us (31%)
  starting transfers between devices  21.8 us (24%)
  local copies, waits for them, and re-layouts  2.34 us (3%)
    pallas_call x18, Pallas kernels, call(): pl.pallas_call(viewed, name=name, grid=(1,), in_specs=[spec.spec if isins...  35.2 us
    ppermute x8, waiting for transfers between devices, exchange(): return lax.ppermute(value, ('band', 'feat'), pairs(lax.axis_size('band')))  26.2 us
    ppermute x8, starting transfers between devices, exchange(): return lax.ppermute(value, ('band', 'feat'), pairs(lax.axis_size('band')))  11.1 us
    ppermute x11, starting transfers between devices, swap(): return lax.ppermute(value, 'feat', [(0, 1), (1, 0)])  10.7 us
    pallas_call x2, Pallas kernels, body(): pl.pallas_call(functools.partial(final_kernel, index * half), name=f'fina...  3.31 us
    ppermute x11, waiting for transfers between devices, swap(): return lax.ppermute(value, 'feat', [(0, 1), (1, 0)])  2.56 us
    unnamed x30, local copies, waits for them, and re-layouts  2.34 us
  transfers between devices with their start and end apart: 19, of which 9 were waited for; matrix products, arithmetic and copies ran while one was open for 0% of the time, Pallas kernels for 34%

profile of v3, /device:TPU:129, one launch (start us, length us, event | category | flops | bytes accessed | tf_op | source)
XLA Modules:
  0.0 92.4 jit_solution(4839502137515401736)
XLA Ops:
  5.2 1.9 %encode_skip.1 = (bf16[1024,512]{1,0:T(8,128)(2,1)S(1)}, bf16[512,512]{1,0:T(8,128)(2,1)S(1)}) custom-call(s32[2]{0:T(128)S(1)} %pad_add_fusion.refs_0_.meta, bf16[1024,256]{1,0:T(8,128)(2,1)S(1)} %copy-done.4, bf16[1024,256]{1,0:T(8,128)(2,1)S(1)} %collective-permute-done.refs_2_, f32[1024,256]{1,0:T(8,128)S(1)} %encode_begin.1.refs_3_, ...), custom_call_target="tpu_custom_call" | custom-call | flops 16777216 | bytes 24576 | tf_op jit(solution)/shard_map/encode_skip/pallas_call | solution.py:134
  7.5 4.7 %collective-permute-start.4 = (bf16[512,512]{1,0:T(8,128)(2,1)S(1)}, bf16[512,512]{1,0:T(8,128)(2,1)S(1)}, u32[]{:S(2)}, u32[]{:S(2)}) collective-permute-start(bf16[512,512]{1,0:T(8,128)(2,1)S(1)} %get-tuple-element.44), channel_id=1, source_target_pairs={{0,4},{1,0},{2,6},{3,2},{4,8},{5,1},{6,10},{7,3},{8,12},{9,5},{10,... | collective-permute-start | bytes 1572872 | tf_op jit(solution)/shard_map/ppermute | solution.py:56
  12.2 2.0 %encode_near.1 = (bf16[512,512]{1,0:T(8,128)(2,1)S(1)}, bf16[512,512]{1,0:T(8,128)(2,1)S(1)}, bf16[512,512]{1,0:T(8,128)(2,1)S(1)}) custom-call(s32[2]{0:T(128)S(1)} %pad_add_fusion.refs_0_.meta, bf16[512,256]{1,0:T(8,128)(2,1)S(1)} %copy-done.6, bf16[512,256]{1,0:T(8,128)(2,1)S(1)} %collective-permute-done.1.refs_2_.refs_6_, ...), custom_call_target="tpu_custom_call" | custom-call | flops 16777216 | bytes 24576 | tf_op jit(solution)/shard_map/encode_near/pallas_call | solution.py:134
  15.2 6.0 %collective-permute-done.4.refs_1_ = bf16[512,512]{1,0:T(8,128)(2,1)S(1)} collective-permute-done((bf16[512,512]{1,0:T(8,128)(2,1)S(1)}, bf16[512,512]{1,0:T(8,128)(2,1)S(1)}, u32[]{:S(2)}, u32[]{:S(2)}) %collective-permute-start.4) | collective-permute-done | bytes 524320 | tf_op jit(solution)/shard_map/ppermute | solution.py:56
  21.2 2.2 %encode_skip_sum.1 = (f32[512,512]{1,0:T(8,128)S(1)}, bf16[512,512]{1,0:T(8,128)(2,1)S(1)}, bf16[320,512]{1,0:T(8,128)(2,1)S(1)}) custom-call(s32[2]{0:T(128)S(1)} %pad_add_fusion.refs_0_.meta, bf16[512,512]{1,0:T(8,128)(2,1)S(1)} %collective-permute-done.4.refs_1_, bf16[512,512]{1,0:T(8,128)(2,1)S(1)} %get-tuple-element.45.refs_2_, ...), custom_call_target="tpu_custom_call" | custom-call | flops 12582912 | bytes 29696 | tf_op jit(solution)/shard_map/encode_skip_sum/pallas_call | solution.py:134
  23.4 5.9 %collective-permute-done.3.refs_1_ = bf16[512,512]{1,0:T(8,128)(2,1)S(1)} collective-permute-done((bf16[512,512]{1,0:T(8,128)(2,1)S(1)}, bf16[512,512]{1,0:T(8,128)(2,1)S(1)}, u32[]{:S(2)}, u32[]{:S(2)}) %collective-permute-start.3) | collective-permute-done | bytes 524320 | tf_op jit(solution)/shard_map/ppermute | solution.py:56
  30.4 2.4 %collective-permute-start.6 = (bf16[320,512]{1,0:T(8,128)(2,1)S(1)}, bf16[320,512]{1,0:T(8,128)(2,1)S(1)}, u32[]{:S(2)}, u32[]{:S(2)}) collective-permute-start(bf16[320,512]{1,0:T(8,128)(2,1)S(1)} %get-tuple-element.49), channel_id=1, source_target_pairs={{0,1},{1,0},{2,3},{3,2},{4,5},{5,4},{6,7},{7,6},{8,9},{9,8},{10,11... | collective-permute-start | bytes 983048 | tf_op jit(solution)/shard_map/ppermute | solution.py:23
  38.9 2.1 %layer_gather_0.1.refs_1_ = bf16[8,320,512]{2,1,0:T(8,128)(2,1)S(1)} custom-call(s32[2]{0:T(128)S(1)} %pad_add_fusion.refs_0_.meta, bf16[256,512]{1,0:T(8,128)(2,1)S(1)} %get-tuple-element.55.refs_1_, bf16[256,512]{1,0:T(8,128)(2,1)S(1)} %get-tuple-element.56.refs_2_, s32[8,512]{1,0:T(8,128)S(1)} %bitcast.19), custom_call_target="tpu_custom_call" | custom-call | flops 16777216 | bytes 40960 | tf_op jit(solution)/shard_map/layer_gather_0/pallas_call | solution.py:134
  41.0 3.8 %collective-permute-done.10.refs_4_ = bf16[64,512]{1,0:T(8,128)(2,1)S(1)} collective-permute-done((bf16[64,512]{1,0:T(8,128)(2,1)S(1)}, bf16[64,512]{1,0:T(8,128)(2,1)S(1)}, u32[]{:S(2)}, u32[]{:S(2)}) %collective-permute-start.10) | collective-permute-done | bytes 65568 | tf_op jit(solution)/shard_map/ppermute | solution.py:56
  44.8 3.0 %layer_update_0.1 = (bf16[256,512]{1,0:T(8,128)(2,1)S(1)}, bf16[64,512]{1,0:T(8,128)(2,1)S(1)}, bf16[64,512]{1,0:T(8,128)(2,1)S(1)}) custom-call(s32[2]{0:T(128)S(1)} %pad_add_fusion.refs_0_.meta, bf16[8,320,512]{2,1,0:T(8,128)(2,1)S(1)} %layer_gather_0.1.refs_1_, bf16[320,512]{1,0:T(8,128)(2,1)S(1)} %get-tuple-element.57.refs_2_, ...), custom_call_target="tpu_custom_call" | custom-call | flops 6291456 | bytes 6144 | tf_op jit(solution)/shard_map/layer_update_0/pallas_call | solution.py:134
  48.9 1.7 %collective-permute-start.12 = (bf16[64,512]{1,0:T(8,128)(2,1)S(1)}, bf16[64,512]{1,0:T(8,128)(2,1)S(1)}, u32[]{:S(2)}, u32[]{:S(2)}) collective-permute-start(bf16[64,512]{1,0:T(8,128)(2,1)S(1)} %get-tuple-element.67), channel_id=1, source_target_pairs={{0,1},{1,0},{2,4},{3,5},{4,2},{5,3},{6,8},{7,9},{8,6},{9,7},{10,12... | collective-permute-start | bytes 196616 | tf_op jit(solution)/shard_map/ppermute | solution.py:56
  52.0 1.9 %layer_gather_1.1.refs_1_ = bf16[8,256,512]{2,1,0:T(8,128)(2,1)S(1)} custom-call(s32[2]{0:T(128)S(1)} %pad_add_fusion.refs_0_.meta, bf16[256,512]{1,0:T(8,128)(2,1)S(1)} %get-tuple-element.64.refs_1_, bf16[256,512]{1,0:T(8,128)(2,1)S(1)} %get-tuple-element.65.refs_2_, s32[8,512]{1,0:T(8,128)S(1)} %bitcast.21), custom_call_target="tpu_custom_call" | custom-call | flops 16777216 | bytes 32768 | tf_op jit(solution)/shard_map/layer_gather_1/pallas_call | solution.py:134
  53.8 4.1 %collective-permute-done.12.refs_3_ = bf16[64,512]{1,0:T(8,128)(2,1)S(1)} collective-permute-done((bf16[64,512]{1,0:T(8,128)(2,1)S(1)}, bf16[64,512]{1,0:T(8,128)(2,1)S(1)}, u32[]{:S(2)}, u32[]{:S(2)}) %collective-permute-start.12) | collective-permute-done | bytes 65568 | tf_op jit(solution)/shard_map/ppermute | solution.py:56
  58.0 2.0 %layer_sum_1.1.refs_5_ = bf16[256,512]{1,0:T(8,128)(2,1)S(1)} custom-call(s32[2]{0:T(128)S(1)} %pad_add_fusion.refs_0_.meta, bf16[8,256,512]{2,1,0:T(8,128)(2,1)S(1)} %layer_gather_1.1.refs_1_, bf16[256,512]{1,0:T(8,128)(2,1)S(1)} %get-tuple-element.66.refs_2_, bf16[64,512]{1,0:T(8,128)(2,1)S(1)} %collective-permute-done.12.refs_3_, ...), custom_call_target="tpu_custom_call" | custom-call | flops 4194304 | bytes 4096 | tf_op jit(solution)/shard_map/layer_sum_1/pallas_call | solution.py:134
  62.1 1.8 %last_update.1 = (bf16[512,256]{1,0:T(8,128)(2,1)S(1)}, bf16[512,512]{1,0:T(8,128)(2,1)S(1)}) custom-call(s32[2]{0:T(128)S(1)} %pad_add_fusion.refs_0_.meta, bf16[256,512]{1,0:T(8,128)(2,1)S(1)} %get-tuple-element.61.refs_1_, bf16[256,512]{1,0:T(8,128)(2,1)S(1)} %collective-permute-done.11.refs_2_, bf16[256,512]{1,0:T(8,128)(2,1)S(1)} %get-tuple-element.62.refs_3_, ...), custom_call_target="tpu_custom_call" | custom-call | flops 8388608 | bytes 12288 | tf_op jit(solution)/shard_map/last_update/pallas_call | solution.py:134
  63.8 2.1 %collective-permute-start.16 = (bf16[512,512]{1,0:T(8,128)(2,1)S(1)}, bf16[512,512]{1,0:T(8,128)(2,1)S(1)}, u32[]{:S(2)}, u32[]{:S(2)}) collective-permute-start(bf16[512,512]{1,0:T(8,128)(2,1)S(1)} %get-tuple-element.72.refs_1_), channel_id=1, source_target_pairs={{0,4},{1,0},{2,6},{3,2},{4,8},{5,1},{6,10},{7,3},{8,12},{9,5},{10,... | collective-permute-start | bytes 1572872 | tf_op jit(solution)/shard_map/ppermute | solution.py:56
  66.0 5.1 %decode_prepare.1 = (bf16[512,512]{1,0:T(8,128)(2,1)S(1)}, bf16[1024,512]{1,0:T(8,128)(2,1)S(1)}, bf16[1024,512]{1,0:T(8,128)(2,1)S(1)}, bf16[1024,256]{1,0:T(8,128)(2,1)S(1)}, bf16[512,256]{1,0:T(8,128)(2,1)}) custom-call(s32[2]{0:T(128)S(1)} %pad_add_fusion.refs_0_.meta, bf16[1024,256]{1,0:T(8,128)(2,1)S(1)} %copy-done.5, ...), custom_call_target="tpu_custom_call" | custom-call | flops 50331648 | bytes 53248 | tf_op jit(solution)/shard_map/decode_prepare/pallas_call | solution.py:134
  71.1 1.7 %decode_own.1.refs_6_ = bf16[1024,512]{1,0:T(8,128)(2,1)S(1)} custom-call(s32[2]{0:T(128)S(1)} %pad_add_fusion.refs_0_.meta, bf16[512,512]{1,0:T(8,128)(2,1)S(1)} %get-tuple-element.72.refs_1_, bf16[512,512]{1,0:T(8,128)(2,1)S(1)} %get-tuple-element.75.refs_2_, s32[5,1,1024]{2,1,0:T(1,128)S(1)} %bitcast.23, s32[5,1,1024]{2,1,0:T(1,128)S(1)} %bitcast.11, ...), custom_call_target="tpu_custom_call" | custom-call | flops 12582912 | bytes 16384 | tf_op jit(solution)/shard_map/decode_own/pallas_call | solution.py:134
  72.7 6.3 %collective-permute-done.16.refs_1_ = bf16[512,512]{1,0:T(8,128)(2,1)S(1)} collective-permute-done((bf16[512,512]{1,0:T(8,128)(2,1)S(1)}, bf16[512,512]{1,0:T(8,128)(2,1)S(1)}, u32[]{:S(2)}, u32[]{:S(2)}) %collective-permute-start.16) | collective-permute-done | bytes 524320 | tf_op jit(solution)/shard_map/ppermute | solution.py:56
  79.1 2.4 %decode_skip.1.refs_6_.refs_4_ = bf16[1024,512]{1,0:T(8,128)(2,1)S(1)} custom-call(s32[2]{0:T(128)S(1)} %pad_add_fusion.refs_0_.meta, bf16[512,512]{1,0:T(8,128)(2,1)S(1)} %collective-permute-done.16.refs_1_, bf16[1024,512]{1,0:T(8,128)(2,1)S(1)} %get-tuple-element.74.refs_2_, s32[5,1,1024]{2,1,0:T(1,128)S(1)} %bitcast.24, s32[5,1,1024]{2,1,0:T(1,128)S(1)} %bitcast.12, ...), custom_call_target="tpu_custom_call" | custom-call | flops 25165824 | bytes 16384 | tf_op jit(solution)/shard_map/decode_skip/pallas_call | solution.py:134
  81.5 1.9 %decode_near.1 = (bf16[512,512]{1,0:T(8,128)(2,1)S(1)}, bf16[1024,512]{1,0:T(8,128)(2,1)S(1)}) custom-call(s32[2]{0:T(128)S(1)} %pad_add_fusion.refs_0_.meta, bf16[512,512]{1,0:T(8,128)(2,1)S(1)} %collective-permute-done.15.refs_1_, bf16[1024,512]{1,0:T(8,128)(2,1)S(1)} %get-tuple-element.73.refs_2_, s32[5,1,1024]{2,1,0:T(1,128)S(1)} %bitcast.25, ...), custom_call_target="tpu_custom_call" | custom-call | flops 25165824 | bytes 24576 | tf_op jit(solution)/shard_map/decode_near/pallas_call | solution.py:134
  83.5 4.0 %collective-permute-start.18 = (bf16[512,512]{1,0:T(8,128)(2,1)S(1)}, bf16[512,512]{1,0:T(8,128)(2,1)S(1)}, u32[]{:S(2)}, u32[]{:S(2)}) collective-permute-start(bf16[512,512]{1,0:T(8,128)(2,1)S(1)} %get-tuple-element.77.sum_own), channel_id=1, source_target_pairs={{0,1},{1,0},{2,3},{3,2},{4,5},{5,4},{6,7},{7,6},{8,9},{9,8},{10,11... | collective-permute-start | bytes 1572872 | tf_op jit(solution)/shard_map/ppermute | solution.py:23
  89.0 1.7 %final_update_0.1.refs_0_ = bf16[1024,256]{1,0:T(8,128)(2,1)} custom-call(s32[2]{0:T(128)S(1)} %pad_add_fusion.refs_0_.meta, bf16[1024,256]{1,0:T(8,128)(2,1)S(1)} %copy-done.5, bf16[1024,256]{1,0:T(8,128)(2,1)S(1)} %get-tuple-element.71.self_term, bf16[512,512]{1,0:T(8,128)(2,1)S(1)} %get-tuple-element.77.sum_own, ...), custom_call_target="tpu_custom_call" | custom-call | tf_op jit(solution)/shard_map/final_update_0/pallas_call | solution.py:696
  90.7 1.7 %final_update_1.1 = bf16[1024,256]{1,0:T(8,128)(2,1)} custom-call(s32[2]{0:T(128)S(1)} %pad_add_fusion.refs_0_.meta, bf16[1024,256]{1,0:T(8,128)(2,1)S(1)} %copy-done.5, bf16[1024,256]{1,0:T(8,128)(2,1)S(1)} %get-tuple-element.71.self_term, bf16[512,512]{1,0:T(8,128)(2,1)S(1)} %decode_rest.1.sum_own, ...), custom_call_target="tpu_custom_call", output_to_operand_aliasing={{}: (6, {})} | custom-call | tf_op jit(solution)/shard_map/final_update_1/pallas_call | solution.py:696
  (65 shorter events, 19.0 us)
Async XLA Ops:
  0.6 4.5 %collective-permute-start.2 = (bf16[4,512,256]{2,1,0:T(8,128)(2,1)}, bf16[4,512,256]{2,1,0:T(8,128)(2,1)S(1)}, u32[]{:S(2)}, u32[]{:S(2)}) collective-permute-start(bf16[4,512,256]{2,1,0:T(8,128)(2,1)} %refs_6_.1), channel_id=1, source_target_pairs={{0,1},{1,0},{2,3},{3,2},{4,5},{5,4},{6,7},{7,6},{8,9},{9,8},{10,11... | collective-permute-start | bytes 3145736 | tf_op jit(solution)/shard_map/ppermute | solution.py:23
  1.4 3.7 %collective-permute-start = (bf16[1024,256]{1,0:T(8,128)(2,1)}, bf16[1024,256]{1,0:T(8,128)(2,1)S(1)}, u32[]{:S(2)}, u32[]{:S(2)}) collective-permute-start(bf16[1024,256]{1,0:T(8,128)(2,1)} %own.3), channel_id=1, source_target_pairs={{0,1},{1,0},{2,3},{3,2},{4,5},{5,4},{6,7},{7,6},{8,9},{9,8},{10,11... | collective-permute-start | bytes 1572872 | tf_op jit(solution)/shard_map/ppermute | solution.py:23
  1.5 3.6 %collective-permute-start.1 = (bf16[512,256]{1,0:T(8,128)(2,1)}, bf16[512,256]{1,0:T(8,128)(2,1)S(1)}, u32[]{:S(2)}, u32[]{:S(2)}) collective-permute-start(bf16[512,256]{1,0:T(8,128)(2,1)} %refs_1_.8), channel_id=1, source_target_pairs={{0,1},{1,0},{2,3},{3,2},{4,5},{5,4},{6,7},{7,6},{8,9},{9,8},{10,11... | collective-permute-start | bytes 786440 | tf_op jit(solution)/shard_map/ppermute | solution.py:23
  5.2 7.1 %copy-start.2 = (bf16[4,512,256]{2,1,0:T(8,128)(2,1)S(1)}, bf16[4,512,256]{2,1,0:T(8,128)(2,1)}, u32[]{:S(2)}) copy-start(bf16[4,512,256]{2,1,0:T(8,128)(2,1)} %refs_6_.1) | copy-start | bytes 3145732
  5.2 7.0 %copy-start.6 = (bf16[512,256]{1,0:T(8,128)(2,1)S(1)}, bf16[512,256]{1,0:T(8,128)(2,1)}, u32[]{:S(2)}) copy-start(bf16[512,256]{1,0:T(8,128)(2,1)} %refs_1_.8) | copy-start | bytes 786436
  5.2 7.0 %copy-start.12 = (s32[1,5,512]{2,0,1:T(1,128)S(1)}, s32[1,5,512]{2,0,1:T(1,128)}, u32[]{:S(2)}) copy-start(s32[1,5,512]{2,0,1:T(1,128)} %param.19) | copy-start | bytes 30724
  7.1 14.1 %copy-start.14 = (s32[1,5,512]{2,0,1:T(1,128)S(1)}, s32[1,5,512]{2,0,1:T(1,128)}, u32[]{:S(2)}) copy-start(s32[1,5,512]{2,0,1:T(1,128)} %param.20) | copy-start | bytes 30724
  7.1 26.9 %collective-permute-start.7 = (bf16[2,4,512,256]{3,2,1,0:T(8,128)(2,1)S(1)}, bf16[2,4,512,256]{3,2,1,0:T(8,128)(2,1)S(1)}, u32[]{:S(2)}, u32[]{:S(2)}) collective-permute-start(bf16[2,4,512,256]{3,2,1,0:T(8,128)(2,1)S(1)} %copy-done), channel_id=1, source_target_pairs={{0,1},{1,0},{2,3},{3,2},{4,5},{5,4},{6,7},{7,6},{8,9},{9,8},{10,11... | collective-permute-start | bytes 6291464 | tf_op jit(solution)/shard_map/ppermute | solution.py:23
  7.5 13.7 %collective-permute-start.4 = (bf16[512,512]{1,0:T(8,128)(2,1)S(1)}, bf16[512,512]{1,0:T(8,128)(2,1)S(1)}, u32[]{:S(2)}, u32[]{:S(2)}) collective-permute-start(bf16[512,512]{1,0:T(8,128)(2,1)S(1)} %get-tuple-element.44), channel_id=1, source_target_pairs={{0,4},{1,0},{2,6},{3,2},{4,8},{5,1},{6,10},{7,3},{8,12},{9,5},{10,... | collective-permute-start | bytes 1572872 | tf_op jit(solution)/shard_map/ppermute | solution.py:56
  14.2 15.1 %collective-permute-start.3 = (bf16[512,512]{1,0:T(8,128)(2,1)S(1)}, bf16[512,512]{1,0:T(8,128)(2,1)S(1)}, u32[]{:S(2)}, u32[]{:S(2)}) collective-permute-start(bf16[512,512]{1,0:T(8,128)(2,1)S(1)} %get-tuple-element.43), channel_id=1, source_target_pairs={{0,2},{1,0},{2,4},{3,1},{4,6},{5,3},{6,8},{7,5},{8,10},{9,7},{10,1... | collective-permute-start | bytes 1572872 | tf_op jit(solution)/shard_map/ppermute | solution.py:56
  23.4 9.4 %copy-start.3 = (bf16[4,512,256]{2,1,0:T(8,128)(2,1)S(1)}, bf16[4,512,256]{2,1,0:T(8,128)(2,1)}, u32[]{:S(2)}) copy-start(bf16[4,512,256]{2,1,0:T(8,128)(2,1)} %weights.3) | copy-start | bytes 3145732
  30.4 3.7 %collective-permute-start.6 = (bf16[320,512]{1,0:T(8,128)(2,1)S(1)}, bf16[320,512]{1,0:T(8,128)(2,1)S(1)}, u32[]{:S(2)}, u32[]{:S(2)}) collective-permute-start(bf16[320,512]{1,0:T(8,128)(2,1)S(1)} %get-tuple-element.49), channel_id=1, source_target_pairs={{0,1},{1,0},{2,3},{3,2},{4,5},{5,4},{6,7},{7,6},{8,9},{9,8},{10,11... | collective-permute-start | bytes 983048 | tf_op jit(solution)/shard_map/ppermute | solution.py:23
  32.8 28.1 %collective-permute-start.5 = (bf16[4,512,256]{2,1,0:T(8,128)(2,1)S(1)}, bf16[4,512,256]{2,1,0:T(8,128)(2,1)S(1)}, u32[]{:S(2)}, u32[]{:S(2)}) collective-permute-start(bf16[4,512,256]{2,1,0:T(8,128)(2,1)S(1)} %copy-done.3), channel_id=1, source_target_pairs={{0,1},{1,0},{2,3},{3,2},{4,5},{5,4},{6,7},{7,6},{8,9},{9,8},{10,11... | collective-permute-start | bytes 3145736 | tf_op jit(solution)/shard_map/ppermute | solution.py:23
  35.4 2.0 %collective-permute-start.8 = (bf16[256,512]{1,0:T(8,128)(2,1)S(1)}, bf16[256,512]{1,0:T(8,128)(2,1)S(1)}, u32[]{:S(2)}, u32[]{:S(2)}) collective-permute-start(bf16[256,512]{1,0:T(8,128)(2,1)S(1)} %get-tuple-element.54.refs_1_.refs_7_), channel_id=1, source_target_pairs={{0,1},{1,0},{2,3},{3,2},{4,5},{5,4},{6,7},{7,6},{8,9},{9,8},{10,11... | collective-permute-start | bytes 786440 | tf_op jit(solution)/shard_map/ppermute | solution.py:23
  35.8 9.0 %collective-permute-start.10 = (bf16[64,512]{1,0:T(8,128)(2,1)S(1)}, bf16[64,512]{1,0:T(8,128)(2,1)S(1)}, u32[]{:S(2)}, u32[]{:S(2)}) collective-permute-start(bf16[64,512]{1,0:T(8,128)(2,1)S(1)} %get-tuple-element.59), channel_id=1, source_target_pairs={{0,1},{1,0},{2,4},{3,5},{4,2},{5,3},{6,8},{7,9},{8,6},{9,7},{10,12... | collective-permute-start | bytes 196616 | tf_op jit(solution)/shard_map/ppermute | solution.py:56
  37.4 7.4 %collective-permute-start.9 = (bf16[64,512]{1,0:T(8,128)(2,1)S(1)}, bf16[64,512]{1,0:T(8,128)(2,1)S(1)}, u32[]{:S(2)}, u32[]{:S(2)}) collective-permute-start(bf16[64,512]{1,0:T(8,128)(2,1)S(1)} %get-tuple-element.58), channel_id=1, source_target_pairs={{0,2},{1,3},{2,0},{3,1},{4,6},{5,7},{6,4},{7,5},{8,10},{9,11},{10,... | collective-permute-start | bytes 196616 | tf_op jit(solution)/shard_map/ppermute | solution.py:56
  47.8 2.7 %collective-permute-start.11 = (bf16[256,512]{1,0:T(8,128)(2,1)S(1)}, bf16[256,512]{1,0:T(8,128)(2,1)S(1)}, u32[]{:S(2)}, u32[]{:S(2)}) collective-permute-start(bf16[256,512]{1,0:T(8,128)(2,1)S(1)} %get-tuple-element.61.refs_1_), channel_id=1, source_target_pairs={{0,1},{1,0},{2,3},{3,2},{4,5},{5,4},{6,7},{7,6},{8,9},{9,8},{10,11... | collective-permute-start | bytes 786440 | tf_op jit(solution)/shard_map/ppermute | solution.py:23
  48.9 9.1 %collective-permute-start.12 = (bf16[64,512]{1,0:T(8,128)(2,1)S(1)}, bf16[64,512]{1,0:T(8,128)(2,1)S(1)}, u32[]{:S(2)}, u32[]{:S(2)}) collective-permute-start(bf16[64,512]{1,0:T(8,128)(2,1)S(1)} %get-tuple-element.67), channel_id=1, source_target_pairs={{0,1},{1,0},{2,4},{3,5},{4,2},{5,3},{6,8},{7,9},{8,6},{9,7},{10,12... | collective-permute-start | bytes 196616 | tf_op jit(solution)/shard_map/ppermute | solution.py:56
  50.6 7.4 %collective-permute-start.13 = (bf16[64,512]{1,0:T(8,128)(2,1)S(1)}, bf16[64,512]{1,0:T(8,128)(2,1)S(1)}, u32[]{:S(2)}, u32[]{:S(2)}) collective-permute-start(bf16[64,512]{1,0:T(8,128)(2,1)S(1)} %get-tuple-element.68), channel_id=1, source_target_pairs={{0,2},{1,3},{2,0},{3,1},{4,6},{5,7},{6,4},{7,5},{8,10},{9,11},{10,... | collective-permute-start | bytes 196616 | tf_op jit(solution)/shard_map/ppermute | solution.py:56
  59.9 2.1 %collective-permute-start.14 = (bf16[256,512]{1,0:T(8,128)(2,1)S(1)}, bf16[256,512]{1,0:T(8,128)(2,1)S(1)}, u32[]{:S(2)}, u32[]{:S(2)}) collective-permute-start(bf16[256,512]{1,0:T(8,128)(2,1)S(1)} %layer_sum_1.1.refs_5_), channel_id=1, source_target_pairs={{0,1},{1,0},{2,3},{3,2},{4,5},{5,4},{6,7},{7,6},{8,9},{9,8},{10,11... | collective-permute-start | bytes 786440 | tf_op jit(solution)/shard_map/ppermute | solution.py:23
  63.8 15.2 %collective-permute-start.16 = (bf16[512,512]{1,0:T(8,128)(2,1)S(1)}, bf16[512,512]{1,0:T(8,128)(2,1)S(1)}, u32[]{:S(2)}, u32[]{:S(2)}) collective-permute-start(bf16[512,512]{1,0:T(8,128)(2,1)S(1)} %get-tuple-element.72.refs_1_), channel_id=1, source_target_pairs={{0,4},{1,0},{2,6},{3,2},{4,8},{5,1},{6,10},{7,3},{8,12},{9,5},{10,... | collective-permute-start | bytes 1572872 | tf_op jit(solution)/shard_map/ppermute | solution.py:56
  66.0 15.6 %collective-permute-start.15 = (bf16[512,512]{1,0:T(8,128)(2,1)S(1)}, bf16[512,512]{1,0:T(8,128)(2,1)S(1)}, u32[]{:S(2)}, u32[]{:S(2)}) collective-permute-start(bf16[512,512]{1,0:T(8,128)(2,1)S(1)} %get-tuple-element.72.refs_1_), channel_id=1, source_target_pairs={{0,2},{1,0},{2,4},{3,1},{4,6},{5,3},{6,8},{7,5},{8,10},{9,7},{10,1... | collective-permute-start | bytes 1572872 | tf_op jit(solution)/shard_map/ppermute | solution.py:56
  83.5 5.5 %collective-permute-start.18 = (bf16[512,512]{1,0:T(8,128)(2,1)S(1)}, bf16[512,512]{1,0:T(8,128)(2,1)S(1)}, u32[]{:S(2)}, u32[]{:S(2)}) collective-permute-start(bf16[512,512]{1,0:T(8,128)(2,1)S(1)} %get-tuple-element.77.sum_own), channel_id=1, source_target_pairs={{0,1},{1,0},{2,3},{3,2},{4,5},{5,4},{6,7},{7,6},{8,9},{9,8},{10,11... | collective-permute-start | bytes 1572872 | tf_op jit(solution)/shard_map/ppermute | solution.py:23
  88.7 2.0 %collective-permute-start.17 = (bf16[512,512]{1,0:T(8,128)(2,1)S(1)}, bf16[512,512]{1,0:T(8,128)(2,1)S(1)}, u32[]{:S(2)}, u32[]{:S(2)}) collective-permute-start(bf16[512,512]{1,0:T(8,128)(2,1)S(1)} %decode_rest.1.sum_own), channel_id=1, source_target_pairs={{0,1},{1,0},{2,3},{3,2},{4,5},{5,4},{6,7},{7,6},{8,9},{9,8},{10,11... | collective-permute-start | bytes 1572872 | tf_op jit(solution)/shard_map/ppermute | solution.py:23
  (10 other events, 34.2 us)

commit v4 on v3

--- a/solution.py
+++ b/solution.py
@@ -187,25 +187,22 @@
     return jnp.where(live[offset, :, columns] > 0, targets[offset, :, columns], -1)
 
 
-def encode_near_kernel(
-    meta, own, other, w1, w1_other, sent, senders, targets, piece, recv, before
-):
+def encode_near_kernel(meta, sent, senders, piece):
     gather_slots(senders[near_offset(meta)], sent, piece)
-    mine, rest = window(meta[0]), window(1 - meta[0])
-    for start in range(0, own.shape[0], HALF):
-        rows = pl.ds(start, HALF)
-        a, b = own[rows, :], other[rows, :]
-        recv[rows, mine] = (dot(a, w1[mine, :]) + dot(b, w1[rest, :])).astype(BF16)
-        recv[rows, rest] = (dot(a, w1_other[mine, :]) + dot(b, w1_other[rest, :])).astype(BF16)
-    gather_slots(targets[skip_offset(meta)], recv, before)
 
 
 def encode_skip_sum_kernel(
-    meta, rows, before, recv, sent, own, other, w2, w2_other, senders, targets, live,
-    total, before_near, self_term, message, own_message,
+    meta, rows, sent, own, other, w1, w1_other, w2, w2_other, senders, targets, live,
+    total, before_near, self_term, message, own_message, recv, before,
 ):
     mine, rest = window(meta[0]), window(1 - meta[0])
     nodes = recv.shape[0]
+    for start in range(0, nodes, HALF):
+        part_rows = pl.ds(start, HALF)
+        a, b = own[part_rows, :], other[part_rows, :]
+        recv[part_rows, mine] = (dot(a, w1[mine, :]) + dot(b, w1[rest, :])).astype(BF16)
+        recv[part_rows, rest] = (dot(a, w1_other[mine, :]) + dot(b, w1_other[rest, :])).astype(BF16)
+    gather_slots(targets[skip_offset(meta)], recv, before)
     from_rows = hot_columns(column(senders[REACH, :, mine]), sent.shape[0])
     to_rows = hot_columns(column(targets[REACH, :, mine]), nodes)
     own_message[...] = silu_message(dot(from_rows, sent[...]) + dot(to_rows, recv[...]))
@@ -484,30 +481,26 @@
     )
     skip_rows = exchange(skip_piece, skip_shift)
     layer_other = swap(after(layer_weights, skip_piece))
-    operands = (
-        meta, mesh_latent, mesh_other, encode_weights, encode_other, sent, senders, targets
-    )
-    near_piece, recv, before_skip = call(
+    operands = (meta, sent, senders)
+    (near_piece,) = call(
         encode_near_kernel,
         "encode_near",
         operands,
-        [SMEM, whole(mesh_latent), whole(mesh_other)]
-        + [part(encode_weights, 1), part(encode_other, 1)]
-        + [whole(sent), whole(senders), whole(targets)],
-        [shape(slots, full), shape(mesh_rows, full), shape(slots, full)],
-        2 * full * (mesh_rows * full + slots * (grid_rows + mesh_rows)),
+        [SMEM, whole(sent), whole(senders)],
+        [shape(slots, full)],
+        2 * full * slots * grid_rows,
     )
     near_rows = exchange(near_piece, near_shift)
     operands = (
-        meta, skip_rows, before_skip, recv, sent, mesh_latent, mesh_other,
+        meta, skip_rows, sent, mesh_latent, mesh_other, encode_weights, encode_other,
         encode_weights, encode_other, senders, targets, live,
     )
     total, before_near, self_term = call(
         encode_skip_sum_kernel,
         "encode_skip_sum",
         operands,
-        [SMEM] + [whole(x) for x in operands[1:7]]
-        + [part(encode_weights, 2), part(encode_other, 2)]
+        [SMEM] + [whole(x) for x in operands[1:5]]
+        + [part(operands[5 + i], 1 + i // 2) for i in range(4)]
         + [whole(x) for x in operands[9:]],
         [
             shape(mesh_rows, full, dtype=F32),
@@ -515,7 +508,12 @@
             shape(HELD, full),
         ],
         2 * full * mesh_rows * slots * 3,
-        [pltpu.VMEM((slots, full), BF16), pltpu.VMEM((HALF, full), BF16)],
+        [
+            pltpu.VMEM((slots, full), BF16),
+            pltpu.VMEM((HALF, full), BF16),
+            pltpu.VMEM((mesh_rows, full), BF16),
+            pltpu.VMEM((slots, full), BF16),
+        ],
     )
     operands = (meta, near_rows, before_near, targets, live, total)
     sum_own, sum_other = call(

time: 92.6 us -> 92.5 us (level)
  no operation moved by 1% of the time
where the time goes in v4:
time: 92.5 us; the launch traced here: 92.3 us
  Pallas kernels  38.4 us (42%)
  waiting for transfers between devices  29.1 us (31%)
  starting transfers between devices  21.5 us (23%)
  local copies, waits for them, and re-layouts  2.34 us (3%)
  between operations  0.93 us (1%)
    pallas_call x18, Pallas kernels, call(): pl.pallas_call(viewed, name=name, grid=(1,), in_specs=[spec.spec if isins...  35.1 us
    ppermute x8, waiting for transfers between devices, exchange(): return lax.ppermute(value, ('band', 'feat'), pairs(lax.axis_size('band')))  26.5 us
    ppermute x8, starting transfers between devices, exchange(): return lax.ppermute(value, ('band', 'feat'), pairs(lax.axis_size('band')))  11.2 us
    ppermute x11, starting transfers between devices, swap(): return lax.ppermute(value, 'feat', [(0, 1), (1, 0)])  10.3 us
    pallas_call x2, Pallas kernels, body(): pl.pallas_call(functools.partial(final_kernel, index * half), name=f'fina...  3.3 us
    ppermute x11, waiting for transfers between devices, swap(): return lax.ppermute(value, 'feat', [(0, 1), (1, 0)])  2.56 us
    unnamed x30, local copies, waits for them, and re-layouts  2.34 us
  transfers between devices with their start and end apart: 19, of which 9 were waited for; matrix products, arithmetic and copies ran while one was open for 0% of the time, Pallas kernels for 34%

profile of v4, /device:TPU:129, one launch (start us, length us, event | category | flops | bytes accessed | tf_op | source)
XLA Modules:
  0.0 92.3 jit_solution(7570710615395760520)
XLA Ops:
  5.2 1.9 %encode_skip.1 = (bf16[1024,512]{1,0:T(8,128)(2,1)S(1)}, bf16[512,512]{1,0:T(8,128)(2,1)S(1)}) custom-call(s32[2]{0:T(128)S(1)} %pad_add_fusion.refs_0_.meta, bf16[1024,256]{1,0:T(8,128)(2,1)S(1)} %copy-done.4, bf16[1024,256]{1,0:T(8,128)(2,1)S(1)} %collective-permute-done.refs_2_, f32[1024,256]{1,0:T(8,128)S(1)} %encode_begin.1.refs_3_, ...), custom_call_target="tpu_custom_call" | custom-call | flops 16777216 | bytes 24576 | tf_op jit(solution)/shard_map/encode_skip/pallas_call | solution.py:134
  7.5 4.7 %collective-permute-start.4 = (bf16[512,512]{1,0:T(8,128)(2,1)S(1)}, bf16[512,512]{1,0:T(8,128)(2,1)S(1)}, u32[]{:S(2)}, u32[]{:S(2)}) collective-permute-start(bf16[512,512]{1,0:T(8,128)(2,1)S(1)} %get-tuple-element.39), channel_id=1, source_target_pairs={{0,4},{1,0},{2,6},{3,2},{4,8},{5,1},{6,10},{7,3},{8,12},{9,5},{10,... | collective-permute-start | bytes 1572872 | tf_op jit(solution)/shard_map/ppermute | solution.py:56
  14.4 6.7 %collective-permute-done.4.refs_1_ = bf16[512,512]{1,0:T(8,128)(2,1)S(1)} collective-permute-done((bf16[512,512]{1,0:T(8,128)(2,1)S(1)}, bf16[512,512]{1,0:T(8,128)(2,1)S(1)}, u32[]{:S(2)}, u32[]{:S(2)}) %collective-permute-start.4) | collective-permute-done | bytes 524320 | tf_op jit(solution)/shard_map/ppermute | solution.py:56
  21.2 2.9 %encode_skip_sum.1 = (f32[512,512]{1,0:T(8,128)S(1)}, bf16[512,512]{1,0:T(8,128)(2,1)S(1)}, bf16[320,512]{1,0:T(8,128)(2,1)S(1)}) custom-call(s32[2]{0:T(128)S(1)} %pad_add_fusion.refs_0_.meta, bf16[512,512]{1,0:T(8,128)(2,1)S(1)} %collective-permute-done.4.refs_1_, bf16[1024,512]{1,0:T(8,128)(2,1)S(1)} %get-tuple-element.38.refs_1_.refs_2_, ...), custom_call_target="tpu_custom_call" | custom-call | flops 12582912 | bytes 29696 | tf_op jit(solution)/shard_map/encode_skip_sum/pallas_call | solution.py:134
  24.1 5.2 %collective-permute-done.3.refs_1_ = bf16[512,512]{1,0:T(8,128)(2,1)S(1)} collective-permute-done((bf16[512,512]{1,0:T(8,128)(2,1)S(1)}, bf16[512,512]{1,0:T(8,128)(2,1)S(1)}, u32[]{:S(2)}, u32[]{:S(2)}) %collective-permute-start.3) | collective-permute-done | bytes 524320 | tf_op jit(solution)/shard_map/ppermute | solution.py:56
  30.4 2.4 %collective-permute-start.6 = (bf16[320,512]{1,0:T(8,128)(2,1)S(1)}, bf16[320,512]{1,0:T(8,128)(2,1)S(1)}, u32[]{:S(2)}, u32[]{:S(2)}) collective-permute-start(bf16[320,512]{1,0:T(8,128)(2,1)S(1)} %get-tuple-element.43), channel_id=1, source_target_pairs={{0,1},{1,0},{2,3},{3,2},{4,5},{5,4},{6,7},{7,6},{8,9},{9,8},{10,11... | collective-permute-start | bytes 983048 | tf_op jit(solution)/shard_map/ppermute | solution.py:23
  35.8 1.6 %collective-permute-start.10 = (bf16[64,512]{1,0:T(8,128)(2,1)S(1)}, bf16[64,512]{1,0:T(8,128)(2,1)S(1)}, u32[]{:S(2)}, u32[]{:S(2)}) collective-permute-start(bf16[64,512]{1,0:T(8,128)(2,1)S(1)} %get-tuple-element.53), channel_id=1, source_target_pairs={{0,1},{1,0},{2,4},{3,5},{4,2},{5,3},{6,8},{7,9},{8,6},{9,7},{10,12... | collective-permute-start | bytes 196616 | tf_op jit(solution)/shard_map/ppermute | solution.py:56
  38.9 2.1 %layer_gather_0.1.refs_1_ = bf16[8,320,512]{2,1,0:T(8,128)(2,1)S(1)} custom-call(s32[2]{0:T(128)S(1)} %pad_add_fusion.refs_0_.meta, bf16[256,512]{1,0:T(8,128)(2,1)S(1)} %get-tuple-element.49.refs_1_, bf16[256,512]{1,0:T(8,128)(2,1)S(1)} %get-tuple-element.50.refs_2_, s32[8,512]{1,0:T(8,128)S(1)} %bitcast.19), custom_call_target="tpu_custom_call" | custom-call | flops 16777216 | bytes 40960 | tf_op jit(solution)/shard_map/layer_gather_0/pallas_call | solution.py:134
  41.0 3.8 %collective-permute-done.10.refs_4_ = bf16[64,512]{1,0:T(8,128)(2,1)S(1)} collective-permute-done((bf16[64,512]{1,0:T(8,128)(2,1)S(1)}, bf16[64,512]{1,0:T(8,128)(2,1)S(1)}, u32[]{:S(2)}, u32[]{:S(2)}) %collective-permute-start.10) | collective-permute-done | bytes 65568 | tf_op jit(solution)/shard_map/ppermute | solution.py:56
  44.8 3.0 %layer_update_0.1 = (bf16[256,512]{1,0:T(8,128)(2,1)S(1)}, bf16[64,512]{1,0:T(8,128)(2,1)S(1)}, bf16[64,512]{1,0:T(8,128)(2,1)S(1)}) custom-call(s32[2]{0:T(128)S(1)} %pad_add_fusion.refs_0_.meta, bf16[8,320,512]{2,1,0:T(8,128)(2,1)S(1)} %layer_gather_0.1.refs_1_, bf16[320,512]{1,0:T(8,128)(2,1)S(1)} %get-tuple-element.51.refs_2_, ...), custom_call_target="tpu_custom_call" | custom-call | flops 6291456 | bytes 6144 | tf_op jit(solution)/shard_map/layer_update_0/pallas_call | solution.py:134
  48.9 1.8 %collective-permute-start.12 = (bf16[64,512]{1,0:T(8,128)(2,1)S(1)}, bf16[64,512]{1,0:T(8,128)(2,1)S(1)}, u32[]{:S(2)}, u32[]{:S(2)}) collective-permute-start(bf16[64,512]{1,0:T(8,128)(2,1)S(1)} %get-tuple-element.61), channel_id=1, source_target_pairs={{0,1},{1,0},{2,4},{3,5},{4,2},{5,3},{6,8},{7,9},{8,6},{9,7},{10,12... | collective-permute-start | bytes 196616 | tf_op jit(solution)/shard_map/ppermute | solution.py:56
  52.0 1.8 %layer_gather_1.1.refs_1_ = bf16[8,256,512]{2,1,0:T(8,128)(2,1)S(1)} custom-call(s32[2]{0:T(128)S(1)} %pad_add_fusion.refs_0_.meta, bf16[256,512]{1,0:T(8,128)(2,1)S(1)} %get-tuple-element.58.refs_1_, bf16[256,512]{1,0:T(8,128)(2,1)S(1)} %get-tuple-element.59.refs_2_, s32[8,512]{1,0:T(8,128)S(1)} %bitcast.21), custom_call_target="tpu_custom_call" | custom-call | flops 16777216 | bytes 32768 | tf_op jit(solution)/shard_map/layer_gather_1/pallas_call | solution.py:134
  53.9 4.1 %collective-permute-done.12.refs_3_ = bf16[64,512]{1,0:T(8,128)(2,1)S(1)} collective-permute-done((bf16[64,512]{1,0:T(8,128)(2,1)S(1)}, bf16[64,512]{1,0:T(8,128)(2,1)S(1)}, u32[]{:S(2)}, u32[]{:S(2)}) %collective-permute-start.12) | collective-permute-done | bytes 65568 | tf_op jit(solution)/shard_map/ppermute | solution.py:56
  57.9 2.0 %layer_sum_1.1.refs_5_ = bf16[256,512]{1,0:T(8,128)(2,1)S(1)} custom-call(s32[2]{0:T(128)S(1)} %pad_add_fusion.refs_0_.meta, bf16[8,256,512]{2,1,0:T(8,128)(2,1)S(1)} %layer_gather_1.1.refs_1_, bf16[256,512]{1,0:T(8,128)(2,1)S(1)} %get-tuple-element.60.refs_2_, bf16[64,512]{1,0:T(8,128)(2,1)S(1)} %collective-permute-done.12.refs_3_, ...), custom_call_target="tpu_custom_call" | custom-call | flops 4194304 | bytes 4096 | tf_op jit(solution)/shard_map/layer_sum_1/pallas_call | solution.py:134
  62.0 1.8 %last_update.1 = (bf16[512,256]{1,0:T(8,128)(2,1)S(1)}, bf16[512,512]{1,0:T(8,128)(2,1)S(1)}) custom-call(s32[2]{0:T(128)S(1)} %pad_add_fusion.refs_0_.meta, bf16[256,512]{1,0:T(8,128)(2,1)S(1)} %get-tuple-element.55.refs_1_, bf16[256,512]{1,0:T(8,128)(2,1)S(1)} %collective-permute-done.11.refs_2_, bf16[256,512]{1,0:T(8,128)(2,1)S(1)} %get-tuple-element.56.refs_3_, ...), custom_call_target="tpu_custom_call" | custom-call | flops 8388608 | bytes 12288 | tf_op jit(solution)/shard_map/last_update/pallas_call | solution.py:134
  63.8 2.1 %collective-permute-start.16 = (bf16[512,512]{1,0:T(8,128)(2,1)S(1)}, bf16[512,512]{1,0:T(8,128)(2,1)S(1)}, u32[]{:S(2)}, u32[]{:S(2)}) collective-permute-start(bf16[512,512]{1,0:T(8,128)(2,1)S(1)} %get-tuple-element.66.refs_1_), channel_id=1, source_target_pairs={{0,4},{1,0},{2,6},{3,2},{4,8},{5,1},{6,10},{7,3},{8,12},{9,5},{10,... | collective-permute-start | bytes 1572872 | tf_op jit(solution)/shard_map/ppermute | solution.py:56
  66.0 5.1 %decode_prepare.1 = (bf16[512,512]{1,0:T(8,128)(2,1)S(1)}, bf16[1024,512]{1,0:T(8,128)(2,1)S(1)}, bf16[1024,512]{1,0:T(8,128)(2,1)S(1)}, bf16[1024,256]{1,0:T(8,128)(2,1)S(1)}, bf16[512,256]{1,0:T(8,128)(2,1)}) custom-call(s32[2]{0:T(128)S(1)} %pad_add_fusion.refs_0_.meta, bf16[1024,256]{1,0:T(8,128)(2,1)S(1)} %copy-done.5, ...), custom_call_target="tpu_custom_call" | custom-call | flops 50331648 | bytes 53248 | tf_op jit(solution)/shard_map/decode_prepare/pallas_call | solution.py:134
  71.1 1.7 %decode_own.1.refs_6_ = bf16[1024,512]{1,0:T(8,128)(2,1)S(1)} custom-call(s32[2]{0:T(128)S(1)} %pad_add_fusion.refs_0_.meta, bf16[512,512]{1,0:T(8,128)(2,1)S(1)} %get-tuple-element.66.refs_1_, bf16[512,512]{1,0:T(8,128)(2,1)S(1)} %get-tuple-element.69.refs_2_, s32[5,1,1024]{2,1,0:T(1,128)S(1)} %bitcast.23, s32[5,1,1024]{2,1,0:T(1,128)S(1)} %bitcast.11, ...), custom_call_target="tpu_custom_call" | custom-call | flops 12582912 | bytes 16384 | tf_op jit(solution)/shard_map/decode_own/pallas_call | solution.py:134
  72.7 6.7 %collective-permute-done.16.refs_1_ = bf16[512,512]{1,0:T(8,128)(2,1)S(1)} collective-permute-done((bf16[512,512]{1,0:T(8,128)(2,1)S(1)}, bf16[512,512]{1,0:T(8,128)(2,1)S(1)}, u32[]{:S(2)}, u32[]{:S(2)}) %collective-permute-start.16) | collective-permute-done | bytes 524320 | tf_op jit(solution)/shard_map/ppermute | solution.py:56
  79.4 2.5 %decode_skip.1.refs_6_.refs_4_ = bf16[1024,512]{1,0:T(8,128)(2,1)S(1)} custom-call(s32[2]{0:T(128)S(1)} %pad_add_fusion.refs_0_.meta, bf16[512,512]{1,0:T(8,128)(2,1)S(1)} %collective-permute-done.16.refs_1_, bf16[1024,512]{1,0:T(8,128)(2,1)S(1)} %get-tuple-element.68.refs_2_, s32[5,1,1024]{2,1,0:T(1,128)S(1)} %bitcast.24, s32[5,1,1024]{2,1,0:T(1,128)S(1)} %bitcast.12, ...), custom_call_target="tpu_custom_call" | custom-call | flops 25165824 | bytes 16384 | tf_op jit(solution)/shard_map/decode_skip/pallas_call | solution.py:134
  81.9 1.9 %decode_near.1 = (bf16[512,512]{1,0:T(8,128)(2,1)S(1)}, bf16[1024,512]{1,0:T(8,128)(2,1)S(1)}) custom-call(s32[2]{0:T(128)S(1)} %pad_add_fusion.refs_0_.meta, bf16[512,512]{1,0:T(8,128)(2,1)S(1)} %collective-permute-done.15.refs_1_, bf16[1024,512]{1,0:T(8,128)(2,1)S(1)} %get-tuple-element.67.refs_2_, s32[5,1,1024]{2,1,0:T(1,128)S(1)} %bitcast.25, ...), custom_call_target="tpu_custom_call" | custom-call | flops 25165824 | bytes 24576 | tf_op jit(solution)/shard_map/decode_near/pallas_call | solution.py:134
  83.8 3.6 %collective-permute-start.18 = (bf16[512,512]{1,0:T(8,128)(2,1)S(1)}, bf16[512,512]{1,0:T(8,128)(2,1)S(1)}, u32[]{:S(2)}, u32[]{:S(2)}) collective-permute-start(bf16[512,512]{1,0:T(8,128)(2,1)S(1)} %get-tuple-element.71.sum_own), channel_id=1, source_target_pairs={{0,1},{1,0},{2,3},{3,2},{4,5},{5,4},{6,7},{7,6},{8,9},{9,8},{10,11... | collective-permute-start | bytes 1572872 | tf_op jit(solution)/shard_map/ppermute | solution.py:23
  89.0 1.7 %final_update_0.1.refs_0_ = bf16[1024,256]{1,0:T(8,128)(2,1)} custom-call(s32[2]{0:T(128)S(1)} %pad_add_fusion.refs_0_.meta, bf16[1024,256]{1,0:T(8,128)(2,1)S(1)} %copy-done.5, bf16[1024,256]{1,0:T(8,128)(2,1)S(1)} %get-tuple-element.65.self_term, bf16[512,512]{1,0:T(8,128)(2,1)S(1)} %get-tuple-element.71.sum_own, ...), custom_call_target="tpu_custom_call" | custom-call | tf_op jit(solution)/shard_map/final_update_0/pallas_call | solution.py:694
  90.7 1.7 %final_update_1.1 = bf16[1024,256]{1,0:T(8,128)(2,1)} custom-call(s32[2]{0:T(128)S(1)} %pad_add_fusion.refs_0_.meta, bf16[1024,256]{1,0:T(8,128)(2,1)S(1)} %copy-done.5, bf16[1024,256]{1,0:T(8,128)(2,1)S(1)} %get-tuple-element.65.self_term, bf16[512,512]{1,0:T(8,128)(2,1)S(1)} %decode_rest.1.sum_own, ...), custom_call_target="tpu_custom_call", output_to_operand_aliasing={{}: (6, {})} | custom-call | tf_op jit(solution)/shard_map/final_update_1/pallas_call | solution.py:694
  (65 shorter events, 18.8 us)
Async XLA Ops:
  0.6 4.5 %collective-permute-start.2 = (bf16[4,512,256]{2,1,0:T(8,128)(2,1)}, bf16[4,512,256]{2,1,0:T(8,128)(2,1)S(1)}, u32[]{:S(2)}, u32[]{:S(2)}) collective-permute-start(bf16[4,512,256]{2,1,0:T(8,128)(2,1)} %refs_6_.1), channel_id=1, source_target_pairs={{0,1},{1,0},{2,3},{3,2},{4,5},{5,4},{6,7},{7,6},{8,9},{9,8},{10,11... | collective-permute-start | bytes 3145736 | tf_op jit(solution)/shard_map/ppermute | solution.py:23
  1.4 3.7 %collective-permute-start = (bf16[1024,256]{1,0:T(8,128)(2,1)}, bf16[1024,256]{1,0:T(8,128)(2,1)S(1)}, u32[]{:S(2)}, u32[]{:S(2)}) collective-permute-start(bf16[1024,256]{1,0:T(8,128)(2,1)} %own.3), channel_id=1, source_target_pairs={{0,1},{1,0},{2,3},{3,2},{4,5},{5,4},{6,7},{7,6},{8,9},{9,8},{10,11... | collective-permute-start | bytes 1572872 | tf_op jit(solution)/shard_map/ppermute | solution.py:23
  1.5 3.6 %collective-permute-start.1 = (bf16[512,256]{1,0:T(8,128)(2,1)}, bf16[512,256]{1,0:T(8,128)(2,1)S(1)}, u32[]{:S(2)}, u32[]{:S(2)}) collective-permute-start(bf16[512,256]{1,0:T(8,128)(2,1)} %refs_1_.6), channel_id=1, source_target_pairs={{0,1},{1,0},{2,3},{3,2},{4,5},{5,4},{6,7},{7,6},{8,9},{9,8},{10,11... | collective-permute-start | bytes 786440 | tf_op jit(solution)/shard_map/ppermute | solution.py:23
  5.2 16.0 %copy-start.3 = (bf16[4,512,256]{2,1,0:T(8,128)(2,1)S(1)}, bf16[4,512,256]{2,1,0:T(8,128)(2,1)}, u32[]{:S(2)}) copy-start(bf16[4,512,256]{2,1,0:T(8,128)(2,1)} %refs_6_.1) | copy-start | bytes 3145732
  5.2 16.0 %copy-start.6 = (bf16[512,256]{1,0:T(8,128)(2,1)S(1)}, bf16[512,256]{1,0:T(8,128)(2,1)}, u32[]{:S(2)}) copy-start(bf16[512,256]{1,0:T(8,128)(2,1)} %refs_1_.6) | copy-start | bytes 786436
  5.2 16.0 %copy-start.13 = (s32[1,5,512]{2,0,1:T(1,128)S(1)}, s32[1,5,512]{2,0,1:T(1,128)}, u32[]{:S(2)}) copy-start(s32[1,5,512]{2,0,1:T(1,128)} %param.19) | copy-start | bytes 30724
  5.2 16.0 %copy-start.14 = (s32[1,5,512]{2,0,1:T(1,128)S(1)}, s32[1,5,512]{2,0,1:T(1,128)}, u32[]{:S(2)}) copy-start(s32[1,5,512]{2,0,1:T(1,128)} %param.20) | copy-start | bytes 30724
  7.1 26.9 %collective-permute-start.7 = (bf16[2,4,512,256]{3,2,1,0:T(8,128)(2,1)S(1)}, bf16[2,4,512,256]{3,2,1,0:T(8,128)(2,1)S(1)}, u32[]{:S(2)}, u32[]{:S(2)}) collective-permute-start(bf16[2,4,512,256]{3,2,1,0:T(8,128)(2,1)S(1)} %copy-done), channel_id=1, source_target_pairs={{0,1},{1,0},{2,3},{3,2},{4,5},{5,4},{6,7},{7,6},{8,9},{9,8},{10,11... | collective-permute-start | bytes 6291464 | tf_op jit(solution)/shard_map/ppermute | solution.py:23
  7.5 13.7 %collective-permute-start.4 = (bf16[512,512]{1,0:T(8,128)(2,1)S(1)}, bf16[512,512]{1,0:T(8,128)(2,1)S(1)}, u32[]{:S(2)}, u32[]{:S(2)}) collective-permute-start(bf16[512,512]{1,0:T(8,128)(2,1)S(1)} %get-tuple-element.39), channel_id=1, source_target_pairs={{0,4},{1,0},{2,6},{3,2},{4,8},{5,1},{6,10},{7,3},{8,12},{9,5},{10,... | collective-permute-start | bytes 1572872 | tf_op jit(solution)/shard_map/ppermute | solution.py:56
  13.5 15.8 %collective-permute-start.3 = (bf16[512,512]{1,0:T(8,128)(2,1)S(1)}, bf16[512,512]{1,0:T(8,128)(2,1)S(1)}, u32[]{:S(2)}, u32[]{:S(2)}) collective-permute-start(bf16[512,512]{1,0:T(8,128)(2,1)S(1)} %encode_near.1), channel_id=1, source_target_pairs={{0,2},{1,0},{2,4},{3,1},{4,6},{5,3},{6,8},{7,5},{8,10},{9,7},{10,1... | collective-permute-start | bytes 1572872 | tf_op jit(solution)/shard_map/ppermute | solution.py:56
  24.1 8.7 %copy-start.1 = (bf16[4,512,256]{2,1,0:T(8,128)(2,1)S(1)}, bf16[4,512,256]{2,1,0:T(8,128)(2,1)}, u32[]{:S(2)}) copy-start(bf16[4,512,256]{2,1,0:T(8,128)(2,1)} %weights.3) | copy-start | bytes 3145732
  30.4 3.7 %collective-permute-start.6 = (bf16[320,512]{1,0:T(8,128)(2,1)S(1)}, bf16[320,512]{1,0:T(8,128)(2,1)S(1)}, u32[]{:S(2)}, u32[]{:S(2)}) collective-permute-start(bf16[320,512]{1,0:T(8,128)(2,1)S(1)} %get-tuple-element.43), channel_id=1, source_target_pairs={{0,1},{1,0},{2,3},{3,2},{4,5},{5,4},{6,7},{7,6},{8,9},{9,8},{10,11... | collective-permute-start | bytes 983048 | tf_op jit(solution)/shard_map/ppermute | solution.py:23
  32.8 28.1 %collective-permute-start.5 = (bf16[4,512,256]{2,1,0:T(8,128)(2,1)S(1)}, bf16[4,512,256]{2,1,0:T(8,128)(2,1)S(1)}, u32[]{:S(2)}, u32[]{:S(2)}) collective-permute-start(bf16[4,512,256]{2,1,0:T(8,128)(2,1)S(1)} %copy-done.1), channel_id=1, source_target_pairs={{0,1},{1,0},{2,3},{3,2},{4,5},{5,4},{6,7},{7,6},{8,9},{9,8},{10,11... | collective-permute-start | bytes 3145736 | tf_op jit(solution)/shard_map/ppermute | solution.py:23
  35.4 2.1 %collective-permute-start.8 = (bf16[256,512]{1,0:T(8,128)(2,1)S(1)}, bf16[256,512]{1,0:T(8,128)(2,1)S(1)}, u32[]{:S(2)}, u32[]{:S(2)}) collective-permute-start(bf16[256,512]{1,0:T(8,128)(2,1)S(1)} %get-tuple-element.48.refs_1_.refs_7_), channel_id=1, source_target_pairs={{0,1},{1,0},{2,3},{3,2},{4,5},{5,4},{6,7},{7,6},{8,9},{9,8},{10,11... | collective-permute-start | bytes 786440 | tf_op jit(solution)/shard_map/ppermute | solution.py:23
  35.8 9.0 %collective-permute-start.10 = (bf16[64,512]{1,0:T(8,128)(2,1)S(1)}, bf16[64,512]{1,0:T(8,128)(2,1)S(1)}, u32[]{:S(2)}, u32[]{:S(2)}) collective-permute-start(bf16[64,512]{1,0:T(8,128)(2,1)S(1)} %get-tuple-element.53), channel_id=1, source_target_pairs={{0,1},{1,0},{2,4},{3,5},{4,2},{5,3},{6,8},{7,9},{8,6},{9,7},{10,12... | collective-permute-start | bytes 196616 | tf_op jit(solution)/shard_map/ppermute | solution.py:56
  37.4 7.4 %collective-permute-start.9 = (bf16[64,512]{1,0:T(8,128)(2,1)S(1)}, bf16[64,512]{1,0:T(8,128)(2,1)S(1)}, u32[]{:S(2)}, u32[]{:S(2)}) collective-permute-start(bf16[64,512]{1,0:T(8,128)(2,1)S(1)} %get-tuple-element.52), channel_id=1, source_target_pairs={{0,2},{1,3},{2,0},{3,1},{4,6},{5,7},{6,4},{7,5},{8,10},{9,11},{10,... | collective-permute-start | bytes 196616 | tf_op jit(solution)/shard_map/ppermute | solution.py:56
  47.8 2.8 %collective-permute-start.11 = (bf16[256,512]{1,0:T(8,128)(2,1)S(1)}, bf16[256,512]{1,0:T(8,128)(2,1)S(1)}, u32[]{:S(2)}, u32[]{:S(2)}) collective-permute-start(bf16[256,512]{1,0:T(8,128)(2,1)S(1)} %get-tuple-element.55.refs_1_), channel_id=1, source_target_pairs={{0,1},{1,0},{2,3},{3,2},{4,5},{5,4},{6,7},{7,6},{8,9},{9,8},{10,11... | collective-permute-start | bytes 786440 | tf_op jit(solution)/shard_map/ppermute | solution.py:23
  48.9 9.1 %collective-permute-start.12 = (bf16[64,512]{1,0:T(8,128)(2,1)S(1)}, bf16[64,512]{1,0:T(8,128)(2,1)S(1)}, u32[]{:S(2)}, u32[]{:S(2)}) collective-permute-start(bf16[64,512]{1,0:T(8,128)(2,1)S(1)} %get-tuple-element.61), channel_id=1, source_target_pairs={{0,1},{1,0},{2,4},{3,5},{4,2},{5,3},{6,8},{7,9},{8,6},{9,7},{10,12... | collective-permute-start | bytes 196616 | tf_op jit(solution)/shard_map/ppermute | solution.py:56
  50.6 7.3 %collective-permute-start.13 = (bf16[64,512]{1,0:T(8,128)(2,1)S(1)}, bf16[64,512]{1,0:T(8,128)(2,1)S(1)}, u32[]{:S(2)}, u32[]{:S(2)}) collective-permute-start(bf16[64,512]{1,0:T(8,128)(2,1)S(1)} %get-tuple-element.62), channel_id=1, source_target_pairs={{0,2},{1,3},{2,0},{3,1},{4,6},{5,7},{6,4},{7,5},{8,10},{9,11},{10,... | collective-permute-start | bytes 196616 | tf_op jit(solution)/shard_map/ppermute | solution.py:56
  59.9 2.1 %collective-permute-start.14 = (bf16[256,512]{1,0:T(8,128)(2,1)S(1)}, bf16[256,512]{1,0:T(8,128)(2,1)S(1)}, u32[]{:S(2)}, u32[]{:S(2)}) collective-permute-start(bf16[256,512]{1,0:T(8,128)(2,1)S(1)} %layer_sum_1.1.refs_5_), channel_id=1, source_target_pairs={{0,1},{1,0},{2,3},{3,2},{4,5},{5,4},{6,7},{7,6},{8,9},{9,8},{10,11... | collective-permute-start | bytes 786440 | tf_op jit(solution)/shard_map/ppermute | solution.py:23
  63.8 15.6 %collective-permute-start.16 = (bf16[512,512]{1,0:T(8,128)(2,1)S(1)}, bf16[512,512]{1,0:T(8,128)(2,1)S(1)}, u32[]{:S(2)}, u32[]{:S(2)}) collective-permute-start(bf16[512,512]{1,0:T(8,128)(2,1)S(1)} %get-tuple-element.66.refs_1_), channel_id=1, source_target_pairs={{0,4},{1,0},{2,6},{3,2},{4,8},{5,1},{6,10},{7,3},{8,12},{9,5},{10,... | collective-permute-start | bytes 1572872 | tf_op jit(solution)/shard_map/ppermute | solution.py:56
  66.0 15.9 %collective-permute-start.15 = (bf16[512,512]{1,0:T(8,128)(2,1)S(1)}, bf16[512,512]{1,0:T(8,128)(2,1)S(1)}, u32[]{:S(2)}, u32[]{:S(2)}) collective-permute-start(bf16[512,512]{1,0:T(8,128)(2,1)S(1)} %get-tuple-element.66.refs_1_), channel_id=1, source_target_pairs={{0,2},{1,0},{2,4},{3,1},{4,6},{5,3},{6,8},{7,5},{8,10},{9,7},{10,1... | collective-permute-start | bytes 1572872 | tf_op jit(solution)/shard_map/ppermute | solution.py:56
  83.8 5.1 %collective-permute-start.18 = (bf16[512,512]{1,0:T(8,128)(2,1)S(1)}, bf16[512,512]{1,0:T(8,128)(2,1)S(1)}, u32[]{:S(2)}, u32[]{:S(2)}) collective-permute-start(bf16[512,512]{1,0:T(8,128)(2,1)S(1)} %get-tuple-element.71.sum_own), channel_id=1, source_target_pairs={{0,1},{1,0},{2,3},{3,2},{4,5},{5,4},{6,7},{7,6},{8,9},{9,8},{10,11... | collective-permute-start | bytes 1572872 | tf_op jit(solution)/shard_map/ppermute | solution.py:23
  88.7 2.0 %collective-permute-start.17 = (bf16[512,512]{1,0:T(8,128)(2,1)S(1)}, bf16[512,512]{1,0:T(8,128)(2,1)S(1)}, u32[]{:S(2)}, u32[]{:S(2)}) collective-permute-start(bf16[512,512]{1,0:T(8,128)(2,1)S(1)} %decode_rest.1.sum_own), channel_id=1, source_target_pairs={{0,1},{1,0},{2,3},{3,2},{4,5},{5,4},{6,7},{7,6},{8,9},{9,8},{10,11... | collective-permute-start | bytes 1572872 | tf_op jit(solution)/shard_map/ppermute | solution.py:23
  (10 other events, 34.2 us)

commit v5 on v4

--- a/solution.py
+++ b/solution.py
@@ -423,16 +423,18 @@
 
 def decode_rest_kernel(offset_of, meta, message, targets, live, total, out):
     row = live_targets(targets, live, offset_of(meta))
-    decode_scatter(row, message, total, out.shape[0], out)
-
-
-def final_kernel(first, meta, own, self_term, sum_own, sum_other, weights, *refs):
-    out, w3 = refs[-1], weights.at[3]
+    decode_scatter(row, message, total, total.shape[0] - out.shape[0], out)
+
+
+def final_kernel(meta, own, self_term, head, head_in, tail, tail_in, w3, out):
     for start in range(0, out.shape[0], HALF):
-        rows, from_rows = pl.ds(start, HALF), pl.ds(first + start, HALF)
-        summed = sum_own[rows, :] + sum_other[rows, :]
-        step = silu(self_term[from_rows, :].astype(F32) + dot(summed, w3[...]))
-        out[rows, :] = (own[from_rows, :].astype(F32) + step).astype(BF16)
+        rows = pl.ds(start, HALF)
+        first = start < head.shape[0]
+        sums, lead = ((head, head_in), 0) if first else ((tail, tail_in), head.shape[0])
+        part_rows = pl.ds(start - lead, HALF)
+        summed = sums[0][part_rows, :] + sums[1][part_rows, :]
+        step = silu(self_term[rows, :].astype(F32) + dot(summed, w3[...]))
+        out[rows, :] = (own[rows, :].astype(F32) + step).astype(BF16)
 
 
 def body(
@@ -664,14 +666,14 @@
         flops,
         message_space,
     )
-    half = grid_rows // 2
+    rest = HALF
     operands = (meta, near_rows, before_near, senders, targets, live, total)
     head, message = call(
         functools.partial(decode_sum_kernel, near_offset),
         "decode_near",
         operands,
         [SMEM] + [whole(x) for x in operands[1:]],
-        [shape(half, full), shape(slots, full)],
+        [shape(grid_rows - rest, full), shape(slots, full)],
         flops,
     )
     operands = (meta, message, targets, live, total)
@@ -680,27 +682,20 @@
         "decode_rest",
         operands,
         [SMEM] + [whole(x) for x in operands[1:]],
-        [shape(half, full)],
+        [shape(rest, full)],
         flops // 2,
     )
-    grid_now = None
-    for index, summed in enumerate((head, tail)):
-        block = pl.BlockSpec((half, cols), lambda i, index=index: (index, 0))
-        operands = (meta, grid_latent, self_term, summed, swap(summed), decode_weights)
-        specs = [SMEM] + [whole(x) for x in operands[1:]]
-        aliases = {}
-        if index:
-            operands, specs, aliases = operands + (grid_now,), specs + [pl.BlockSpec(memory_space=pl.ANY)], {6: 0}
-        grid_now = pl.pallas_call(
-            functools.partial(final_kernel, index * half),
-            name=f"final_update_{index}",
-            grid=(1,),
-            in_specs=specs,
-            out_specs=block,
-            out_shape=shape(grid_rows, cols),
-            input_output_aliases=aliases,
-            compiler_params=pltpu.CompilerParams(vmem_limit_bytes=VMEM_LIMIT),
-        )(*operands)
+    operands = (
+        meta, grid_latent, self_term, head, swap(head), tail, swap(tail), decode_weights
+    )
+    (grid_now,) = call(
+        final_kernel,
+        "final_update",
+        operands,
+        [SMEM] + [whole(x) for x in operands[1:7]] + [part(decode_weights, 3)],
+        [shape(grid_rows, cols)],
+        2 * full * grid_rows * cols,
+    )
     return mesh_now, grid_now
 
 

time: 92.5 us -> 92.5 us (level)
  Pallas kernels: 38.4 us -> 37.1 us
  waiting for transfers between devices: 29.1 us -> 30.3 us
    pallas_call x2 -> x0, Pallas kernels: 3.3 us -> none  [body(): pl.pallas_call(functools.partial(final_kernel, index * half), name=f'fina...]
    pallas_call x18 -> x19, Pallas kernels: 35.1 us -> 37.1 us  [call(): pl.pallas_call(viewed, name=name, grid=(1,), in_specs=[spec.spec if isins...]
    ppermute x11, waiting for transfers between devices: 2.56 us -> 3.84 us  [swap(): return lax.ppermute(value, 'feat', [(0, 1), (1, 0)])]
  transfers between devices with their start and end apart: 19 -> 19, of which waited for: 9 -> 8; matrix products, arithmetic and copies ran while one was open for 0% -> 0% of each run, Pallas kernels for 34% -> 32%
where the time goes in v5:
time: 92.5 us; the launch traced here: 92.3 us
  Pallas kernels  37.1 us (40%)
  waiting for transfers between devices  30.3 us (33%)
  starting transfers between devices  21.5 us (23%)
  local copies, waits for them, and re-layouts  2.34 us (3%)
  between operations  0.93 us (1%)
    pallas_call x19, Pallas kernels, call(): pl.pallas_call(viewed, name=name, grid=(1,), in_specs=[spec.spec if isins...  37.1 us
    ppermute x8, waiting for transfers between devices, exchange(): return lax.ppermute(value, ('band', 'feat'), pairs(lax.axis_size('band')))  26.5 us
    ppermute x8, starting transfers between devices, exchange(): return lax.ppermute(value, ('band', 'feat'), pairs(lax.axis_size('band')))  11.2 us
    ppermute x11, starting transfers between devices, swap(): return lax.ppermute(value, 'feat', [(0, 1), (1, 0)])  10.3 us
    ppermute x11, waiting for transfers between devices, swap(): return lax.ppermute(value, 'feat', [(0, 1), (1, 0)])  3.84 us
    unnamed x30, local copies, waits for them, and re-layouts  2.34 us
  transfers between devices with their start and end apart: 19, of which 8 were waited for; matrix products, arithmetic and copies ran while one was open for 0% of the time, Pallas kernels for 32%

profile of v5, /device:TPU:129, one launch (start us, length us, event | category | flops | bytes accessed | tf_op | source)
XLA Modules:
  0.0 92.3 jit_solution(18045798896734646266)
XLA Ops:
  5.2 1.9 %encode_skip.1 = (bf16[1024,512]{1,0:T(8,128)(2,1)S(1)}, bf16[512,512]{1,0:T(8,128)(2,1)S(1)}) custom-call(s32[2]{0:T(128)S(1)} %pad_add_fusion.refs_0_, bf16[1024,256]{1,0:T(8,128)(2,1)S(1)} %copy-done.4, bf16[1024,256]{1,0:T(8,128)(2,1)S(1)} %collective-permute-done.refs_2_, f32[1024,256]{1,0:T(8,128)S(1)} %encode_begin.1.refs_3_, ...), custom_call_target="tpu_custom_call" | custom-call | flops 16777216 | bytes 24576 | tf_op jit(solution)/shard_map/encode_skip/pallas_call | solution.py:134
  7.5 4.7 %collective-permute-start.4 = (bf16[512,512]{1,0:T(8,128)(2,1)S(1)}, bf16[512,512]{1,0:T(8,128)(2,1)S(1)}, u32[]{:S(2)}, u32[]{:S(2)}) collective-permute-start(bf16[512,512]{1,0:T(8,128)(2,1)S(1)} %get-tuple-element.39), channel_id=1, source_target_pairs={{0,4},{1,0},{2,6},{3,2},{4,8},{5,1},{6,10},{7,3},{8,12},{9,5},{10,... | collective-permute-start | bytes 1572872 | tf_op jit(solution)/shard_map/ppermute | solution.py:56
  14.4 6.7 %collective-permute-done.4.refs_1_ = bf16[512,512]{1,0:T(8,128)(2,1)S(1)} collective-permute-done((bf16[512,512]{1,0:T(8,128)(2,1)S(1)}, bf16[512,512]{1,0:T(8,128)(2,1)S(1)}, u32[]{:S(2)}, u32[]{:S(2)}) %collective-permute-start.4) | collective-permute-done | bytes 524320 | tf_op jit(solution)/shard_map/ppermute | solution.py:56
  21.2 2.9 %encode_skip_sum.1 = (f32[512,512]{1,0:T(8,128)S(1)}, bf16[512,512]{1,0:T(8,128)(2,1)S(1)}, bf16[320,512]{1,0:T(8,128)(2,1)S(1)}) custom-call(s32[2]{0:T(128)S(1)} %pad_add_fusion.refs_0_, bf16[512,512]{1,0:T(8,128)(2,1)S(1)} %collective-permute-done.4.refs_1_, bf16[1024,512]{1,0:T(8,128)(2,1)S(1)} %get-tuple-element.38.refs_1_.refs_2_, ...), custom_call_target="tpu_custom_call" | custom-call | flops 12582912 | bytes 29696 | tf_op jit(solution)/shard_map/encode_skip_sum/pallas_call | solution.py:134
  24.1 5.2 %collective-permute-done.3.refs_1_ = bf16[512,512]{1,0:T(8,128)(2,1)S(1)} collective-permute-done((bf16[512,512]{1,0:T(8,128)(2,1)S(1)}, bf16[512,512]{1,0:T(8,128)(2,1)S(1)}, u32[]{:S(2)}, u32[]{:S(2)}) %collective-permute-start.3) | collective-permute-done | bytes 524320 | tf_op jit(solution)/shard_map/ppermute | solution.py:56
  30.4 2.4 %collective-permute-start.6 = (bf16[320,512]{1,0:T(8,128)(2,1)S(1)}, bf16[320,512]{1,0:T(8,128)(2,1)S(1)}, u32[]{:S(2)}, u32[]{:S(2)}) collective-permute-start(bf16[320,512]{1,0:T(8,128)(2,1)S(1)} %get-tuple-element.43), channel_id=1, source_target_pairs={{0,1},{1,0},{2,3},{3,2},{4,5},{5,4},{6,7},{7,6},{8,9},{9,8},{10,11... | collective-permute-start | bytes 983048 | tf_op jit(solution)/shard_map/ppermute | solution.py:23
  35.8 1.6 %collective-permute-start.10 = (bf16[64,512]{1,0:T(8,128)(2,1)S(1)}, bf16[64,512]{1,0:T(8,128)(2,1)S(1)}, u32[]{:S(2)}, u32[]{:S(2)}) collective-permute-start(bf16[64,512]{1,0:T(8,128)(2,1)S(1)} %get-tuple-element.53), channel_id=1, source_target_pairs={{0,1},{1,0},{2,4},{3,5},{4,2},{5,3},{6,8},{7,9},{8,6},{9,7},{10,12... | collective-permute-start | bytes 196616 | tf_op jit(solution)/shard_map/ppermute | solution.py:56
  38.9 2.1 %layer_gather_0.1.refs_1_ = bf16[8,320,512]{2,1,0:T(8,128)(2,1)S(1)} custom-call(s32[2]{0:T(128)S(1)} %pad_add_fusion.refs_0_, bf16[256,512]{1,0:T(8,128)(2,1)S(1)} %get-tuple-element.49.refs_1_, bf16[256,512]{1,0:T(8,128)(2,1)S(1)} %get-tuple-element.50.refs_2_, s32[8,512]{1,0:T(8,128)S(1)} %bitcast.19), custom_call_target="tpu_custom_call" | custom-call | flops 16777216 | bytes 40960 | tf_op jit(solution)/shard_map/layer_gather_0/pallas_call | solution.py:134
  41.0 3.8 %collective-permute-done.10.refs_4_ = bf16[64,512]{1,0:T(8,128)(2,1)S(1)} collective-permute-done((bf16[64,512]{1,0:T(8,128)(2,1)S(1)}, bf16[64,512]{1,0:T(8,128)(2,1)S(1)}, u32[]{:S(2)}, u32[]{:S(2)}) %collective-permute-start.10) | collective-permute-done | bytes 65568 | tf_op jit(solution)/shard_map/ppermute | solution.py:56
  44.8 3.0 %layer_update_0.1 = (bf16[256,512]{1,0:T(8,128)(2,1)S(1)}, bf16[64,512]{1,0:T(8,128)(2,1)S(1)}, bf16[64,512]{1,0:T(8,128)(2,1)S(1)}) custom-call(s32[2]{0:T(128)S(1)} %pad_add_fusion.refs_0_, bf16[8,320,512]{2,1,0:T(8,128)(2,1)S(1)} %layer_gather_0.1.refs_1_, bf16[320,512]{1,0:T(8,128)(2,1)S(1)} %get-tuple-element.51.refs_2_, ...), custom_call_target="tpu_custom_call" | custom-call | flops 6291456 | bytes 6144 | tf_op jit(solution)/shard_map/layer_update_0/pallas_call | solution.py:134
  48.9 1.8 %collective-permute-start.12 = (bf16[64,512]{1,0:T(8,128)(2,1)S(1)}, bf16[64,512]{1,0:T(8,128)(2,1)S(1)}, u32[]{:S(2)}, u32[]{:S(2)}) collective-permute-start(bf16[64,512]{1,0:T(8,128)(2,1)S(1)} %get-tuple-element.61), channel_id=1, source_target_pairs={{0,1},{1,0},{2,4},{3,5},{4,2},{5,3},{6,8},{7,9},{8,6},{9,7},{10,12... | collective-permute-start | bytes 196616 | tf_op jit(solution)/shard_map/ppermute | solution.py:56
  52.0 1.8 %layer_gather_1.1.refs_1_ = bf16[8,256,512]{2,1,0:T(8,128)(2,1)S(1)} custom-call(s32[2]{0:T(128)S(1)} %pad_add_fusion.refs_0_, bf16[256,512]{1,0:T(8,128)(2,1)S(1)} %get-tuple-element.58.refs_1_, bf16[256,512]{1,0:T(8,128)(2,1)S(1)} %get-tuple-element.59.refs_2_, s32[8,512]{1,0:T(8,128)S(1)} %bitcast.21), custom_call_target="tpu_custom_call" | custom-call | flops 16777216 | bytes 32768 | tf_op jit(solution)/shard_map/layer_gather_1/pallas_call | solution.py:134
  53.9 4.1 %collective-permute-done.12.refs_3_ = bf16[64,512]{1,0:T(8,128)(2,1)S(1)} collective-permute-done((bf16[64,512]{1,0:T(8,128)(2,1)S(1)}, bf16[64,512]{1,0:T(8,128)(2,1)S(1)}, u32[]{:S(2)}, u32[]{:S(2)}) %collective-permute-start.12) | collective-permute-done | bytes 65568 | tf_op jit(solution)/shard_map/ppermute | solution.py:56
  57.9 2.0 %layer_sum_1.1.refs_5_ = bf16[256,512]{1,0:T(8,128)(2,1)S(1)} custom-call(s32[2]{0:T(128)S(1)} %pad_add_fusion.refs_0_, bf16[8,256,512]{2,1,0:T(8,128)(2,1)S(1)} %layer_gather_1.1.refs_1_, bf16[256,512]{1,0:T(8,128)(2,1)S(1)} %get-tuple-element.60.refs_2_, bf16[64,512]{1,0:T(8,128)(2,1)S(1)} %collective-permute-done.12.refs_3_, ...), custom_call_target="tpu_custom_call" | custom-call | flops 4194304 | bytes 4096 | tf_op jit(solution)/shard_map/layer_sum_1/pallas_call | solution.py:134
  62.0 1.8 %last_update.1 = (bf16[512,256]{1,0:T(8,128)(2,1)S(1)}, bf16[512,512]{1,0:T(8,128)(2,1)S(1)}) custom-call(s32[2]{0:T(128)S(1)} %pad_add_fusion.refs_0_, bf16[256,512]{1,0:T(8,128)(2,1)S(1)} %get-tuple-element.55.refs_1_, bf16[256,512]{1,0:T(8,128)(2,1)S(1)} %collective-permute-done.11.refs_2_, bf16[256,512]{1,0:T(8,128)(2,1)S(1)} %get-tuple-element.56.refs_3_, ...), custom_call_target="tpu_custom_call" | custom-call | flops 8388608 | bytes 12288 | tf_op jit(solution)/shard_map/last_update/pallas_call | solution.py:134
  63.8 2.1 %collective-permute-start.16 = (bf16[512,512]{1,0:T(8,128)(2,1)S(1)}, bf16[512,512]{1,0:T(8,128)(2,1)S(1)}, u32[]{:S(2)}, u32[]{:S(2)}) collective-permute-start(bf16[512,512]{1,0:T(8,128)(2,1)S(1)} %get-tuple-element.66.refs_1_), channel_id=1, source_target_pairs={{0,4},{1,0},{2,6},{3,2},{4,8},{5,1},{6,10},{7,3},{8,12},{9,5},{10,... | collective-permute-start | bytes 1572872 | tf_op jit(solution)/shard_map/ppermute | solution.py:56
  66.0 5.1 %decode_prepare.1 = (bf16[512,512]{1,0:T(8,128)(2,1)S(1)}, bf16[1024,512]{1,0:T(8,128)(2,1)S(1)}, bf16[1024,512]{1,0:T(8,128)(2,1)S(1)}, bf16[1024,256]{1,0:T(8,128)(2,1)S(1)}, bf16[512,256]{1,0:T(8,128)(2,1)}) custom-call(s32[2]{0:T(128)S(1)} %pad_add_fusion.refs_0_, bf16[1024,256]{1,0:T(8,128)(2,1)S(1)} %copy-done.5, ...), custom_call_target="tpu_custom_call" | custom-call | flops 50331648 | bytes 53248 | tf_op jit(solution)/shard_map/decode_prepare/pallas_call | solution.py:134
  71.1 1.7 %decode_own.1.refs_6_ = bf16[1024,512]{1,0:T(8,128)(2,1)S(1)} custom-call(s32[2]{0:T(128)S(1)} %pad_add_fusion.refs_0_, bf16[512,512]{1,0:T(8,128)(2,1)S(1)} %get-tuple-element.66.refs_1_, bf16[512,512]{1,0:T(8,128)(2,1)S(1)} %get-tuple-element.69.refs_2_, s32[5,1,1024]{2,1,0:T(1,128)S(1)} %bitcast.23, s32[5,1,1024]{2,1,0:T(1,128)S(1)} %bitcast.11, ...), custom_call_target="tpu_custom_call" | custom-call | flops 12582912 | bytes 16384 | tf_op jit(solution)/shard_map/decode_own/pallas_call | solution.py:134
  72.7 6.7 %collective-permute-done.16.refs_1_ = bf16[512,512]{1,0:T(8,128)(2,1)S(1)} collective-permute-done((bf16[512,512]{1,0:T(8,128)(2,1)S(1)}, bf16[512,512]{1,0:T(8,128)(2,1)S(1)}, u32[]{:S(2)}, u32[]{:S(2)}) %collective-permute-start.16) | collective-permute-done | bytes 524320 | tf_op jit(solution)/shard_map/ppermute | solution.py:56
  79.4 2.5 %decode_skip.1.refs_6_.refs_4_ = bf16[1024,512]{1,0:T(8,128)(2,1)S(1)} custom-call(s32[2]{0:T(128)S(1)} %pad_add_fusion.refs_0_, bf16[512,512]{1,0:T(8,128)(2,1)S(1)} %collective-permute-done.16.refs_1_, bf16[1024,512]{1,0:T(8,128)(2,1)S(1)} %get-tuple-element.68.refs_2_, s32[5,1,1024]{2,1,0:T(1,128)S(1)} %bitcast.24, s32[5,1,1024]{2,1,0:T(1,128)S(1)} %bitcast.12, ...), custom_call_target="tpu_custom_call" | custom-call | flops 25165824 | bytes 16384 | tf_op jit(solution)/shard_map/decode_skip/pallas_call | solution.py:134
  81.9 2.2 %decode_near.1 = (bf16[768,512]{1,0:T(8,128)(2,1)S(1)}, bf16[1024,512]{1,0:T(8,128)(2,1)S(1)}) custom-call(s32[2]{0:T(128)S(1)} %pad_add_fusion.refs_0_, bf16[512,512]{1,0:T(8,128)(2,1)S(1)} %collective-permute-done.15.refs_1_, bf16[1024,512]{1,0:T(8,128)(2,1)S(1)} %get-tuple-element.67.refs_2_, s32[5,1,1024]{2,1,0:T(1,128)S(1)} %bitcast.25, ...), custom_call_target="tpu_custom_call" | custom-call | flops 25165824 | bytes 28672 | tf_op jit(solution)/shard_map/decode_near/pallas_call | solution.py:134
  84.1 3.6 %collective-permute-start.17 = (bf16[768,512]{1,0:T(8,128)(2,1)S(1)}, bf16[768,512]{1,0:T(8,128)(2,1)S(1)}, u32[]{:S(2)}, u32[]{:S(2)}) collective-permute-start(bf16[768,512]{1,0:T(8,128)(2,1)S(1)} %get-tuple-element.70.refs_3_), channel_id=1, source_target_pairs={{0,1},{1,0},{2,3},{3,2},{4,5},{5,4},{6,7},{7,6},{8,9},{9,8},{10,11... | collective-permute-start | bytes 2359304 | tf_op jit(solution)/shard_map/ppermute | solution.py:23
  88.8 1.5 %collective-permute-done.18.refs_6_ = bf16[256,512]{1,0:T(8,128)(2,1)S(1)} collective-permute-done((bf16[256,512]{1,0:T(8,128)(2,1)S(1)}, bf16[256,512]{1,0:T(8,128)(2,1)S(1)}, u32[]{:S(2)}, u32[]{:S(2)}) %collective-permute-start.18) | collective-permute-done | bytes 262176 | tf_op jit(solution)/shard_map/ppermute | solution.py:23
  90.3 2.0 %final_update.1 = bf16[1024,256]{1,0:T(8,128)(2,1)} custom-call(s32[2]{0:T(128)S(1)} %pad_add_fusion.refs_0_, bf16[1024,256]{1,0:T(8,128)(2,1)S(1)} %copy-done.5, bf16[1024,256]{1,0:T(8,128)(2,1)S(1)} %get-tuple-element.65.refs_2_, bf16[768,512]{1,0:T(8,128)(2,1)S(1)} %get-tuple-element.70.refs_3_, bf16[768,512]{1,0:T(8,128)(2,1)S(1)} %collective-permute-done.17.refs_4_, ...), custom_call_target="tpu_custom_call" | custom-call | flops 4194304 | bytes 8192 | tf_op jit(solution)/shard_map/final_update/pallas_call | solution.py:134
  (64 shorter events, 18.2 us)
Async XLA Ops:
  0.6 4.5 %collective-permute-start.2 = (bf16[4,512,256]{2,1,0:T(8,128)(2,1)}, bf16[4,512,256]{2,1,0:T(8,128)(2,1)S(1)}, u32[]{:S(2)}, u32[]{:S(2)}) collective-permute-start(bf16[4,512,256]{2,1,0:T(8,128)(2,1)} %refs_6_.1), channel_id=1, source_target_pairs={{0,1},{1,0},{2,3},{3,2},{4,5},{5,4},{6,7},{7,6},{8,9},{9,8},{10,11... | collective-permute-start | bytes 3145736 | tf_op jit(solution)/shard_map/ppermute | solution.py:23
  1.4 3.7 %collective-permute-start = (bf16[1024,256]{1,0:T(8,128)(2,1)}, bf16[1024,256]{1,0:T(8,128)(2,1)S(1)}, u32[]{:S(2)}, u32[]{:S(2)}) collective-permute-start(bf16[1024,256]{1,0:T(8,128)(2,1)} %refs_1_.9), channel_id=1, source_target_pairs={{0,1},{1,0},{2,3},{3,2},{4,5},{5,4},{6,7},{7,6},{8,9},{9,8},{10,11... | collective-permute-start | bytes 1572872 | tf_op jit(solution)/shard_map/ppermute | solution.py:23
  1.5 3.6 %collective-permute-start.1 = (bf16[512,256]{1,0:T(8,128)(2,1)}, bf16[512,256]{1,0:T(8,128)(2,1)S(1)}, u32[]{:S(2)}, u32[]{:S(2)}) collective-permute-start(bf16[512,256]{1,0:T(8,128)(2,1)} %refs_1_.7), channel_id=1, source_target_pairs={{0,1},{1,0},{2,3},{3,2},{4,5},{5,4},{6,7},{7,6},{8,9},{9,8},{10,11... | collective-permute-start | bytes 786440 | tf_op jit(solution)/shard_map/ppermute | solution.py:23
  5.2 16.0 %copy-start.2 = (bf16[4,512,256]{2,1,0:T(8,128)(2,1)S(1)}, bf16[4,512,256]{2,1,0:T(8,128)(2,1)}, u32[]{:S(2)}) copy-start(bf16[4,512,256]{2,1,0:T(8,128)(2,1)} %refs_6_.1) | copy-start | bytes 3145732
  5.2 16.0 %copy-start.6 = (bf16[512,256]{1,0:T(8,128)(2,1)S(1)}, bf16[512,256]{1,0:T(8,128)(2,1)}, u32[]{:S(2)}) copy-start(bf16[512,256]{1,0:T(8,128)(2,1)} %refs_1_.7) | copy-start | bytes 786436
  5.2 16.0 %copy-start.13 = (s32[1,5,512]{2,0,1:T(1,128)S(1)}, s32[1,5,512]{2,0,1:T(1,128)}, u32[]{:S(2)}) copy-start(s32[1,5,512]{2,0,1:T(1,128)} %param.19) | copy-start | bytes 30724
  5.2 16.0 %copy-start.14 = (s32[1,5,512]{2,0,1:T(1,128)S(1)}, s32[1,5,512]{2,0,1:T(1,128)}, u32[]{:S(2)}) copy-start(s32[1,5,512]{2,0,1:T(1,128)} %param.20) | copy-start | bytes 30724
  7.1 26.9 %collective-permute-start.7 = (bf16[2,4,512,256]{3,2,1,0:T(8,128)(2,1)S(1)}, bf16[2,4,512,256]{3,2,1,0:T(8,128)(2,1)S(1)}, u32[]{:S(2)}, u32[]{:S(2)}) collective-permute-start(bf16[2,4,512,256]{3,2,1,0:T(8,128)(2,1)S(1)} %copy-done), channel_id=1, source_target_pairs={{0,1},{1,0},{2,3},{3,2},{4,5},{5,4},{6,7},{7,6},{8,9},{9,8},{10,11... | collective-permute-start | bytes 6291464 | tf_op jit(solution)/shard_map/ppermute | solution.py:23
  7.5 13.7 %collective-permute-start.4 = (bf16[512,512]{1,0:T(8,128)(2,1)S(1)}, bf16[512,512]{1,0:T(8,128)(2,1)S(1)}, u32[]{:S(2)}, u32[]{:S(2)}) collective-permute-start(bf16[512,512]{1,0:T(8,128)(2,1)S(1)} %get-tuple-element.39), channel_id=1, source_target_pairs={{0,4},{1,0},{2,6},{3,2},{4,8},{5,1},{6,10},{7,3},{8,12},{9,5},{10,... | collective-permute-start | bytes 1572872 | tf_op jit(solution)/shard_map/ppermute | solution.py:56
  13.5 15.8 %collective-permute-start.3 = (bf16[512,512]{1,0:T(8,128)(2,1)S(1)}, bf16[512,512]{1,0:T(8,128)(2,1)S(1)}, u32[]{:S(2)}, u32[]{:S(2)}) collective-permute-start(bf16[512,512]{1,0:T(8,128)(2,1)S(1)} %encode_near.1), channel_id=1, source_target_pairs={{0,2},{1,0},{2,4},{3,1},{4,6},{5,3},{6,8},{7,5},{8,10},{9,7},{10,1... | collective-permute-start | bytes 1572872 | tf_op jit(solution)/shard_map/ppermute | solution.py:56
  24.1 8.7 %copy-start.3 = (bf16[4,512,256]{2,1,0:T(8,128)(2,1)S(1)}, bf16[4,512,256]{2,1,0:T(8,128)(2,1)}, u32[]{:S(2)}) copy-start(bf16[4,512,256]{2,1,0:T(8,128)(2,1)} %refs_7_.9) | copy-start | bytes 3145732
  30.4 3.7 %collective-permute-start.6 = (bf16[320,512]{1,0:T(8,128)(2,1)S(1)}, bf16[320,512]{1,0:T(8,128)(2,1)S(1)}, u32[]{:S(2)}, u32[]{:S(2)}) collective-permute-start(bf16[320,512]{1,0:T(8,128)(2,1)S(1)} %get-tuple-element.43), channel_id=1, source_target_pairs={{0,1},{1,0},{2,3},{3,2},{4,5},{5,4},{6,7},{7,6},{8,9},{9,8},{10,11... | collective-permute-start | bytes 983048 | tf_op jit(solution)/shard_map/ppermute | solution.py:23
  32.8 28.1 %collective-permute-start.5 = (bf16[4,512,256]{2,1,0:T(8,128)(2,1)S(1)}, bf16[4,512,256]{2,1,0:T(8,128)(2,1)S(1)}, u32[]{:S(2)}, u32[]{:S(2)}) collective-permute-start(bf16[4,512,256]{2,1,0:T(8,128)(2,1)S(1)} %copy-done.3), channel_id=1, source_target_pairs={{0,1},{1,0},{2,3},{3,2},{4,5},{5,4},{6,7},{7,6},{8,9},{9,8},{10,11... | collective-permute-start | bytes 3145736 | tf_op jit(solution)/shard_map/ppermute | solution.py:23
  35.4 2.1 %collective-permute-start.8 = (bf16[256,512]{1,0:T(8,128)(2,1)S(1)}, bf16[256,512]{1,0:T(8,128)(2,1)S(1)}, u32[]{:S(2)}, u32[]{:S(2)}) collective-permute-start(bf16[256,512]{1,0:T(8,128)(2,1)S(1)} %get-tuple-element.48.refs_1_.refs_7_), channel_id=1, source_target_pairs={{0,1},{1,0},{2,3},{3,2},{4,5},{5,4},{6,7},{7,6},{8,9},{9,8},{10,11... | collective-permute-start | bytes 786440 | tf_op jit(solution)/shard_map/ppermute | solution.py:23
  35.8 9.0 %collective-permute-start.10 = (bf16[64,512]{1,0:T(8,128)(2,1)S(1)}, bf16[64,512]{1,0:T(8,128)(2,1)S(1)}, u32[]{:S(2)}, u32[]{:S(2)}) collective-permute-start(bf16[64,512]{1,0:T(8,128)(2,1)S(1)} %get-tuple-element.53), channel_id=1, source_target_pairs={{0,1},{1,0},{2,4},{3,5},{4,2},{5,3},{6,8},{7,9},{8,6},{9,7},{10,12... | collective-permute-start | bytes 196616 | tf_op jit(solution)/shard_map/ppermute | solution.py:56
  37.4 7.4 %collective-permute-start.9 = (bf16[64,512]{1,0:T(8,128)(2,1)S(1)}, bf16[64,512]{1,0:T(8,128)(2,1)S(1)}, u32[]{:S(2)}, u32[]{:S(2)}) collective-permute-start(bf16[64,512]{1,0:T(8,128)(2,1)S(1)} %get-tuple-element.52), channel_id=1, source_target_pairs={{0,2},{1,3},{2,0},{3,1},{4,6},{5,7},{6,4},{7,5},{8,10},{9,11},{10,... | collective-permute-start | bytes 196616 | tf_op jit(solution)/shard_map/ppermute | solution.py:56
  47.8 2.8 %collective-permute-start.11 = (bf16[256,512]{1,0:T(8,128)(2,1)S(1)}, bf16[256,512]{1,0:T(8,128)(2,1)S(1)}, u32[]{:S(2)}, u32[]{:S(2)}) collective-permute-start(bf16[256,512]{1,0:T(8,128)(2,1)S(1)} %get-tuple-element.55.refs_1_), channel_id=1, source_target_pairs={{0,1},{1,0},{2,3},{3,2},{4,5},{5,4},{6,7},{7,6},{8,9},{9,8},{10,11... | collective-permute-start | bytes 786440 | tf_op jit(solution)/shard_map/ppermute | solution.py:23
  48.9 9.1 %collective-permute-start.12 = (bf16[64,512]{1,0:T(8,128)(2,1)S(1)}, bf16[64,512]{1,0:T(8,128)(2,1)S(1)}, u32[]{:S(2)}, u32[]{:S(2)}) collective-permute-start(bf16[64,512]{1,0:T(8,128)(2,1)S(1)} %get-tuple-element.61), channel_id=1, source_target_pairs={{0,1},{1,0},{2,4},{3,5},{4,2},{5,3},{6,8},{7,9},{8,6},{9,7},{10,12... | collective-permute-start | bytes 196616 | tf_op jit(solution)/shard_map/ppermute | solution.py:56
  50.6 7.3 %collective-permute-start.13 = (bf16[64,512]{1,0:T(8,128)(2,1)S(1)}, bf16[64,512]{1,0:T(8,128)(2,1)S(1)}, u32[]{:S(2)}, u32[]{:S(2)}) collective-permute-start(bf16[64,512]{1,0:T(8,128)(2,1)S(1)} %get-tuple-element.62), channel_id=1, source_target_pairs={{0,2},{1,3},{2,0},{3,1},{4,6},{5,7},{6,4},{7,5},{8,10},{9,11},{10,... | collective-permute-start | bytes 196616 | tf_op jit(solution)/shard_map/ppermute | solution.py:56
  59.9 2.1 %collective-permute-start.14 = (bf16[256,512]{1,0:T(8,128)(2,1)S(1)}, bf16[256,512]{1,0:T(8,128)(2,1)S(1)}, u32[]{:S(2)}, u32[]{:S(2)}) collective-permute-start(bf16[256,512]{1,0:T(8,128)(2,1)S(1)} %layer_sum_1.1.refs_5_), channel_id=1, source_target_pairs={{0,1},{1,0},{2,3},{3,2},{4,5},{5,4},{6,7},{7,6},{8,9},{9,8},{10,11... | collective-permute-start | bytes 786440 | tf_op jit(solution)/shard_map/ppermute | solution.py:23
  63.8 15.6 %collective-permute-start.16 = (bf16[512,512]{1,0:T(8,128)(2,1)S(1)}, bf16[512,512]{1,0:T(8,128)(2,1)S(1)}, u32[]{:S(2)}, u32[]{:S(2)}) collective-permute-start(bf16[512,512]{1,0:T(8,128)(2,1)S(1)} %get-tuple-element.66.refs_1_), channel_id=1, source_target_pairs={{0,4},{1,0},{2,6},{3,2},{4,8},{5,1},{6,10},{7,3},{8,12},{9,5},{10,... | collective-permute-start | bytes 1572872 | tf_op jit(solution)/shard_map/ppermute | solution.py:56
  66.0 15.9 %collective-permute-start.15 = (bf16[512,512]{1,0:T(8,128)(2,1)S(1)}, bf16[512,512]{1,0:T(8,128)(2,1)S(1)}, u32[]{:S(2)}, u32[]{:S(2)}) collective-permute-start(bf16[512,512]{1,0:T(8,128)(2,1)S(1)} %get-tuple-element.66.refs_1_), channel_id=1, source_target_pairs={{0,2},{1,0},{2,4},{3,1},{4,6},{5,3},{6,8},{7,5},{8,10},{9,7},{10,1... | collective-permute-start | bytes 1572872 | tf_op jit(solution)/shard_map/ppermute | solution.py:56
  84.1 6.2 %collective-permute-start.17 = (bf16[768,512]{1,0:T(8,128)(2,1)S(1)}, bf16[768,512]{1,0:T(8,128)(2,1)S(1)}, u32[]{:S(2)}, u32[]{:S(2)}) collective-permute-start(bf16[768,512]{1,0:T(8,128)(2,1)S(1)} %get-tuple-element.70.refs_3_), channel_id=1, source_target_pairs={{0,1},{1,0},{2,3},{3,2},{4,5},{5,4},{6,7},{7,6},{8,9},{9,8},{10,11... | collective-permute-start | bytes 2359304 | tf_op jit(solution)/shard_map/ppermute | solution.py:23
  88.7 1.6 %collective-permute-start.18 = (bf16[256,512]{1,0:T(8,128)(2,1)S(1)}, bf16[256,512]{1,0:T(8,128)(2,1)S(1)}, u32[]{:S(2)}, u32[]{:S(2)}) collective-permute-start(bf16[256,512]{1,0:T(8,128)(2,1)S(1)} %decode_rest.1.refs_5_), channel_id=1, source_target_pairs={{0,1},{1,0},{2,3},{3,2},{4,5},{5,4},{6,7},{7,6},{8,9},{9,8},{10,11... | collective-permute-start | bytes 786440 | tf_op jit(solution)/shard_map/ppermute | solution.py:23
  (10 other events, 34.2 us)
